TPU v7x, 256 devices: a whole 4x4x8 slice. The times are simulated.
256 devices in a mesh: seq: 32 (over x, y, core), dp: 8 (over z).
Axes of the slice: x: 4, y: 4, z: 8, core: 2. Of those that a mesh axis runs over, the one named last changes fastest.
Arguments:
- hidden_states: bfloat16 [8, 4096, 8192], P('dp', 'seq'), may hold values from -6 to 6
- teacher_queries: bfloat16 [8, 4096, 4096], P('dp', 'seq'), may hold values from -200 to 200
- teacher_keys: bfloat16 [8, 4096, 1024], P('dp', 'seq'), may hold values from -6 to 6
- teacher_values: bfloat16 [8, 4096, 1024], P('dp', 'seq'), may hold values from -6 to 6
- doc_ids: int32 [8, 4096], P('dp', 'seq'), may hold values from 0 to 3, never falling along the last dimension, each value on 1 to 2048 neighbouring positions
- w_proj: bfloat16 [8192, 288], P('dp'), may hold values from -0.0625 to 0.0625
- conv_weight: float32 [4, 256], replicated, may hold values from -3 to 3
- dt_bias: float32 [32], replicated, may hold values from -4 to -2
- decay_rate: float32 [32], replicated, may hold values from 0.0001 to 1
Outputs:
- grad_proj: float32 [8192, 288], P('dp')
All inputs are finite; a program needn't handle non-finite values.
Results may differ from a plain program's by a relative error of at most 0.002.
The roundings to bfloat16 on the way count: a program that leaves them out, or rounds other values in their place, can miss the bound.
Values may be sent and summed in bfloat16 or wider, within the bound.
No kernel may reach another device: no remote copies, remote signals or barrier semaphores. Data moves between devices by JAX's collectives and lax.ppermute only.
A program may use at most 128 MiB of HBM per device.

v0:
```python
import math

import jax
import jax.numpy as jnp
from jax import lax
from jax.sharding import PartitionSpec as P

KV_HEADS = 8
HEAD_DIM = 128
STATE = 16


HIGHEST_MODE = lax.Precision.HIGHEST
NEG_FILL = -1e30


def from_behind(block, axis, distance):
    devices = range(lax.axis_size(axis))
    route = [(i - distance, i) for i in devices if i - distance in devices]
    return lax.ppermute(block, axis, route)


def prefix(part, axis, combine, identity, reverse):
    count = lax.axis_size(axis)
    place = lax.axis_index(axis)
    ahead = count - 1 - place if reverse else place
    gathered = jax.tree.map(lambda a: lax.all_gather(a, axis), part)
    state = jax.tree.map(lambda a, e: jnp.zeros_like(a) + jnp.asarray(e, a.dtype), part, identity)

    def one(step, state):
        source = count - 1 - step if reverse else step
        return combine(
            state, jax.tree.map(lambda a: lax.dynamic_index_in_dim(a, source, 0, False), gathered)
        )

    return lax.fori_loop(0, ahead, one, state)


def combine_states(earlier, later):
    return (earlier[0] * later[0], later[0][:, None, None] * earlier[1] + later[1])


def add_pair(first, second):
    return first + second


def attend(query_rows, key_rows, value_rows, doc_all, local_heads):
    seq_len = query_rows.shape[0]
    head_dim = query_rows.shape[1] // local_heads
    key_count = key_rows.shape[1] // head_dim
    query_heads = query_rows.reshape(seq_len, local_heads, head_dim)
    key_heads = key_rows.reshape(seq_len, key_count, head_dim)
    value_heads = value_rows.reshape(seq_len, key_count, head_dim)
    score_scale = head_dim ** (-0.5)
    block_rows = max(min(512, seq_len), seq_len // 8)
    positions = jnp.arange(seq_len)
    pieces = []
    for row_start in range(0, seq_len, block_rows):
        row_end = row_start + block_rows
        query_block = query_heads[row_start:row_end]
        scores = jnp.einsum(
            "qhd,kd->hqk", query_block, key_heads[:row_end, 0], preferred_element_type=jnp.float32
        )
        allowed = (positions[None, :row_end] <= positions[row_start:row_end, None]) & (
            doc_all[None, :row_end] == doc_all[row_start:row_end, None]
        )
        scores = jnp.where(allowed[None], scores * score_scale, NEG_FILL)
        row_max = jnp.max(scores, axis=2, keepdims=True)
        weights = jnp.exp(scores - row_max)
        totals = jnp.sum(weights, axis=2)
        probabilities = weights.astype(jnp.bfloat16)
        mixed_rows = jnp.einsum(
            "hqk,kd->qhd",
            probabilities,
            value_heads[:row_end, 0],
            preferred_element_type=jnp.float32,
        )
        mixed_rows = mixed_rows / totals.T[:, :, None]
        pieces.append(mixed_rows.astype(jnp.bfloat16).reshape(block_rows, local_heads * head_dim))
    return jnp.concatenate(pieces, 0)


def conv_inputs(projected, prev_rows, labels, prev_labels, conv_weight, dt_bias, decay_rate):
    local_rows = projected.shape[0]
    taps = conv_weight.shape[0]
    bc_width = conv_weight.shape[1]
    gate_width = bc_width // 2
    source = projected[:, :bc_width]
    extended = jnp.concatenate([prev_rows, source], 0)
    ext_labels = jnp.concatenate([prev_labels, labels], 0)
    pre_act = conv_weight[0] * source
    for offset in range(1, taps):
        lagged = extended[taps - 1 - offset : taps - 1 - offset + local_rows]
        lag_labels = ext_labels[taps - 1 - offset : taps - 1 - offset + local_rows]
        pre_act = pre_act + conv_weight[offset] * jnp.where(
            (lag_labels == labels)[:, None], lagged, 0.0
        )
    gates = jax.nn.silu(pre_act)
    input_gate = gates[:, :gate_width].reshape(local_rows, KV_HEADS, STATE)
    output_gate = gates[:, gate_width:].reshape(local_rows, KV_HEADS, STATE)
    step_size = jax.nn.softplus(projected[:, bc_width:] + dt_bias)
    cum_log = jnp.cumsum(-step_size * decay_rate, axis=0)
    return (input_gate, output_gate, step_size, cum_log)


def student_outputs(parts, state_in, labels, prev_labels, value_rows):
    input_gate, output_gate, step_size, cum_log = parts
    local_rows = step_size.shape[0]
    head_total = step_size.shape[1]
    group_size = head_total // KV_HEADS
    order = jnp.arange(local_rows)
    same_doc = ((labels[:, None] == labels[None, :]) & (order[None, :] <= order[:, None])).astype(
        jnp.float32
    )
    gaps = cum_log.T[:, :, None] - cum_log.T[:, None, :]
    mixing = jnp.exp(gaps * same_doc[None]) * same_doc[None] * step_size.T[:, None, :]
    intersection = jnp.einsum("tgn,sgn->gts", output_gate, input_gate, precision=HIGHEST_MODE)
    mixing = mixing.reshape(KV_HEADS, group_size, local_rows, local_rows) * intersection[:, None]
    local_out = jnp.einsum("gkts,sgp->tgkp", mixing, value_rows, precision=HIGHEST_MODE)
    keep_in = (labels == prev_labels[-1]).astype(jnp.float32)
    carried = jnp.einsum(
        "tgn,gknp->tgkp",
        output_gate,
        state_in.reshape(KV_HEADS, group_size, STATE, HEAD_DIM),
        precision=HIGHEST_MODE,
    )
    scale_in = (jnp.exp(cum_log) * keep_in[:, None]).reshape(local_rows, KV_HEADS, group_size)
    return (local_out + carried * scale_in[..., None]).reshape(local_rows, head_total, HEAD_DIM)


def block_state(parts, labels, prev_labels, value_rows):
    input_gate, output_gate, step_size, cum_log = parts
    local_rows = step_size.shape[0]
    head_total = step_size.shape[1]
    group_size = head_total // KV_HEADS
    tail_same = (labels == labels[-1]).astype(jnp.float32)
    tail_weight = (
        jnp.exp((cum_log[-1][None, :] - cum_log) * tail_same[:, None])
        * tail_same[:, None]
        * step_size
    )
    state_local = jnp.einsum(
        "sgk,sgn,sgp->gknp",
        tail_weight.reshape(local_rows, KV_HEADS, group_size),
        input_gate,
        value_rows,
        precision=HIGHEST_MODE,
    )
    keep_last = (labels[-1] == prev_labels[-1]).astype(jnp.float32)
    decay_total = jnp.exp(cum_log[-1]) * keep_last
    return (decay_total, state_local.reshape(head_total, STATE, HEAD_DIM))


def local(
    hidden_states,
    teacher_queries,
    teacher_keys,
    teacher_values,
    doc_ids,
    w_proj,
    conv_weight,
    dt_bias,
    decay_rate,
):
    local_rows = hidden_states.shape[1]
    seq_devices = lax.axis_size("seq")
    data_devices = lax.axis_size("dp")
    seq_len = local_rows * seq_devices
    head_total = dt_bias.shape[0]
    head_dim = teacher_keys.shape[2] // KV_HEADS
    local_heads = head_total // seq_devices
    group_size = head_total // KV_HEADS
    taps = conv_weight.shape[0]
    bc_width = conv_weight.shape[1]
    tokens_in = hidden_states[0]
    columns = tokens_in
    projected = jnp.dot(
        columns,
        lax.all_gather(w_proj, "dp", axis=0, tiled=True),
        preferred_element_type=jnp.float32,
    )
    key_split = teacher_keys.reshape(1, local_rows, KV_HEADS, head_dim)
    value_split = teacher_values.reshape(1, local_rows, KV_HEADS, head_dim)
    keys_wide = jnp.repeat(key_split, group_size, axis=2).reshape(
        1, local_rows, head_total * head_dim
    )
    values_wide = jnp.repeat(value_split, group_size, axis=2).reshape(
        1, local_rows, head_total * head_dim
    )
    query_heads, key_heads, value_heads = (
        lax.all_to_all(teacher_queries, "seq", split_axis=2, concat_axis=1, tiled=True),
        lax.all_to_all(keys_wide, "seq", split_axis=2, concat_axis=1, tiled=True),
        lax.all_to_all(values_wide, "seq", split_axis=2, concat_axis=1, tiled=True),
    )
    doc_all = lax.all_gather(doc_ids, "seq", axis=1, tiled=True)
    teacher_heads = attend(query_heads[0], key_heads[0], value_heads[0], doc_all[0], local_heads)
    teacher_rows = lax.all_to_all(
        teacher_heads[None], "seq", split_axis=1, concat_axis=2, tiled=True
    )
    teacher_tok = teacher_rows[0].reshape(local_rows, head_total, head_dim).astype(jnp.float32)
    segment = doc_ids[0]
    labels = segment.astype(jnp.float32)
    edge_rows = projected[local_rows - taps + 1 :, :bc_width]
    edge_labels = labels[local_rows - taps + 1 :]
    prev_rows, prev_labels = from_behind((edge_rows, edge_labels), "seq", 1)
    value_rows = teacher_values[0].reshape(local_rows, KV_HEADS, head_dim).astype(jnp.float32)

    def conv_fn(proj_rows, edge_in):
        return conv_inputs(
            proj_rows, edge_in, labels, prev_labels, conv_weight, dt_bias, decay_rate
        )

    def state_fn(parts):
        return block_state(parts, labels, prev_labels, value_rows)

    def outputs_fn(parts, state_in):
        return student_outputs(parts, state_in, labels, prev_labels, value_rows)

    conv_parts, conv_vjp = jax.vjp(conv_fn, projected, prev_rows)
    (decay_total, state_local), state_vjp = jax.vjp(state_fn, conv_parts)
    identity = (jnp.ones_like(decay_total), jnp.zeros_like(state_local))
    state_in = prefix((decay_total, state_local), "seq", combine_states, identity, False)[1]
    student_out, outputs_vjp = jax.vjp(outputs_fn, conv_parts, state_in)
    loss_weight = 1.0 / math.sqrt(head_total * head_dim * data_devices * seq_len)
    grad_out = (student_out - teacher_tok) * loss_weight
    grad_parts_out, grad_state_in = outputs_vjp(grad_out)
    adjoint = prefix((decay_total, grad_state_in), "seq", combine_states, identity, True)[1]
    grad_decay = jnp.sum(adjoint * state_in, axis=(1, 2))
    grad_parts_state = state_vjp((grad_decay, adjoint))[0]
    grad_parts = jax.tree.map(add_pair, grad_parts_out, grad_parts_state)
    grad_first, grad_prev = conv_vjp(grad_parts)
    returned = from_behind(grad_prev, "seq", -1)
    grad_pre = grad_first.at[local_rows - taps + 1 :, :bc_width].add(returned)
    grad_rounded = grad_pre.astype(jnp.bfloat16)
    columns = tokens_in
    row_sums = lax.psum_scatter(
        jnp.dot(columns.T, grad_rounded, preferred_element_type=jnp.float32),
        "dp",
        scatter_dimension=0,
        tiled=True,
    )
    summed = lax.psum(row_sums, "seq")
    return summed


def solution(mesh):
    placed = (
        P("dp", "seq", None),
        P("dp", "seq", None),
        P("dp", "seq", None),
        P("dp", "seq", None),
        P("dp", "seq"),
        P("dp", None),
        P(),
        P(),
        P(),
    )
    return jax.shard_map(
        local, mesh=mesh, in_specs=placed, out_specs=P("dp", None), check_vma=False
    )
```

profile of v0, /device:TPU:1, one launch (start us, length us, event | category | flops | bytes accessed | tf_op | source)
XLA Modules:
  0.0 868.6 jit_solution(6827954505286688363)
XLA Ops:
  8.0 4.6 collective-permute-start
  17.1 2.4 compare_convert_fusion
  19.6 53.2 %all-gather.5.cloned.1.call-done = bf16[8192,288]{0,1:T(8,128)(2,1)} async-done(((bf16[1024,288]{0,1:T(8,128)(2,1)}), bf16[8192,288]{0,1:T(8,128)(2,1)}) %all-gather.5.cloned.1.call-update) | async-done | bytes 4718608 | tf_op jit(solution)/shard_map/all_gather | solution.py:179
  72.7 3.7 fusion.43
  76.6 3.7 collective-permute-start.1
  84.8 17.0 %copy.223 = bf16[1,128,4096]{1,0,2:T(2,128)(2,1)} copy(bf16[1,128,4096]{1,2,0:T(8,128)(2,1)S(1)} %bitcast.530) | data formatting | bytes 2097152 | tf_op jit(solution)/shard_map/broadcast_in_dim | solution.py:184
  102.4 23.4 %reduce.36 = bf16[4096,128]{1,0:T(8,128)(2,1)S(1)} reduce(bf16[4096,1,128]{2,1,0:T(2,128)(2,1)} %bitcast.520, bf16[]{:T(256)} %broadcast.823), dimensions={1}, to_apply=%bitcast.488.reduce_sub_computation | reduce | bytes 2097154
  126.9 8.5 all-to-all-start
  137.5 17.0 %copy.222 = bf16[1,128,4096]{1,0,2:T(2,128)(2,1)} copy(bf16[1,128,4096]{1,2,0:T(8,128)(2,1)S(1)} %bitcast.531) | data formatting | bytes 2097152 | tf_op jit(solution)/shard_map/broadcast_in_dim | solution.py:187
  154.6 24.4 %reduce.35 = bf16[4096,128]{1,0:T(8,128)(2,1)} reduce(bf16[4096,1,128]{2,1,0:T(2,128)(2,1)} %bitcast.522, bf16[]{:T(256)} %broadcast.823), dimensions={1}, to_apply=%bitcast.487.reduce_sub_computation | reduce | bytes 2097154
  178.9 2.1 reshape.1315
  181.1 7.9 all-to-all-start.2
  189.6 5.5 copy.136
  195.1 24.4 %reduce.37 = bf16[4096,128]{1,0:T(8,128)(2,1)} reduce(bf16[4096,1,128]{2,1,0:T(2,128)(2,1)} %bitcast.524, bf16[]{:T(256)} %broadcast.823), dimensions={1}, to_apply=%bitcast.439.reduce_sub_computation | reduce | bytes 2097154
  219.5 2.2 reshape.1319
  227.0 7.4 all-to-all-start.1
  234.4 29.8 %all_gather.21 = s32[1,4096]{1,0:T(1,128)S(1)} all-gather(s32[1,128]{1,0:T(1,128)} %param.19), channel_id=1, replica_groups=mesh['seq'=32,'dp'=8] {'seq'}, dimensions={1}, use_global_device_ids=true | all-gather | bytes 16896 | tf_op jit(solution)/shard_map/all_gather | solution.py:195
  269.7 3.4 reshape.1318
  273.1 1.7 copy.198
  276.2 5.8 reshape.1316
  282.0 1.7 copy.200
  297.0 1.7 copy.135
  298.7 5.8 reshape.1320
  304.5 1.7 copy.199
  307.2 1.7 copy.137
  308.8 1.7 copy.140
  310.5 1.8 copy.141
  312.3 1.7 copy.142
  314.0 1.8 copy.143
  315.8 1.9 copy.144
  317.7 1.7 copy.145
  319.4 1.9 copy.146
  321.3 2.1 copy.147
  325.0 2.0 copy.149
  327.0 2.2 copy.150
  329.2 1.7 copy.151
  330.9 2.2 copy.152
  333.1 2.3 copy.153
  337.0 2.3 copy.155
  339.3 2.2 copy.156
  341.6 1.7 copy.157
  343.2 2.2 copy.158
  348.7 2.3 fusion.228
  364.0 1.9 fusion.233
  368.4 2.0 fusion.234
  374.2 17.3 %copy.221 = bf16[1,4096,128]{2,0,1:T(2,128)(2,1)} copy(bf16[1,4096,128]{2,1,0:T(8,128)(2,1)S(1)} %bitcast.546) | data formatting | bytes 2097152 | tf_op jit(solution)/shard_map/broadcast_in_dim | solution.py:198
  391.4 23.4 %reduce.38 = bf16[4096,128]{1,0:T(8,128)(2,1)S(1)} reduce(bf16[4096,1,128]{2,1,0:T(2,128)(2,1)} %bitcast.521, bf16[]{:T(256)} %broadcast.823), dimensions={1}, to_apply=%bitcast.486.reduce_sub_computation | reduce | bytes 2097154
  416.0 4.9 all-to-all-start.3
  422.3 15.4 %all-to-all-done.3 = bf16[32,2,8192]{2,1,0:T(2,128)(2,1)S(1)} async-done(((bf16[32,2,8192]{2,1,0:T(2,128)(2,1)}), bf16[32,2,8192]{2,1,0:T(2,128)(2,1)S(1)}, u32[]{:S(2)}, u32[]{:S(2)}) %all-to-all-start.3) | async-done | bytes 1048608 | tf_op jit(solution)/shard_map/all_to_all | solution.py:197
  437.8 3.4 reshape.1322
  441.2 4.8 bitcast_convert_fusion
  446.0 2.9 copy.163
  449.0 19.6 %all-gather = f32[32,1,32]{2,1,0:T(1,128)S(1)} all-gather(f32[1,1,32]{2,1,0:T(1,128)S(1)} %bitcast.608), channel_id=1, replica_groups=mesh['seq'=32,'dp'=8] {'seq'}, dimensions={0}, use_global_device_ids=true | all-gather | bytes 4224 | tf_op jit(solution)/shard_map/all_gather | solution.py:27
  471.2 3.4 fusion.236
  474.7 4.4 fusion.41
  480.4 2.7 fusion.35
  483.1 5.7 fusion.163
  492.3 77.3 %all-gather.9.cloned.1.call-done = f32[32,32,16,128]{3,2,1,0:T(8,128)} async-done(((f32[1,32,16,128]{3,2,1,0:T(8,128)}), f32[32,32,16,128]{3,2,1,0:T(8,128)}) %all-gather.9.cloned.1.call-update) | async-done | bytes 8388624 | tf_op jit(solution)/shard_map/all_gather | solution.py:27
  569.7 53.6 %while.28 = (s32[]{:T(128)}, f32[32,16,128]{2,1,0:T(8,128)S(1)}, s32[]{:T(128)}, f32[32,32]{1,0:T(8,128)}, f32[32,32,16,128]{3,2,1,0:T(8,128)}, /*index=5*/s32[]{:T(128)}, s32[]{:T(128)}, s32[]{:T(128)}, s32[]{:T(128)}) while((s32[]{:T(128)}, f32[32,16,128]{2,1,0:T(8,128)S(1)}, s32[]{:T(128)}, f32[32,32]{1,0:T(8,128)}, ...), condition=%wide.region_21.22_spmd, body=%wide.region_20.21_spmd.sunk | while | flops 131078 | bytes 786963 | solution.py:36
  628.6 3.9 collective-permute-start.2
  636.6 5.1 convolution_bitcast_fusion
  641.8 100.9 %reduce-scatter.2.cloned.1.call-done = f32[1024,288]{0,1:T(8,128)} async-done(((f32[8192,288]{0,1:T(8,128)}), f32[1024,288]{0,1:T(8,128)}) %reduce-scatter.2.cloned.1.call-update) | async-done | bytes 1179664 | tf_op jit(solution)/shard_map/reduce_scatter | solution.py:236
  742.7 116.8 %all-reduce.11.cloned.1.call-done = f32[1024,288]{0,1:T(8,128)} async-done(((f32[1024,288]{0,1:T(8,128)}), f32[1024,288]{0,1:T(8,128)}) %all-reduce.11.cloned.1.call-update) | async-done | bytes 1179664 | tf_op jit(solution)/shard_map/psum | solution.py:242
  859.5 2.4 copy.247
  (366 shorter events, 138.1 us)
Async XLA Ops:
  6.5 66.2 %copy-start = (bf16[1,128,8192]{2,1,0:T(8,128)(2,1)S(1)}, bf16[1,128,8192]{2,1,0:T(8,128)(2,1)}, u32[]{:S(2)}) copy-start(bf16[1,128,8192]{2,1,0:T(8,128)(2,1)} %param.15) | copy-start | bytes 6291460
  6.5 66.2 %all-gather.5.cloned.1.call-start = ((), (), s32[]{:S(2)}) async-start(), calls=%async_computation.5 | async-start | bytes 5308416 | tf_op jit(solution)/shard_map/all_gather | solution.py:179
  7.3 462.4 %all-gather.7.cloned.1.call-start = ((), (), s32[]{:S(2)}) async-start(), calls=%async_computation.6 | async-start | bytes 8650752 | tf_op jit(solution)/shard_map/all_gather | solution.py:27
  8.0 68.5 %copy-start.60 = (f32[128]{0:T(128)}, f32[128]{0:T(128)S(1)}, u32[]{:S(2)}) copy-start(f32[128]{0:T(128)S(1)} %get-tuple-element.217) | copy-start | bytes 1540
  8.0 7.0 collective-permute-start
  15.1 67.1 %copy-start.48 = (f32[1,256]{1,0:T(1,128)}, f32[1,256]{1,0:T(1,128)S(1)}, u32[]{:S(2)}) copy-start(f32[1,256]{1,0:T(1,128)S(1)} %get-tuple-element.205) | copy-start | bytes 3076
  15.1 67.1 %copy-start.50 = (f32[1,256]{1,0:T(1,128)}, f32[1,256]{1,0:T(1,128)S(1)}, u32[]{:S(2)}) copy-start(f32[1,256]{1,0:T(1,128)S(1)} %get-tuple-element.206) | copy-start | bytes 3076
  15.1 67.1 %copy-start.51 = (f32[1,256]{1,0:T(1,128)}, f32[1,256]{1,0:T(1,128)S(1)}, u32[]{:S(2)}) copy-start(f32[1,256]{1,0:T(1,128)S(1)} %get-tuple-element.208) | copy-start | bytes 3076
  15.1 67.1 %copy-start.52 = (f32[1,256]{1,0:T(1,128)}, f32[1,256]{1,0:T(1,128)S(1)}, u32[]{:S(2)}) copy-start(f32[1,256]{1,0:T(1,128)S(1)} %get-tuple-element.207) | copy-start | bytes 3076
  19.5 62.0 %copy-start.55 = (f32[128]{0:T(128)}, f32[128]{0:T(128)S(1)}, u32[]{:S(2)}) copy-start(f32[128]{0:T(128)S(1)} %get-tuple-element.213) | copy-start | bytes 1540
  19.5 62.7 %copy-start.63 = (pred[128]{0:T(512)(128)(4,1)}, pred[128]{0:T(512)(128)(4,1)S(1)}, u32[]{:S(2)}) copy-start(pred[128]{0:T(512)(128)(4,1)S(1)} %get-tuple-element.214) | copy-start | bytes 388
  19.5 62.7 %copy-start.64 = (pred[128]{0:T(512)(128)(4,1)}, pred[128]{0:T(512)(128)(4,1)S(1)}, u32[]{:S(2)}) copy-start(pred[128]{0:T(512)(128)(4,1)S(1)} %get-tuple-element.216) | copy-start | bytes 388
  19.5 62.7 %copy-start.65 = (pred[128]{0:T(512)(128)(4,1)}, pred[128]{0:T(512)(128)(4,1)S(1)}, u32[]{:S(2)}) copy-start(pred[128]{0:T(512)(128)(4,1)S(1)} %get-tuple-element.215) | copy-start | bytes 388
  19.5 60.7 %copy-start.66 = (f32[32]{0:T(128)S(1)}, f32[32]{0:T(128)}, u32[]{:S(2)}) copy-start(f32[32]{0:T(128)} %param.23) | copy-start | bytes 388
  19.5 60.7 %copy-start.68 = (f32[32]{0:T(128)S(1)}, f32[32]{0:T(128)}, u32[]{:S(2)}) copy-start(f32[32]{0:T(128)} %param.22) | copy-start | bytes 388
  19.6 64.8 %copy-start.26 = (bf16[1,128,1024]{2,1,0:T(8,128)(2,1)S(1)}, bf16[1,128,1024]{2,1,0:T(8,128)(2,1)}, u32[]{:S(2)}) copy-start(bf16[1,128,1024]{2,1,0:T(8,128)(2,1)} %param.17) | copy-start | bytes 786436
  76.5 25.4 %copy-start.10 = (f32[128,288]{0,1:T(8,128)}, f32[128,288]{0,1:T(8,128)S(1)}, u32[]{:S(2)}) copy-start(f32[128,288]{0,1:T(8,128)S(1)} %fusion.43) | copy-start | bytes 442372
  76.6 5.6 collective-permute-start.1
  80.4 2.9 copy-start.20
  80.6 2.6 copy-start.15
  81.5 1.8 copy-start.53
  82.1 19.7 %copy-start.29 = (f32[128,32]{0,1:T(8,128)}, f32[128,32]{0,1:T(8,128)S(1)}, u32[]{:S(2)}) copy-start(f32[128,32]{0,1:T(8,128)S(1)} %get-tuple-element.196) | copy-start | bytes 49156
  126.9 54.2 %all-to-all-start = ((bf16[32,2,8192]{2,1,0:T(2,128)(2,1)}), bf16[32,2,8192]{2,1,0:T(2,128)(2,1)S(1)}, u32[]{:S(2)}, u32[]{:S(2)}) async-start(bf16[32,2,8192]{2,1,0:T(2,128)(2,1)} %reshape.1317), calls=%async_computation | async-start | bytes 2097152 | tf_op jit(solution)/shard_map/all_to_all | solution.py:192
  181.1 45.9 %all-to-all-start.2 = ((bf16[32,2,8192]{2,1,0:T(2,128)(2,1)}), bf16[32,2,8192]{2,1,0:T(2,128)(2,1)}, u32[]{:S(2)}, u32[]{:S(2)}) async-start(bf16[32,2,8192]{2,1,0:T(2,128)(2,1)} %reshape.1315), calls=%async_computation.2 | async-start | bytes 2097152 | tf_op jit(solution)/shard_map/all_to_all | solution.py:193
  227.0 71.7 %all-to-all-start.1 = ((bf16[32,2,8192]{2,1,0:T(2,128)(2,1)}), bf16[32,2,8192]{2,1,0:T(2,128)(2,1)}, u32[]{:S(2)}, u32[]{:S(2)}) async-start(bf16[32,2,8192]{2,1,0:T(2,128)(2,1)} %reshape.1319), calls=%async_computation.1 | async-start | bytes 2097152 | tf_op jit(solution)/shard_map/all_to_all | solution.py:191
  264.2 4.9 copy-start.18
  283.7 9.4 %copy-start.1 = (bf16[1,128,4096]{1,2,0:T(8,128)(2,1)}, bf16[1,128,4096]{1,2,0:T(8,128)(2,1)S(1)}, u32[]{:S(2)}) copy-start(bf16[1,128,4096]{1,2,0:T(8,128)(2,1)S(1)} %copy.200) | copy-start | bytes 3145732
  348.7 2.7 copy-start.24
  348.7 2.7 copy-start.36
  348.7 2.7 copy-start.57
  348.7 2.7 copy-start.59
  348.7 2.7 copy-start.75
  348.7 2.7 copy-start.82
  354.9 1.7 copy-start.14
  355.0 1.7 copy-start.33
  355.0 1.7 copy-start.46
  355.0 1.7 copy-start.47
  416.0 21.8 %all-to-all-start.3 = ((bf16[32,2,8192]{2,1,0:T(2,128)(2,1)}), bf16[32,2,8192]{2,1,0:T(2,128)(2,1)S(1)}, u32[]{:S(2)}, u32[]{:S(2)}) async-start(bf16[32,2,8192]{2,1,0:T(2,128)(2,1)} %reshape.1321), calls=%async_computation.3 | async-start | bytes 2097152 | tf_op jit(solution)/shard_map/all_to_all | solution.py:197
  420.9 148.8 %all-gather.9.cloned.1.call-start = ((), (), s32[]{:S(2)}) async-start(), calls=%async_computation.7 | async-start | bytes 8650752 | tf_op jit(solution)/shard_map/all_gather | solution.py:27
  446.0 2.9 copy-start.16
  446.0 3.0 copy-start.76
  446.0 22.6 %copy-start.38 = (f32[128,32]{0,1:T(8,128)S(1)}, f32[128,32]{0,1:T(8,128)}, u32[]{:S(2)}) copy-start(f32[128,32]{0,1:T(8,128)} %get-tuple-element.195) | copy-start | bytes 49156
  446.0 22.6 %copy-start.61 = (f32[128]{0:T(128)S(1)}, f32[128]{0:T(128)}, u32[]{:S(2)}) copy-start(f32[128]{0:T(128)} %get-tuple-element.212) | copy-start | bytes 1540
  469.7 5.0 copy-start.21
  469.7 5.0 copy-start.25
  471.2 7.8 copy-start.42
  483.1 259.6 %reduce-scatter.2.cloned.1.call-start = ((), (), s32[]{:S(2)}) async-start(), calls=%async_computation.8 | async-start | bytes 10616832 | tf_op jit(solution)/shard_map/reduce_scatter | solution.py:236
  483.1 6.4 copy-start.3
  488.8 1.9 copy-start.7
  492.3 133.1 %copy-start.8 = (f32[8,128,128]{2,1,0:T(8,128)S(1)}, f32[8,128,128]{2,1,0:T(8,128)}, u32[]{:S(2)}) copy-start(f32[8,128,128]{2,1,0:T(8,128)} %copy-done.7) | copy-start | bytes 1572868
  623.3 4.8 copy-start.49
  624.6 8.1 copy-start.22
  624.6 8.1 copy-start.28
  624.6 8.1 copy-start.54
  624.6 8.1 copy-start.56
  624.6 8.4 copy-start.37
  624.6 8.4 copy-start.39
  624.6 8.4 copy-start.44
  624.6 8.4 copy-start.62
  624.6 9.8 %copy-start.40 = (f32[8,4,128]{2,1,0:T(4,128)S(1)}, f32[8,4,128]{2,1,0:T(4,128)}, u32[]{:S(2)}) copy-start(f32[8,4,128]{2,1,0:T(4,128)} %get-tuple-element.149) | copy-start | bytes 49156
  624.6 9.8 %copy-start.67 = (f32[32]{0:T(128)S(1)}, f32[32]{0:T(128)}, u32[]{:S(2)}) copy-start(f32[32]{0:T(128)} %param.23) | copy-start | bytes 388
  624.6 9.8 %copy-start.69 = (f32[32]{0:T(128)S(1)}, f32[32]{0:T(128)}, u32[]{:S(2)}) copy-start(f32[32]{0:T(128)} %param.22) | copy-start | bytes 388
  628.6 6.7 collective-permute-start.2
  641.7 217.7 %all-reduce.11.cloned.1.call-start = ((), (), s32[]{:S(2)}) async-start(), calls=%async_computation.9 | async-start | bytes 2359296 | tf_op jit(solution)/shard_map/psum | solution.py:242
  (33 other events, 41.6 us)
Sparse Core Ops, SparseCore 0:
  9.2 63.5 all-gather.4
  84.5 59.4 all-gather.6
  483.2 86.4 all-gather.8
  641.9 100.7 reduce-scatter.1
  745.8 113.6 all-reduce.10
where the time goes:
time: 882 us; the launch traced here: 869 us
  waiting for transfers between devices  364 us (41%)
  local copies, waits for them, and re-layouts  184 us (21%)
  other arithmetic  161 us (18%)
  matrix products  51.1 us (6%)
  blocking collectives  49.4 us (6%)
  starting transfers between devices  41.1 us (5%)
  between operations  15.8 us (2%)
    psum x1, waiting for transfers between devices, local(): summed = lax.psum(row_sums, 'seq')  117 us
    reduce_scatter x1, waiting for transfers between devices, local(): lax.psum_scatter(jnp.dot(columns.T, grad_rounded, preferred_element_type=...  101 us
    unnamed x4, other arithmetic  95.6 us
    all_gather x2, waiting for transfers between devices, prefix(): gathered = jax.tree.map(lambda a: lax.all_gather(a, axis), part)  77.3 us
    all_gather x1, waiting for transfers between devices, local(): lax.all_gather(w_proj, 'dp', axis=0, tiled=True)  53.2 us
    unnamed x181, local copies, waits for them, and re-layouts  42.7 us
    add x31, other arithmetic, combine_states(): later[0][:, None, None] * earlier[1] + later[1]  32.9 us
    all_gather x1, blocking collectives, local(): doc_all = lax.all_gather(doc_ids, 'seq', axis=1, tiled=True)  29.8 us
  transfers between devices with their start and end apart: 12, of which 6 were waited for; matrix products, arithmetic and copies ran while one was open for 36% of the time, Pallas kernels for 0%

commit v1 on v0

v1 whole, which is shorter than its diff:
```python
import math

import jax
import jax.numpy as jnp
from jax import lax
from jax.experimental import pallas as pl
from jax.experimental.pallas import tpu as pltpu
from jax.sharding import PartitionSpec as P

D = 8192
HEADS = 32
GROUPS = 8
SHARE = 4
DIM = 128
STATE = 16
TAPS = 4
SEQ = 4096
ROWS = 128
BLOCKS = SEQ // ROWS
PARTS = 8
DOC_ROWS = 16
TEACH_ROWS = 2 * ROWS + DOC_ROWS
COLS = 40
SPAN = 256
CHUNKS = SEQ // SPAN
KEYS = 512
PAD = 256
GRAD_ROWS = 48
QUARTER = SEQ // SHARE

F32 = jnp.float32
BF16 = jnp.bfloat16
NEG = -1e30
VMEM = pl.BlockSpec(memory_space=pltpu.VMEM)
SMEM = pl.BlockSpec(memory_space=pltpu.SMEM)

NT = (((1,), (1,)), ((), ()))


def params(mib=56):
    return pltpu.CompilerParams(vmem_limit_bytes=mib << 20)


def mm(a, b):
    return jnp.dot(a, b, preferred_element_type=F32)


def mm_nt(a, b):
    return lax.dot_general(a, b, NT, preferred_element_type=F32)


def split(x):
    high = x.astype(BF16)
    return high, (x - high.astype(F32)).astype(BF16)


def doc_start(position, n_ref):
    start = jnp.where(position >= n_ref[0], n_ref[0], 0)
    start = jnp.where(position >= n_ref[1], n_ref[1], start)
    return jnp.where(position >= n_ref[2], n_ref[2], start)


def scalar_start(position, n_ref):
    return doc_start(position, n_ref)


def pack_teacher_kernel(q_ref, k_ref, v_ref, doc_ref, out_ref):
    docs = jnp.broadcast_to(doc_ref[...].astype(F32), (DOC_ROWS, ROWS)).astype(BF16)
    for h in range(HEADS):
        g = h // SHARE
        out_ref[h, 0:ROWS, :] = q_ref[0, :, h * DIM : (h + 1) * DIM]
        source = k_ref if h % 2 == 0 else v_ref
        out_ref[h, ROWS : 2 * ROWS, :] = source[0, :, g * DIM : (g + 1) * DIM]
        out_ref[h, 2 * ROWS :, :] = docs


def pack_teacher(q, k, v, docs):
    return pl.pallas_call(
        pack_teacher_kernel,
        out_shape=jax.ShapeDtypeStruct((HEADS, TEACH_ROWS, DIM), BF16),
        in_specs=[VMEM] * 4,
        out_specs=VMEM,
        compiler_params=params(32),
        cost_estimate=pl.CostEstimate(flops=0, bytes_accessed=4 << 20, transcendentals=0),
    )(q, k, v, docs)


def pack_hidden_kernel(hid_ref, out_ref):
    for g in range(GROUPS):
        for d in range(PARTS):
            at = d * 1024 + g * 128
            out_ref[g, :, d * 128 : (d + 1) * 128] = hid_ref[0, :, at : at + 128]


def pack_hidden(hidden):
    return pl.pallas_call(
        pack_hidden_kernel,
        out_shape=jax.ShapeDtypeStruct((GROUPS, ROWS, D // GROUPS), BF16),
        in_specs=[VMEM],
        out_specs=VMEM,
        compiler_params=params(32),
        cost_estimate=pl.CostEstimate(flops=0, bytes_accessed=4 << 20, transcendentals=0),
    )(hidden)


def project_kernel(core_ref, hid_ref, own_ref, other_ref, out_ref, acc_ref):
    step = pl.program_id(0)
    half = own_ref.shape[1]
    mine = pl.multiple_of(core_ref[0] * half, half)
    theirs = pl.multiple_of((1 - core_ref[0]) * half, half)
    part = mm(hid_ref[0, :, pl.ds(mine, half)], own_ref[0])
    part = part + mm(hid_ref[0, :, pl.ds(theirs, half)], other_ref[0])

    @pl.when(step == 0)
    def _():
        acc_ref[...] = jnp.zeros_like(acc_ref)

    acc_ref[:, : part.shape[1]] += part

    @pl.when(step == PARTS - 1)
    def _():
        turned = acc_ref[...].T
        for h in range(HEADS):
            g = h // SHARE
            out_ref[h, 0:STATE, :] = turned[g * STATE : (g + 1) * STATE]
            out_ref[h, STATE : 2 * STATE, :] = turned[128 + g * STATE : 128 + (g + 1) * STATE]
            out_ref[h, 2 * STATE :, :] = jnp.broadcast_to(
                turned[256 + h : 257 + h], (COLS - 2 * STATE, ROWS)
            )


def project(core, hidden, own, other):
    width = own.shape[2]
    half = own.shape[1]
    return pl.pallas_call(
        project_kernel,
        out_shape=jax.ShapeDtypeStruct((HEADS, COLS, ROWS), F32),
        grid_spec=pltpu.PrefetchScalarGridSpec(
            num_scalar_prefetch=1,
            grid=(PARTS,),
            in_specs=[
                pl.BlockSpec((1, ROWS, 2 * half), lambda i, c: (0, 0, i)),
                pl.BlockSpec((1, half, width), lambda i, c: (i, 0, 0)),
                pl.BlockSpec((1, half, width), lambda i, c: (i, 0, 0)),
            ],
            out_specs=pl.BlockSpec((HEADS, COLS, ROWS), lambda i, c: (0, 0, 0)),
            scratch_shapes=[pltpu.VMEM((ROWS, 384), F32)],
        ),
        compiler_params=params(32),
        cost_estimate=pl.CostEstimate(
            flops=2 * ROWS * D * 288, bytes_accessed=8 << 20, transcendentals=0
        ),
    )(core, hidden, own, other)


def attend_kernel(
    core_ref, own_ref, other_ref, teach_ref, v_ref, vt_ref, n_ref, keys, turned, scores
):
    docs = jnp.max(own_ref[:, 2 * ROWS :, :].astype(F32), axis=1)
    for d in range(3):
        n_ref[d] = jnp.sum((docs < d + 0.5).astype(F32)).astype(jnp.int32)
    n_ref[3] = 0
    keys[0:PAD, :] = jnp.zeros((PAD, DIM), BF16)
    turned[:, 0:PAD] = jnp.zeros((DIM, PAD), BF16)

    @pl.when(core_ref[0] == 0)
    def _():
        for s in range(BLOCKS):
            keys[PAD + s * ROWS : PAD + (s + 1) * ROWS, :] = own_ref[s, ROWS : 2 * ROWS, :]
            v_ref[s * ROWS : (s + 1) * ROWS, :] = other_ref[s]

    @pl.when(core_ref[0] != 0)
    def _():
        for s in range(BLOCKS):
            keys[PAD + s * ROWS : PAD + (s + 1) * ROWS, :] = other_ref[s]
            v_ref[s * ROWS : (s + 1) * ROWS, :] = own_ref[s, ROWS : 2 * ROWS, :]

    for s in range(BLOCKS):
        block = v_ref[s * ROWS : (s + 1) * ROWS, :].astype(F32).T.astype(BF16)
        turned[:, PAD + s * ROWS : PAD + (s + 1) * ROWS] = block
        vt_ref[:, s * ROWS : (s + 1) * ROWS] = block

    scale = DIM ** (-0.5) * math.log2(math.e)

    def rows(i, carry):
        q0 = i * SPAN
        query = jnp.concatenate([own_ref[2 * i, 0:ROWS, :], own_ref[2 * i + 1, 0:ROWS, :]], 0)
        first = scalar_start(q0, n_ref)
        last = scalar_start(q0 + SPAN - 1, n_ref)
        count = (q0 + SPAN - first + KEYS - 1) // KEYS
        q_at = q0 + lax.broadcasted_iota(jnp.int32, (1, SPAN), 1)
        start = doc_start(q_at, n_ref)

        def score(j, top):
            low = q0 + SPAN - (j + 1) * KEYS
            at = pl.multiple_of(low + PAD, SPAN)
            s = mm_nt(keys[pl.ds(at, KEYS), :], query)
            k_at = low + lax.broadcasted_iota(jnp.int32, (KEYS, SPAN), 0)
            s = jnp.where((k_at <= q_at) & (k_at >= start), s, NEG)
            scores[pl.ds(pl.multiple_of(j * KEYS, KEYS), KEYS), :] = s
            return jnp.maximum(top, jnp.max(s.reshape(KEYS // 8, 8, SPAN), axis=0))

        def score_plain(j, top):
            low = q0 + SPAN - (j + 1) * KEYS
            at = pl.multiple_of(low + PAD, SPAN)
            s = mm_nt(keys[pl.ds(at, KEYS), :], query)
            scores[pl.ds(pl.multiple_of(j * KEYS, KEYS), KEYS), :] = s
            return jnp.maximum(top, jnp.max(s.reshape(KEYS // 8, 8, SPAN), axis=0))

        top = score(0, jnp.full((8, SPAN), NEG, F32))
        inner = jnp.clip((q0 + SPAN - last) // KEYS, 1, count)
        top = lax.fori_loop(1, inner, score_plain, top)
        top = lax.fori_loop(inner, count, score, top)
        top = jnp.max(top, axis=0, keepdims=True)

        def mix(j, state):
            total, out = state
            low = q0 + SPAN - (j + 1) * KEYS
            at = pl.multiple_of(low + PAD, SPAN)
            s = scores[pl.ds(pl.multiple_of(j * KEYS, KEYS), KEYS), :]
            p = jnp.exp2((s - top) * scale)
            total = total + jnp.sum(p.reshape(KEYS // 8, 8, SPAN), axis=0)
            out = out + mm(turned[:, pl.ds(at, KEYS)], p.astype(BF16))
            return total, out

        total, out = lax.fori_loop(
            0, count, mix, (jnp.zeros((8, SPAN), F32), jnp.zeros((DIM, SPAN), F32))
        )
        total = jnp.sum(total, axis=0, keepdims=True)
        teach_ref[:, pl.ds(pl.multiple_of(q0, SPAN), SPAN)] = (out / total).astype(BF16)
        return carry

    lax.fori_loop(0, CHUNKS, rows, 0)


def attend(core, own, other):
    return pl.pallas_call(
        attend_kernel,
        out_shape=(
            jax.ShapeDtypeStruct((DIM, SEQ), BF16),
            jax.ShapeDtypeStruct((SEQ, DIM), BF16),
            jax.ShapeDtypeStruct((DIM, SEQ), BF16),
            jax.ShapeDtypeStruct((4,), jnp.int32),
        ),
        in_specs=[SMEM, VMEM, VMEM],
        out_specs=(VMEM, VMEM, VMEM, SMEM),
        scratch_shapes=[
            pltpu.VMEM((PAD + SEQ, DIM), BF16),
            pltpu.VMEM((DIM, PAD + SEQ), BF16),
            pltpu.VMEM((SEQ + KEYS, SPAN), F32),
        ],
        compiler_params=params(),
        cost_estimate=pl.CostEstimate(
            flops=8 << 30, bytes_accessed=8 << 20, transcendentals=8 << 20
        ),
    )(core, own, other)


def scan_lanes(x, reverse):
    width = x.shape[1]
    lane = lax.broadcasted_iota(jnp.int32, x.shape, 1)
    step = 1
    while step < width:
        if reverse:
            moved = pltpu.roll(x, width - step, 1)
            x = x + jnp.where(lane < width - step, moved, 0.0)
        else:
            moved = pltpu.roll(x, step, 1)
            x = x + jnp.where(lane >= step, moved, 0.0)
        step *= 2
    return x


def student_kernel(
    head_ref,
    n_ref,
    bias_ref,
    rate_ref,
    taps_ref,
    proj_ref,
    teach_ref,
    v_ref,
    vt_ref,
    out_ref,
    source,
    steps,
    cums,
    columns,
    pre_s,
    sig_s,
    z_s,
    dc_s,
    q_s,
    x_s,
    direct_s,
    state_s,
    dstate_s,
    *,
    weight,
):
    head = head_ref[0]
    group = head // SHARE
    bias = bias_ref[head]
    rate = rate_ref[head]
    lane = lax.broadcasted_iota(jnp.int32, (1, SPAN), 1)
    deep = lax.broadcasted_iota(jnp.int32, (SPAN, SPAN), 0)
    taps_b = taps_ref[pl.ds(pl.multiple_of(group * STATE, STATE), STATE), :]
    taps_c = taps_ref[pl.ds(pl.multiple_of(128 + group * STATE, STATE), STATE), :]
    taps = jnp.concatenate([taps_b, taps_c], 0)

    source[:, 0:128] = jnp.zeros((2 * STATE, 128), F32)
    for s in range(BLOCKS):
        source[:, 128 + s * ROWS : 128 + (s + 1) * ROWS] = proj_ref[s, 0 : 2 * STATE, :]
        steps[s // 2 : s // 2 + 1, (s % 2) * ROWS : (s % 2 + 1) * ROWS] = proj_ref[
            s, 2 * STATE : 2 * STATE + 1, :
        ]
    raw = steps[...] + bias
    step_all = jnp.maximum(raw, 0.0) + jnp.log1p(jnp.exp(-jnp.abs(raw)))
    slope_all = 1.0 / (1.0 + jnp.exp(-raw))
    steps[...] = step_all
    cum_all = scan_lanes(-step_all * rate, False)
    cums[...] = cum_all
    cum_turned = cum_all.T
    for c in range(CHUNKS):
        columns[c] = cum_turned[:, c : c + 1]

    def marks(c):
        base = c * SPAN
        at = base + lane
        start = doc_start(at, n_ref)
        last = scalar_start(base + SPAN - 1, n_ref)
        return base, at, start, last

    def forward(c, state):
        base, at, start, last = marks(c)
        wide = pl.multiple_of(base, SPAN)
        rows = source[:, pl.ds(wide, SPAN + 128)]
        pre = taps[:, 0:1] * rows[:, 128:]
        for j in range(1, TAPS):
            lagged = jnp.where(at - j >= start, pltpu.roll(rows, j, 1)[:, 128:], 0.0)
            pre = pre + taps[:, j : j + 1] * lagged
        sig = 1.0 / (1.0 + jnp.exp(-pre))
        gates = pre * sig
        pre_s[:, pl.ds(wide, SPAN)] = pre
        sig_s[:, pl.ds(wide, SPAN)] = sig
        gate_c = gates[STATE:]
        step = steps[pl.ds(c, 1), :]
        cum = cums[pl.ds(c, 1), :]
        ended = cum[:, SPAN - 1 :]
        fed = gates[:STATE] * step
        fed_high, fed_low = split(fed)
        c_high, c_low = split(gate_c)
        fed_stack = jnp.concatenate([fed, fed_low.astype(F32), fed], 0)
        left = fed_stack.T.astype(BF16)
        inner = mm(left, jnp.concatenate([c_high, c_high, c_low], 0))
        allowed = (deep <= lane) & (deep >= start - base)
        fade = jnp.exp(jnp.where(allowed, cum - columns[c], NEG))
        mixing = fade * inner
        mix_high, mix_low = split(mixing)
        values = v_ref[pl.ds(wide, SPAN), :]
        turned = vt_ref[:, pl.ds(wide, SPAN)]
        enter = jnp.where(start < base, jnp.exp(cum), 0.0)
        entered = gate_c * enter
        in_high, in_low = split(entered)
        s_high, s_low = split(state)
        state_left = jnp.concatenate([state, s_low.astype(F32), state], 0).T.astype(BF16)
        out = mm(turned, mix_high) + mm(turned, mix_low)
        out = out + mm(state_left, jnp.concatenate([in_high, in_high, in_low], 0))
        wanted = teach_ref[:, pl.ds(wide, SPAN)].astype(F32)
        error = (out - wanted) * weight
        q_s[pl.ds(c, 1), :] = jnp.sum(out * error, axis=0, keepdims=True)
        e_high, e_low = split(error)
        e_stack = jnp.concatenate([e_high, e_low], 0)
        pulled = fade * mm(jnp.concatenate([values, values], 1), e_stack)
        h_high, h_low = split(pulled)
        c_stack = jnp.concatenate([c_high, c_low], 0)
        z = mm_nt(c_stack, h_high) + mm_nt(c_stack, h_low)
        z_s[:, pl.ds(wide, SPAN)] = z[:STATE] + z[STATE:]
        fed_pair = jnp.concatenate([fed_high, fed_low], 0)
        dc = mm(fed_pair, h_high) + mm(fed_pair, h_low)
        s_pair = jnp.concatenate([s_high, s_low], 0)
        dc_in = mm(s_pair, e_high) + mm(s_pair, e_low)
        dc_s[:, pl.ds(wide, SPAN)] = dc[:STATE] + dc[STATE:] + enter * (dc_in[:STATE] + dc_in[STATE:])
        in_pair = jnp.concatenate([in_high, in_low], 0)
        ds = mm_nt(in_pair, e_high) + mm_nt(in_pair, e_low)
        dstate_s[c] = ds[:STATE] + ds[STATE:]
        state_s[c] = state
        tail = jnp.where(at >= last, jnp.exp(ended - cum), 0.0)
        t_high, t_low = split(fed * tail)
        new = mm(jnp.concatenate([t_high, t_low], 0), values)
        keep = jnp.where(last < base, 1.0, 0.0) * jnp.exp(ended)
        return keep * state + new[:STATE] + new[STATE:]

    final = lax.fori_loop(0, CHUNKS, forward, jnp.zeros((STATE, DIM), F32))
    state_s[CHUNKS] = final

    def backward(k, carried):
        dstate, later = carried
        c = CHUNKS - 1 - k
        base, at, start, last = marks(c)
        wide = pl.multiple_of(base, SPAN)
        step = steps[pl.ds(c, 1), :]
        cum = cums[pl.ds(c, 1), :]
        ended = cum[:, SPAN - 1 :]
        tail = jnp.where(at >= last, jnp.exp(ended - cum), 0.0)
        d_high, d_low = split(dstate)
        turned = vt_ref[:, pl.ds(wide, SPAN)]
        through = mm(jnp.concatenate([d_high, d_low], 0), turned)
        z = z_s[:, pl.ds(wide, SPAN)] + tail * (through[:STATE] + through[STATE:])
        pre = pre_s[:, pl.ds(wide, SPAN)]
        sig = sig_s[:, pl.ds(wide, SPAN)]
        gates = pre * sig
        direct = jnp.sum(gates[:STATE] * z, axis=0, keepdims=True)
        direct_s[pl.ds(c, 1), :] = direct
        crossing = jnp.sum(jnp.sum(dstate * state_s[c + 1], axis=0, keepdims=True), axis=1, keepdims=True)
        x_s[pl.ds(c, 1), :] = jnp.broadcast_to(crossing, (1, SPAN))
        dgates = jnp.concatenate([step * z, dc_s[:, pl.ds(wide, SPAN)]], 0)
        dpre = dgates * (sig + gates * (1.0 - sig))
        rows = jnp.concatenate([dpre, later], 1)
        back = taps[:, 0:1] * rows[:, :SPAN]
        for j in range(1, TAPS):
            reach = jnp.where(at >= doc_start(at + j, n_ref), pltpu.roll(rows, SPAN + 128 - j, 1)[:, :SPAN], 0.0)
            back = back + taps[:, j : j + 1] * reach
        column = pl.multiple_of((c // 2) * ROWS, ROWS)
        out_ref[2 * (c % 2), 0 : 2 * STATE, pl.ds(column, ROWS)] = back[:, :ROWS]
        out_ref[2 * (c % 2) + 1, 0 : 2 * STATE, pl.ds(column, ROWS)] = back[:, ROWS:]
        keep = jnp.where(last < base, 1.0, 0.0) * jnp.exp(ended)
        return keep * dstate + dstate_s[c], dpre[:, :128]

    nothing = (jnp.zeros((STATE, DIM), F32), jnp.zeros((2 * STATE, 128), F32))
    lax.fori_loop(0, CHUNKS, backward, nothing)

    at_all = lax.broadcasted_iota(jnp.int32, (CHUNKS, SPAN), 0) * SPAN
    at_all = at_all + lax.broadcasted_iota(jnp.int32, (CHUNKS, SPAN), 1)
    direct = direct_s[...]
    dlog = scan_lanes(q_s[...] - step_all * direct, True) + x_s[...]
    dlog = jnp.where(at_all > doc_start(at_all, n_ref), dlog, 0.0)
    dstep = (direct - rate * dlog) * slope_all
    for s in range(BLOCKS):
        piece = dstep[s // 2 : s // 2 + 1, (s % 2) * ROWS : (s % 2 + 1) * ROWS]
        out_ref[s % SHARE, 2 * STATE :, (s // SHARE) * ROWS : (s // SHARE + 1) * ROWS] = (
            jnp.broadcast_to(piece, (COLS - 2 * STATE, ROWS))
        )


def student(head, counts, bias, rate, taps, proj, teach, v, vt, weight):
    return pl.pallas_call(
        lambda *refs: student_kernel(*refs, weight=weight),
        out_shape=jax.ShapeDtypeStruct((SHARE, COLS, QUARTER), F32),
        in_specs=[SMEM, SMEM, SMEM, SMEM, VMEM, VMEM, VMEM, VMEM, VMEM],
        out_specs=VMEM,
        scratch_shapes=[
            pltpu.VMEM((2 * STATE, 128 + SEQ), F32),
            pltpu.VMEM((CHUNKS, SPAN), F32),
            pltpu.VMEM((CHUNKS, SPAN), F32),
            pltpu.VMEM((CHUNKS, SPAN, 1), F32),
            pltpu.VMEM((2 * STATE, SEQ), F32),
            pltpu.VMEM((2 * STATE, SEQ), F32),
            pltpu.VMEM((STATE, SEQ), F32),
            pltpu.VMEM((STATE, SEQ), F32),
            pltpu.VMEM((CHUNKS, SPAN), F32),
            pltpu.VMEM((CHUNKS, SPAN), F32),
            pltpu.VMEM((CHUNKS, SPAN), F32),
            pltpu.VMEM((CHUNKS + 1, STATE, DIM), F32),
            pltpu.VMEM((CHUNKS, STATE, DIM), F32),
        ],
        compiler_params=params(),
        cost_estimate=pl.CostEstimate(
            flops=8 << 30, bytes_accessed=8 << 20, transcendentals=4 << 20
        ),
    )(head, counts, bias, rate, taps, proj, teach, v, vt)


def combine_kernel(in_ref, out_ref):
    gates = in_ref[0, : 2 * STATE] + in_ref[1, : 2 * STATE]
    gates = gates + in_ref[2, : 2 * STATE]
    gates = gates + in_ref[3, : 2 * STATE]
    steps = [in_ref[k, 2 * STATE : 2 * STATE + 1] for k in range(SHARE)]
    rest = jnp.zeros((GRAD_ROWS - 2 * STATE - SHARE, QUARTER), F32)
    rounded = jnp.concatenate([gates] + steps + [rest], 0).astype(BF16)
    for g in range(GROUPS):
        out_ref[g] = rounded


def combine(parts):
    return pl.pallas_call(
        combine_kernel,
        out_shape=jax.ShapeDtypeStruct((GROUPS, GRAD_ROWS, QUARTER), BF16),
        in_specs=[VMEM],
        out_specs=VMEM,
        compiler_params=params(32),
    )(parts)


def product_kernel(grad_ref, hid_ref, out_ref):
    for half in range(2):
        left = grad_ref[half * 4 : half * 4 + 4].reshape(4 * GRAD_ROWS, QUARTER)
        left = left.astype(F32)
        keep = jnp.concatenate(
            [left[i * GRAD_ROWS : i * GRAD_ROWS + COLS] for i in range(4)], 0
        ).astype(BF16)
        for d in range(PARTS):
            hid = hid_ref[:, :, d * 128 : (d + 1) * 128].reshape(QUARTER, 128)
            part = mm(keep, hid)
            out_ref[2 * half, d] = part[: 2 * COLS]
            out_ref[2 * half + 1, d] = part[2 * COLS :]


def product(grads, hidden):
    return pl.pallas_call(
        product_kernel,
        out_shape=jax.ShapeDtypeStruct((SHARE, PARTS, 2 * COLS, 128), F32),
        in_specs=[VMEM, VMEM],
        out_specs=VMEM,
        compiler_params=params(32),
        cost_estimate=pl.CostEstimate(
            flops=2 * 320 * 1024 * 1024, bytes_accessed=4 << 20, transcendentals=0
        ),
    )(grads, hidden)


def place_kernel(in_ref, out_ref):
    for g in range(GROUPS):
        gates_b, gates_c, steps = [], [], []
        for k in range(GROUPS):
            block = in_ref[SHARE * g + k // 2]
            at = (k % 2) * COLS
            gates_b.append(block[at : at + STATE])
            gates_c.append(block[at + STATE : at + 2 * STATE])
            steps.append(block[at + 2 * STATE : at + 2 * STATE + SHARE])
        fill = jnp.zeros((96, 128), F32)
        rows = jnp.concatenate(gates_b + gates_c + steps + [fill], 0)
        out_ref[g * 128 : (g + 1) * 128, :] = rows.T[:, :288]


def place(blocks):
    return pl.pallas_call(
        place_kernel,
        out_shape=jax.ShapeDtypeStruct((1024, 288), F32),
        in_specs=[VMEM],
        out_specs=VMEM,
        compiler_params=params(32),
    )(blocks)


def swap_all(x, axis, groups=None):
    return lax.all_to_all(x, axis, 0, 0, tiled=True, axis_index_groups=groups)


def local(hidden, queries, keys, values, docs, w_proj, conv_weight, dt_bias, decay_rate):
    seq_devices = lax.axis_size("seq")
    data_devices = lax.axis_size("dp")
    seq_len = hidden.shape[1] * seq_devices
    weight = 1.0 / math.sqrt(HEADS * DIM * data_devices * seq_len)
    head = lax.axis_index("seq").astype(jnp.int32)
    core = head % 2
    fours = [[SHARE * g + j for j in range(SHARE)] for g in range(GROUPS)]
    eights = [[SHARE * g + j for g in range(GROUPS)] for j in range(SHARE)]
    partner = [(i, i ^ 1) for i in range(seq_devices)]

    half = w_proj.shape[0] // 2
    own_w = lax.all_gather(lax.dynamic_slice_in_dim(w_proj, core * half, half, 0), "dp", axis=0)
    other_w = lax.ppermute(own_w, "seq", partner)

    own = swap_all(pack_teacher(queries, keys, values, docs), "seq")
    other = lax.ppermute(own[:, ROWS : 2 * ROWS, :], "seq", partner)
    proj = swap_all(project(core[None], hidden, own_w, other_w), "seq")
    teach, v, vt, counts = attend(core[None], own, other)
    hidden_packed = pack_hidden(hidden)
    hidden_packed, proj = lax.optimization_barrier((hidden_packed, proj))
    hidden_part = swap_all(hidden_packed, "seq", eights)
    grads = student(
        head[None], counts, dt_bias, decay_rate, conv_weight.T, proj, teach, v, vt, weight
    )
    quarter = combine(swap_all(grads, "seq", fours))
    spread = swap_all(quarter, "seq", eights)
    partial = product(spread, hidden_part)
    partial = jnp.sum(swap_all(partial, "seq", fours), axis=0)
    total = jnp.sum(swap_all(partial, "dp"), axis=0)
    blocks = swap_all(jnp.broadcast_to(total[None], (seq_devices, 2 * COLS, 128)), "seq")
    return place(blocks)


def solution(mesh):
    placed = (
        P("dp", "seq", None),
        P("dp", "seq", None),
        P("dp", "seq", None),
        P("dp", "seq", None),
        P("dp", "seq"),
        P("dp", None),
        P(),
        P(),
        P(),
    )
    return jax.shard_map(
        local, mesh=mesh, in_specs=placed, out_specs=P("dp", None), check_vma=False
    )
```

time: 882 us -> 274 us (0.31); the launches traced: 869 us -> 273 us
  waiting for transfers between devices: 364 us -> 29.1 us
  other arithmetic: 161 us -> 0.11 us
  local copies, waits for them, and re-layouts: 184 us -> 29.7 us
  blocking collectives: 49.4 us -> 127 us
  Pallas kernels: 0 us -> 54.7 us
  matrix products: 51.1 us -> 0 us
  starting transfers between devices: 41.1 us -> 19.5 us
    all_to_all x0 -> x6, blocking collectives: none -> 127 us  [swap_all(): return lax.all_to_all(x, axis, 0, 0, tiled=True, axis_index_groups=groups)]
    psum x1 -> x0, waiting for transfers between devices: 117 us -> none  [local(): summed = lax.psum(row_sums, 'seq')]
    all_gather x3 -> x1, waiting for transfers between devices: 131 us -> 29.1 us  [local(): lax.all_gather(lax.dynamic_slice_in_dim(w_proj, core * half, half, 0), 'd...]
    reduce_scatter x1 -> x0, waiting for transfers between devices: 101 us -> none  [local(): lax.psum_scatter(jnp.dot(columns.T, grad_rounded, preferred_element_type=...]
    unnamed x4 -> x0, other arithmetic: 95.6 us -> none
    slice x53 -> x1, local copies, waits for them, and re-layouts: 59.6 us -> 2.31 us  [local(): other = lax.ppermute(own[:, ROWS:2 * ROWS, :], 'seq', partner)]
    pallas_call x0 -> x8, Pallas kernels: none -> 54.7 us  [the longest x1 26.1 us: student(): pl.pallas_call(lambda *refs: student_kernel(*refs, weight=weight), out_sh...]
    broadcast_in_dim x7 -> x1, local copies, waits for them, and re-layouts: 52.8 us -> 0.09 us  [local(): jnp.broadcast_to(total[None], (seq_devices, 2 * COLS, 128))]
  transfers between devices with their start and end apart: 12 -> 5, of which waited for: 6 -> 1; matrix products, arithmetic and copies ran while one was open for 36% -> 6% of each run, Pallas kernels for 0% -> 10%
where the time goes in v1:
time: 274 us; the launch traced here: 273 us
  blocking collectives  127 us (46%)
  Pallas kernels  54.7 us (20%)
  local copies, waits for them, and re-layouts  29.7 us (11%)
  waiting for transfers between devices  29.1 us (11%)
  starting transfers between devices  19.5 us (7%)
  between operations  13.5 us (5%)
    all_to_all x6, blocking collectives, swap_all(): return lax.all_to_all(x, axis, 0, 0, tiled=True, axis_index_groups=groups)  127 us
    all_gather x1, waiting for transfers between devices, local(): lax.all_gather(lax.dynamic_slice_in_dim(w_proj, core * half, half, 0), 'd...  29.1 us
    pallas_call x1, Pallas kernels, student(): pl.pallas_call(lambda *refs: student_kernel(*refs, weight=weight), out_sh...  26.1 us
    pallas_call x1, Pallas kernels, attend(): pl.pallas_call(attend_kernel, out_shape=(jax.ShapeDtypeStruct((DIM, SEQ),...  20.4 us
    all_to_all x2, starting transfers between devices, swap_all(): return lax.all_to_all(x, axis, 0, 0, tiled=True, axis_index_groups=groups)  15.8 us
    unnamed x25, local copies, waits for them, and re-layouts  11.6 us
    all_gather x2, local copies, waits for them, and re-layouts, local(): lax.all_gather(lax.dynamic_slice_in_dim(w_proj, core * half, half, 0), 'd...  8.98 us
  transfers between devices with their start and end apart: 5, of which 1 were waited for; matrix products, arithmetic and copies ran while one was open for 6% of the time, Pallas kernels for 10%

profile of v1, /device:TPU:1, one launch (start us, length us, event | category | flops | bytes accessed | tf_op | source)
XLA Modules:
  0.0 273.1 jit_solution(10354584581815198410)
XLA Ops:
  6.5 0.0 copy-start
  6.5 0.0 all-gather.3.cloned.1.call-start
  6.5 1.1 copy-done
  7.6 0.7 constant_dynamic-slice_fusion
  8.3 0.0 all-gather.3.cloned.1.call-update
  8.4 0.0 copy-start.6
  8.4 1.2 copy-done.6
  9.6 0.0 copy-start.7
  9.6 0.9 copy-done.7
  10.5 0.0 copy-start.8
  10.5 0.9 copy-done.8
  11.5 0.0 copy-start.9
  11.5 0.7 copy-done.9
  12.1 1.8 shard_map.91
  13.9 8.6 %all-to-all-start = ((bf16[32,272,128]{2,1,0:T(8,128)(2,1)}), bf16[32,272,128]{2,1,0:T(8,128)(2,1)}, u32[]{:S(2)}, u32[]{:S(2)}) async-start(bf16[32,272,128]{2,1,0:T(8,128)(2,1)} %shard_map.91), calls=%async_computation | async-start | bytes 4456448 | tf_op jit(solution)/shard_map/all_to_all | solution.py:547
  22.6 29.1 %all-gather.3.cloned.1.call-done = bf16[4096,288]{0,1:T(8,128)(2,1)} async-done(((bf16[512,288]{0,1:T(8,128)(2,1)}), bf16[4096,288]{0,1:T(8,128)(2,1)}) %all-gather.3.cloned.1.call-update) | async-done | bytes 2359312 | tf_op jit(solution)/shard_map/all_gather | solution.py:562
  51.6 4.5 %copy.19 = bf16[4096,288]{1,0:T(8,128)(2,1)} copy(bf16[4096,288]{0,1:T(8,128)(2,1)} %all-gather.3.cloned.1.call-done) | data formatting | bytes 4718592 | tf_op jit(solution)/shard_map/all_gather | solution.py:562
  56.1 4.5 %copy.20 = bf16[8,512,288]{1,2,0:T(8,128)(2,1)} copy(bf16[8,512,288]{2,1,0:T(8,128)(2,1)} %bitcast.4) | data formatting | bytes 4718592 | tf_op jit(solution)/shard_map/all_gather | solution.py:562
  60.6 0.0 copy-start.3
  60.6 3.5 %collective-permute-start.1 = (bf16[8,512,288]{1,2,0:T(8,128)(2,1)}, bf16[8,512,288]{1,2,0:T(8,128)(2,1)}, u32[]{:S(2)}, u32[]{:S(2)}) collective-permute-start(bf16[8,512,288]{1,2,0:T(8,128)(2,1)} %copy.20), channel_id=1, source_target_pairs={{0,8},{8,0},{16,24},{24,16},{32,40},{40,32},{48,56},{56,48},{64,72... | collective-permute-start | bytes 7077896 | tf_op jit(solution)/shard_map/ppermute | solution.py:563
  64.1 0.0 all-to-all-done.own_ref
  64.1 2.3 slice.4
  66.4 0.0 copy-start.11
  66.4 0.2 collective-permute-start
  66.6 0.0 copy-done.3
  66.6 0.4 shard_map.93
  67.0 0.0 copy-start.4
  67.0 1.4 copy-done.4
  68.4 0.0 copy-done.11
  68.4 0.8 copy.18
  69.2 0.0 collective-permute-done.1
  69.2 4.5 %copy.21.other_ref = bf16[8,512,288]{2,1,0:T(8,128)(2,1)} copy(bf16[8,512,288]{1,2,0:T(8,128)(2,1)} %collective-permute-done.1) | data formatting | bytes 4718592 | tf_op jit(solution)/shard_map/ppermute | solution.py:563
  73.7 0.0 copy-start.1
  73.7 1.9 copy-done.1
  75.6 0.0 copy-start.2
  75.6 1.9 copy-done.2
  77.5 3.7 %shard_map.94 = f32[32,40,128]{2,1,0:T(8,128)} custom-call(s32[1]{0:T(128)} %bitcast.1.core_ref, bf16[1,128,8192]{2,1,0:T(8,128)(2,1)S(1)} %copy-done.3, bf16[8,512,288]{2,1,0:T(8,128)(2,1)S(1)} %bitcast.5, bf16[8,512,288]{2,1,0:T(8,128)(2,1)S(1)} %copy-done.2), custom_call_target="tpu_custom_call" | custom-call | flops 603979776 | bytes 8388608 | tf_op jit(solution)/shard_map/pallas_call | solution.py:135
  81.3 7.2 %all-to-all-start.1 = ((f32[32,40,128]{2,1,0:T(8,128)}), f32[32,40,128]{2,1,0:T(8,128)S(1)}, u32[]{:S(2)}, u32[]{:S(2)}) async-start(f32[32,40,128]{2,1,0:T(8,128)} %shard_map.94), calls=%async_computation.1 | async-start | bytes 1310720 | tf_op jit(solution)/shard_map/all_to_all | solution.py:547
  88.5 0.0 collective-permute-done.other_ref
  88.5 20.4 %shard_map.92 = (bf16[128,4096]{1,0:T(8,128)(2,1)}, bf16[4096,128]{1,0:T(8,128)(2,1)}, bf16[128,4096]{1,0:T(8,128)(2,1)}, s32[4]{0:T(128)}) custom-call(s32[1]{0:T(128)} %bitcast.1.core_ref, bf16[32,272,128]{2,1,0:T(8,128)(2,1)} %all-to-all-done.own_ref, bf16[32,128,128]{2,1,0:T(8,128)(2,1)} %collective-permute-done.other_ref), custom_call_target="tpu_custom_call" | custom-call | flops 8589934592 | bytes 8388608 | tf_op jit(solution)/shard_map/pallas_call | solution.py:237
  108.9 0.0 all-to-all-done.1.refs_5_
  108.9 0.0 copy-start.10
  108.9 0.8 copy-done.10
  109.8 26.1 %shard_map.95 = f32[4,40,1024]{2,1,0:T(8,128)} custom-call(s32[1]{0:T(128)} %bitcast.refs_0_, s32[4]{0:T(128)} %get-tuple-element.11.refs_1_, f32[32]{0:T(128)} %refs_2_.1, f32[32]{0:T(128)} %refs_3_.1, f32[256,4]{1,0:T(8,128)} %bitcast.6, f32[32,40,128]{2,1,0:T(8,128)} %copy-done.10, bf16[128,4096]{1,0:T(8,128)(2,1)} %get-tuple-element.13.refs_6_, ...), custom_call_target="tpu_custom_call" | custom-call | flops 8589934592 | bytes 8388608 | tf_op jit(solution)/shard_map/pallas_call | solution.py:447
  135.8 0.0 copy-start.5
  135.8 12.9 %all_to_all.40.in_ref = f32[4,40,1024]{2,1,0:T(8,128)S(1)} all-to-all(f32[4,40,1024]{2,1,0:T(8,128)} %shard_map.95), channel_id=1, replica_groups={{0,8,16,24},{32,40,48,56},{64,72,80,88},{96,104,112,120},{128,136,144,1..., dimensions={0} | all-to-all | bytes 1310720 | tf_op jit(solution)/shard_map/all_to_all | solution.py:547
  148.7 0.1 shard_map.96
  148.8 18.7 %all_to_all.41.grad_ref = bf16[8,48,1024]{2,1,0:T(8,128)(2,1)S(1)} all-to-all(bf16[8,48,1024]{2,1,0:T(8,128)(2,1)S(1)} %shard_map.96), channel_id=1, replica_groups={{0,32,64,96,128,160,192,224},{8,40,72,104,136,168,200,232},{16,48,80,11..., dimensions={0} | all-to-all | bytes 1572864 | tf_op jit(solution)/shard_map/all_to_all | solution.py:547
  167.5 0.0 copy-done.5
  167.5 28.1 %all_to_all.42.hid_ref = bf16[8,128,1024]{2,1,0:T(8,128)(2,1)S(1)} all-to-all(bf16[8,128,1024]{2,1,0:T(8,128)(2,1)S(1)} %copy-done.5), channel_id=1, replica_groups={{0,32,64,96,128,160,192,224},{8,40,72,104,136,168,200,232},{16,48,80,11..., dimensions={0} | all-to-all | bytes 4194304 | tf_op jit(solution)/shard_map/all_to_all | solution.py:547
  195.6 1.7 shard_map.97
  197.3 22.8 %all_to_all.43 = f32[4,8,80,128]{3,2,1,0:T(8,128)S(1)} all-to-all(f32[4,8,80,128]{3,2,1,0:T(8,128)S(1)} %shard_map.97), channel_id=1, replica_groups={{0,8,16,24},{32,40,48,56},{64,72,80,88},{96,104,112,120},{128,136,144,1..., dimensions={0} | all-to-all | bytes 2621440 | tf_op jit(solution)/shard_map/all_to_all | solution.py:547
  220.1 0.1 reduce_sum.18
  220.2 17.7 %all_to_all.44 = f32[8,80,128]{2,1,0:T(8,128)S(1)} all-to-all(f32[8,80,128]{2,1,0:T(8,128)S(1)} %reduce_sum.18), channel_id=1, replica_groups=mesh['seq'=32,'dp'=8] {'dp'}, dimensions={0} | all-to-all | bytes 655360 | tf_op jit(solution)/shard_map/all_to_all | solution.py:547
  237.9 0.1 broadcast_in_dim.15
  237.9 26.4 %all_to_all.45.in_ref = f32[32,80,128]{2,1,0:T(8,128)S(1)} all-to-all(f32[32,80,128]{2,1,0:T(8,128)S(1)} %broadcast_in_dim.15), channel_id=1, replica_groups=mesh['seq'=32,'dp'=8] {'seq'}, dimensions={0} | all-to-all | bytes 2621440 | tf_op jit(solution)/shard_map/all_to_all | solution.py:547
  264.4 0.5 shard_map.98
  264.8 1.5 copy.22
  (1 shorter events, 0.0 us)
Async XLA Ops:
  6.5 1.1 copy-start
  6.5 45.1 %all-gather.3.cloned.1.call-start = ((), (), s32[]{:S(2)}) async-start(), calls=%async_computation.8 | async-start | bytes 2654208 | tf_op jit(solution)/shard_map/all_gather | solution.py:562
  8.4 1.2 copy-start.6
  9.6 0.9 copy-start.7
  10.5 0.9 copy-start.8
  11.5 0.7 copy-start.9
  13.9 50.2 %all-to-all-start = ((bf16[32,272,128]{2,1,0:T(8,128)(2,1)}), bf16[32,272,128]{2,1,0:T(8,128)(2,1)}, u32[]{:S(2)}, u32[]{:S(2)}) async-start(bf16[32,272,128]{2,1,0:T(8,128)(2,1)} %shard_map.91), calls=%async_computation | async-start | bytes 4456448 | tf_op jit(solution)/shard_map/all_to_all | solution.py:547
  60.6 6.0 %copy-start.3 = (bf16[1,128,8192]{2,1,0:T(8,128)(2,1)S(1)}, bf16[1,128,8192]{2,1,0:T(8,128)(2,1)}, u32[]{:S(2)}) copy-start(bf16[1,128,8192]{2,1,0:T(8,128)(2,1)} %hid_ref.3) | copy-start | bytes 6291460
  60.6 8.6 %collective-permute-start.1 = (bf16[8,512,288]{1,2,0:T(8,128)(2,1)}, bf16[8,512,288]{1,2,0:T(8,128)(2,1)}, u32[]{:S(2)}, u32[]{:S(2)}) collective-permute-start(bf16[8,512,288]{1,2,0:T(8,128)(2,1)} %copy.20), channel_id=1, source_target_pairs={{0,8},{8,0},{16,24},{24,16},{32,40},{40,32},{48,56},{56,48},{64,72... | collective-permute-start | bytes 7077896 | tf_op jit(solution)/shard_map/ppermute | solution.py:563
  66.4 2.0 copy-start.11
  66.4 22.0 %collective-permute-start = (bf16[32,128,128]{2,1,0:T(8,128)(2,1)}, bf16[32,128,128]{2,1,0:T(8,128)(2,1)}, u32[]{:S(2)}, u32[]{:S(2)}) collective-permute-start(bf16[32,128,128]{2,1,0:T(8,128)(2,1)} %slice.4), channel_id=1, source_target_pairs={{0,8},{8,0},{16,24},{24,16},{32,40},{40,32},{48,56},{56,48},{64,72... | collective-permute-start | bytes 3145736 | tf_op jit(solution)/shard_map/ppermute | solution.py:566
  67.0 1.4 copy-start.4
  73.7 1.9 copy-start.1
  75.6 1.9 copy-start.2
  81.3 27.7 %all-to-all-start.1 = ((f32[32,40,128]{2,1,0:T(8,128)}), f32[32,40,128]{2,1,0:T(8,128)S(1)}, u32[]{:S(2)}, u32[]{:S(2)}) async-start(f32[32,40,128]{2,1,0:T(8,128)} %shard_map.94), calls=%async_computation.1 | async-start | bytes 1310720 | tf_op jit(solution)/shard_map/all_to_all | solution.py:547
  108.9 0.8 copy-start.10
  135.8 31.7 %copy-start.5 = (bf16[8,128,1024]{2,1,0:T(8,128)(2,1)S(1)}, bf16[8,128,1024]{2,1,0:T(8,128)(2,1)}, u32[]{:S(2)}) copy-start(bf16[8,128,1024]{2,1,0:T(8,128)(2,1)} %copy-done.4) | copy-start | bytes 6291460
Sparse Core Ops, SparseCore 0:
  9.2 42.4 all-gather.2

commit v2 on v1

--- a/solution.py
+++ b/solution.py
@@ -25,7 +25,6 @@
 CHUNKS = SEQ // SPAN
 KEYS = 512
 PAD = 256
-GRAD_ROWS = 48
 QUARTER = SEQ // SHARE
 
 F32 = jnp.float32
@@ -66,72 +65,76 @@
 
 def pack_teacher_kernel(q_ref, k_ref, v_ref, doc_ref, out_ref):
     docs = jnp.broadcast_to(doc_ref[...].astype(F32), (DOC_ROWS, ROWS)).astype(BF16)
-    for h in range(HEADS):
-        g = h // SHARE
-        out_ref[h, 0:ROWS, :] = q_ref[0, :, h * DIM : (h + 1) * DIM]
-        source = k_ref if h % 2 == 0 else v_ref
-        out_ref[h, ROWS : 2 * ROWS, :] = source[0, :, g * DIM : (g + 1) * DIM]
-        out_ref[h, 2 * ROWS :, :] = docs
+    for k in range(SHARE):
+        out_ref[k, 0:ROWS, :] = q_ref[0, :, k * DIM : (k + 1) * DIM]
+        source = k_ref if k % 2 == 0 else v_ref
+        out_ref[k, ROWS : 2 * ROWS, :] = source[0]
+        out_ref[k, 2 * ROWS :, :] = docs
 
 
 def pack_teacher(q, k, v, docs):
     return pl.pallas_call(
         pack_teacher_kernel,
         out_shape=jax.ShapeDtypeStruct((HEADS, TEACH_ROWS, DIM), BF16),
-        in_specs=[VMEM] * 4,
-        out_specs=VMEM,
-        compiler_params=params(32),
+        grid=(GROUPS,),
+        in_specs=[
+            pl.BlockSpec((1, ROWS, SHARE * DIM), lambda g: (0, 0, g)),
+            pl.BlockSpec((1, ROWS, DIM), lambda g: (0, 0, g)),
+            pl.BlockSpec((1, ROWS, DIM), lambda g: (0, 0, g)),
+            pl.BlockSpec((1, ROWS), lambda g: (0, 0)),
+        ],
+        out_specs=pl.BlockSpec((SHARE, TEACH_ROWS, DIM), lambda g: (g, 0, 0)),
+        compiler_params=params(60),
         cost_estimate=pl.CostEstimate(flops=0, bytes_accessed=4 << 20, transcendentals=0),
     )(q, k, v, docs)
 
 
 def pack_hidden_kernel(hid_ref, out_ref):
     for g in range(GROUPS):
-        for d in range(PARTS):
-            at = d * 1024 + g * 128
-            out_ref[g, :, d * 128 : (d + 1) * 128] = hid_ref[0, :, at : at + 128]
+        for c in range(2):
+            for i in range(PARTS // 2):
+                at = (4 * c + i) * 1024 + g * 128
+                out_ref[2 * g + c, :, i * 128 : (i + 1) * 128] = hid_ref[0, :, at : at + 128]
 
 
 def pack_hidden(hidden):
     return pl.pallas_call(
         pack_hidden_kernel,
-        out_shape=jax.ShapeDtypeStruct((GROUPS, ROWS, D // GROUPS), BF16),
+        out_shape=jax.ShapeDtypeStruct((2 * GROUPS, ROWS, D // 16), BF16),
         in_specs=[VMEM],
         out_specs=VMEM,
-        compiler_params=params(32),
+        compiler_params=params(60),
         cost_estimate=pl.CostEstimate(flops=0, bytes_accessed=4 << 20, transcendentals=0),
     )(hidden)
 
 
 def project_kernel(core_ref, hid_ref, own_ref, other_ref, out_ref, acc_ref):
     step = pl.program_id(0)
-    half = own_ref.shape[1]
+    half = own_ref.shape[2]
     mine = pl.multiple_of(core_ref[0] * half, half)
     theirs = pl.multiple_of((1 - core_ref[0]) * half, half)
-    part = mm(hid_ref[0, :, pl.ds(mine, half)], own_ref[0])
-    part = part + mm(hid_ref[0, :, pl.ds(theirs, half)], other_ref[0])
 
     @pl.when(step == 0)
     def _():
         acc_ref[...] = jnp.zeros_like(acc_ref)
 
-    acc_ref[:, : part.shape[1]] += part
+    part = mm_nt(own_ref[0], hid_ref[0, :, pl.ds(mine, half)])
+    acc_ref[...] += part + mm_nt(other_ref[0], hid_ref[0, :, pl.ds(theirs, half)])
 
     @pl.when(step == PARTS - 1)
     def _():
-        turned = acc_ref[...].T
         for h in range(HEADS):
             g = h // SHARE
-            out_ref[h, 0:STATE, :] = turned[g * STATE : (g + 1) * STATE]
-            out_ref[h, STATE : 2 * STATE, :] = turned[128 + g * STATE : 128 + (g + 1) * STATE]
+            out_ref[h, 0:STATE, :] = acc_ref[g * STATE : (g + 1) * STATE]
+            out_ref[h, STATE : 2 * STATE, :] = acc_ref[128 + g * STATE : 128 + (g + 1) * STATE]
             out_ref[h, 2 * STATE :, :] = jnp.broadcast_to(
-                turned[256 + h : 257 + h], (COLS - 2 * STATE, ROWS)
+                acc_ref[256 + h : 257 + h], (COLS - 2 * STATE, ROWS)
             )
 
 
 def project(core, hidden, own, other):
-    width = own.shape[2]
-    half = own.shape[1]
+    width = own.shape[1]
+    half = own.shape[2]
     return pl.pallas_call(
         project_kernel,
         out_shape=jax.ShapeDtypeStruct((HEADS, COLS, ROWS), F32),
@@ -140,13 +143,13 @@
             grid=(PARTS,),
             in_specs=[
                 pl.BlockSpec((1, ROWS, 2 * half), lambda i, c: (0, 0, i)),
-                pl.BlockSpec((1, half, width), lambda i, c: (i, 0, 0)),
-                pl.BlockSpec((1, half, width), lambda i, c: (i, 0, 0)),
+                pl.BlockSpec((1, width, half), lambda i, c: (i, 0, 0)),
+                pl.BlockSpec((1, width, half), lambda i, c: (i, 0, 0)),
             ],
             out_specs=pl.BlockSpec((HEADS, COLS, ROWS), lambda i, c: (0, 0, 0)),
-            scratch_shapes=[pltpu.VMEM((ROWS, 384), F32)],
+            scratch_shapes=[pltpu.VMEM((width, ROWS), F32)],
         ),
-        compiler_params=params(32),
+        compiler_params=params(60),
         cost_estimate=pl.CostEstimate(
             flops=2 * ROWS * D * 288, bytes_accessed=8 << 20, transcendentals=0
         ),
@@ -476,7 +479,7 @@
     gates = gates + in_ref[2, : 2 * STATE]
     gates = gates + in_ref[3, : 2 * STATE]
     steps = [in_ref[k, 2 * STATE : 2 * STATE + 1] for k in range(SHARE)]
-    rest = jnp.zeros((GRAD_ROWS - 2 * STATE - SHARE, QUARTER), F32)
+    rest = jnp.zeros((COLS - 2 * STATE - SHARE, QUARTER), F32)
     rounded = jnp.concatenate([gates] + steps + [rest], 0).astype(BF16)
     for g in range(GROUPS):
         out_ref[g] = rounded
@@ -485,62 +488,70 @@
 def combine(parts):
     return pl.pallas_call(
         combine_kernel,
-        out_shape=jax.ShapeDtypeStruct((GROUPS, GRAD_ROWS, QUARTER), BF16),
+        out_shape=jax.ShapeDtypeStruct((GROUPS, COLS, QUARTER), BF16),
         in_specs=[VMEM],
         out_specs=VMEM,
         compiler_params=params(32),
     )(parts)
 
 
-def product_kernel(grad_ref, hid_ref, out_ref):
-    for half in range(2):
-        left = grad_ref[half * 4 : half * 4 + 4].reshape(4 * GRAD_ROWS, QUARTER)
-        left = left.astype(F32)
-        keep = jnp.concatenate(
-            [left[i * GRAD_ROWS : i * GRAD_ROWS + COLS] for i in range(4)], 0
-        ).astype(BF16)
-        for d in range(PARTS):
-            hid = hid_ref[:, :, d * 128 : (d + 1) * 128].reshape(QUARTER, 128)
-            part = mm(keep, hid)
-            out_ref[2 * half, d] = part[: 2 * COLS]
-            out_ref[2 * half + 1, d] = part[2 * COLS :]
-
-
-def product(grads, hidden):
+def product_kernel(place_ref, own_ref, other_ref, hid_ref, keep_ref, send_ref, left):
+    core = place_ref[0]
+    pair = place_ref[1]
+    for k, ref in enumerate((own_ref, other_ref)):
+        for half in range(2):
+            rows = [ref[4 * half + i].astype(F32) for i in range(4)]
+            left[k, half] = jnp.concatenate(rows, 0).astype(BF16)
+    own_hid = hid_ref[:, core].reshape(QUARTER, 512)
+    other_hid = hid_ref[:, 1 - core].reshape(QUARTER, 512)
+    for ref, half in ((send_ref, 1 - pair), (keep_ref, pair)):
+        part = mm(left[0, half], own_hid) + mm(left[1, half], other_hid)
+        for i in range(4):
+            for r in range(2):
+                ref[r, i] = part[r * 80 : (r + 1) * 80, i * 128 : (i + 1) * 128]
+
+
+def product(place, own, other, hidden):
+    shape = jax.ShapeDtypeStruct((2, PARTS // 2, 2 * COLS, 128), F32)
     return pl.pallas_call(
         product_kernel,
-        out_shape=jax.ShapeDtypeStruct((SHARE, PARTS, 2 * COLS, 128), F32),
-        in_specs=[VMEM, VMEM],
-        out_specs=VMEM,
+        out_shape=(shape, shape),
+        in_specs=[SMEM, VMEM, VMEM, VMEM],
+        out_specs=(VMEM, VMEM),
+        scratch_shapes=[pltpu.VMEM((2, 2, 4 * COLS, QUARTER), BF16)],
         compiler_params=params(32),
         cost_estimate=pl.CostEstimate(
             flops=2 * 320 * 1024 * 1024, bytes_accessed=4 << 20, transcendentals=0
         ),
-    )(grads, hidden)
-
-
-def place_kernel(in_ref, out_ref):
+    )(place, own, other, hidden.reshape(GROUPS, 2, ROWS, 512))
+
+
+def arrange_kernel(core_ref, own_ref, other_ref, out_ref):
+    first = core_ref[0] == 0
     for g in range(GROUPS):
-        gates_b, gates_c, steps = [], [], []
+        lanes = slice(g * 128, (g + 1) * 128)
         for k in range(GROUPS):
-            block = in_ref[SHARE * g + k // 2]
-            at = (k % 2) * COLS
-            gates_b.append(block[at : at + STATE])
-            gates_c.append(block[at + STATE : at + 2 * STATE])
-            steps.append(block[at + 2 * STATE : at + 2 * STATE + SHARE])
-        fill = jnp.zeros((96, 128), F32)
-        rows = jnp.concatenate(gates_b + gates_c + steps + [fill], 0)
-        out_ref[g * 128 : (g + 1) * 128, :] = rows.T[:, :288]
-
-
-def place(blocks):
-    return pl.pallas_call(
-        place_kernel,
-        out_shape=jax.ShapeDtypeStruct((1024, 288), F32),
-        in_specs=[VMEM],
+            at = 2 * g + k // 4
+            mine, theirs = own_ref[at], other_ref[at]
+            rows = slice((k % 2) * COLS, (k % 2 + 1) * COLS)
+            if (k // 2) % 2 == 0:
+                block = jnp.where(first, mine[rows], theirs[rows])
+            else:
+                block = jnp.where(first, theirs[rows], mine[rows])
+            out_ref[k * STATE : (k + 1) * STATE, lanes] = block[:STATE]
+            out_ref[128 + k * STATE : 128 + (k + 1) * STATE, lanes] = block[STATE : 2 * STATE]
+            steps = block[2 * STATE : 2 * STATE + SHARE]
+            out_ref[256 + k * SHARE : 256 + (k + 1) * SHARE, lanes] = steps
+
+
+def arrange(core, own, other):
+    return pl.pallas_call(
+        arrange_kernel,
+        out_shape=jax.ShapeDtypeStruct((288, 1024), F32),
+        in_specs=[SMEM, VMEM, VMEM],
         out_specs=VMEM,
         compiler_params=params(32),
-    )(blocks)
+    )(core, own, other)
 
 
 def swap_all(x, axis, groups=None):
@@ -553,13 +564,20 @@
     seq_len = hidden.shape[1] * seq_devices
     weight = 1.0 / math.sqrt(HEADS * DIM * data_devices * seq_len)
     head = lax.axis_index("seq").astype(jnp.int32)
-    core = head % 2
+    core = lax.rem(head, 2)
+    pair = lax.rem(lax.div(head, 2), 2)
+    twos = [[2 * i, 2 * i + 1] for i in range(seq_devices // 2)]
     fours = [[SHARE * g + j for j in range(SHARE)] for g in range(GROUPS)]
     eights = [[SHARE * g + j for g in range(GROUPS)] for j in range(SHARE)]
+    halves = [[SHARE * g + 2 * y + c for g in range(GROUPS) for c in range(2)] for y in range(2)]
+    same_core = [[SHARE * g + 2 * y + c for g in range(GROUPS) for y in range(2)] for c in range(2)]
     partner = [(i, i ^ 1) for i in range(seq_devices)]
-
-    half = w_proj.shape[0] // 2
-    own_w = lax.all_gather(lax.dynamic_slice_in_dim(w_proj, core * half, half, 0), "dp", axis=0)
+    across = [(i, i ^ 2) for i in range(seq_devices)]
+
+    turned_w = w_proj.T
+    half = turned_w.shape[1] // 2
+    own_w = lax.dynamic_slice_in_dim(turned_w, core * half, half, 1)
+    own_w = lax.all_gather(own_w, "dp", axis=0)
     other_w = lax.ppermute(own_w, "seq", partner)
 
     own = swap_all(pack_teacher(queries, keys, values, docs), "seq")
@@ -568,17 +586,21 @@
     teach, v, vt, counts = attend(core[None], own, other)
     hidden_packed = pack_hidden(hidden)
     hidden_packed, proj = lax.optimization_barrier((hidden_packed, proj))
-    hidden_part = swap_all(hidden_packed, "seq", eights)
+    hidden_part = swap_all(hidden_packed, "seq", halves)
     grads = student(
         head[None], counts, dt_bias, decay_rate, conv_weight.T, proj, teach, v, vt, weight
     )
-    quarter = combine(swap_all(grads, "seq", fours))
-    spread = swap_all(quarter, "seq", eights)
-    partial = product(spread, hidden_part)
-    partial = jnp.sum(swap_all(partial, "seq", fours), axis=0)
-    total = jnp.sum(swap_all(partial, "dp"), axis=0)
-    blocks = swap_all(jnp.broadcast_to(total[None], (seq_devices, 2 * COLS, 128)), "seq")
-    return place(blocks)
+    grads, hidden_part = lax.optimization_barrier((grads, hidden_part))
+    own_grads = swap_all(combine(swap_all(grads, "seq", fours)), "seq", eights)
+    other_grads = lax.ppermute(own_grads, "seq", partner)
+    keep, send = product(jnp.stack([core, pair]), own_grads, other_grads, hidden_part)
+    summed = keep + lax.ppermute(send, "seq", across)
+    rows = swap_all(summed, "seq", twos).reshape(PARTS, 2 * COLS, 128)
+    total = jnp.sum(swap_all(rows, "dp"), axis=0)
+    spread = jnp.broadcast_to(total[None], (seq_devices // 2, 2 * COLS, 128))
+    own_blocks = swap_all(spread, "seq", same_core)
+    other_blocks = lax.ppermute(own_blocks, "seq", partner)
+    return arrange(core[None], own_blocks, other_blocks).T
 
 
 def solution(mesh):

time: 274 us -> 275 us (level)
  waiting for transfers between devices: 29.1 us -> 65.4 us
  blocking collectives: 127 us -> 102 us
  local copies, waits for them, and re-layouts: 29.7 us -> 6.55 us
  Pallas kernels: 54.7 us -> 69 us
    all_to_all x6, blocking collectives: 127 us -> 102 us  [swap_all(): return lax.all_to_all(x, axis, 0, 0, tiled=True, axis_index_groups=groups)]
    all_gather x1, waiting for transfers between devices: 29.1 us -> 43.3 us  [local(): own_w = lax.all_gather(own_w, 'dp', axis=0)]
    ppermute x0 -> x3, waiting for transfers between devices: none -> 12.4 us  [the longest x1 8.91 us: local(): summed = keep + lax.ppermute(send, 'seq', across)]
    all_to_all x2, waiting for transfers between devices: 0.01 us -> 9.68 us  [swap_all(): return lax.all_to_all(x, axis, 0, 0, tiled=True, axis_index_groups=groups)]
    all_gather x2 -> x0, local copies, waits for them, and re-layouts: 8.98 us -> none  [local(): lax.all_gather(lax.dynamic_slice_in_dim(w_proj, core * half, half, 0), 'd...]
    all_to_all x2, starting transfers between devices: 15.8 us -> 7.3 us  [swap_all(): return lax.all_to_all(x, axis, 0, 0, tiled=True, axis_index_groups=groups)]
    unnamed x25 -> x11, local copies, waits for them, and re-layouts: 11.6 us -> 4.68 us
    ppermute x0 -> x3, starting transfers between devices: none -> 5.78 us  [the longest x1 2.87 us: local(): other_blocks = lax.ppermute(own_blocks, 'seq', partner)]
  transfers between devices with their start and end apart: 5 -> 8, of which waited for: 1 -> 5; matrix products, arithmetic and copies ran while one was open for 6% -> 1% of each run, Pallas kernels for 10% -> 24%
where the time goes in v2:
time: 275 us; the launch traced here: 274 us
  blocking collectives  102 us (37%)
  Pallas kernels  69 us (25%)
  waiting for transfers between devices  65.4 us (24%)
  starting transfers between devices  17.1 us (6%)
  between operations  13.5 us (5%)
  local copies, waits for them, and re-layouts  6.55 us (2%)
    all_to_all x6, blocking collectives, swap_all(): return lax.all_to_all(x, axis, 0, 0, tiled=True, axis_index_groups=groups)  102 us
    all_gather x1, waiting for transfers between devices, local(): own_w = lax.all_gather(own_w, 'dp', axis=0)  43.3 us
    pallas_call x1, Pallas kernels, student(): pl.pallas_call(lambda *refs: student_kernel(*refs, weight=weight), out_sh...  26.1 us
    pallas_call x1, Pallas kernels, attend(): pl.pallas_call(attend_kernel, out_shape=(jax.ShapeDtypeStruct((DIM, SEQ),...  23.4 us
    all_to_all x2, waiting for transfers between devices, swap_all(): return lax.all_to_all(x, axis, 0, 0, tiled=True, axis_index_groups=groups)  9.68 us
    ppermute x1, waiting for transfers between devices, local(): summed = keep + lax.ppermute(send, 'seq', across)  8.91 us
    pallas_call x1, Pallas kernels, project(): pl.pallas_call(project_kernel, out_shape=jax.ShapeDtypeStruct((HEADS, COL...  7.31 us
    all_to_all x2, starting transfers between devices, swap_all(): return lax.all_to_all(x, axis, 0, 0, tiled=True, axis_index_groups=groups)  7.3 us
  transfers between devices with their start and end apart: 8, of which 5 were waited for; matrix products, arithmetic and copies ran while one was open for 1% of the time, Pallas kernels for 24%

profile of v2, /device:TPU:1, one launch (start us, length us, event | category | flops | bytes accessed | tf_op | source)
XLA Modules:
  0.0 273.9 jit_solution(660692522629948843)
XLA Ops:
  6.5 0.0 copy-start
  6.5 0.0 all-gather.3.cloned.1.call-start
  6.5 1.1 copy-done
  7.6 0.7 dynamic-slice_bitcast_fusion
  8.3 0.0 all-gather.3.cloned.1.call-update
  8.4 43.3 %all-gather.3.cloned.1.call-done = bf16[2304,512]{1,0:T(8,128)(2,1)} async-done(((bf16[288,512]{1,0:T(8,128)(2,1)}), bf16[2304,512]{1,0:T(8,128)(2,1)}) %all-gather.3.cloned.1.call-update) | async-done | bytes 2359312 | tf_op jit(solution)/shard_map/all_gather | solution.py:580
  51.6 3.6 %collective-permute-start.1 = (bf16[8,288,512]{2,1,0:T(8,128)(2,1)}, bf16[8,288,512]{2,1,0:T(8,128)(2,1)S(1)}, u32[]{:S(2)}, u32[]{:S(2)}) collective-permute-start(bf16[8,288,512]{2,1,0:T(8,128)(2,1)} %bitcast.11), channel_id=1, source_target_pairs={{0,8},{8,0},{16,24},{24,16},{32,40},{40,32},{48,56},{56,48},{64,72... | collective-permute-start | bytes 7077896 | tf_op jit(solution)/shard_map/ppermute | solution.py:581
  55.2 5.7 %shard_map.91 = bf16[32,272,128]{2,1,0:T(8,128)(2,1)} custom-call(bf16[1,128,4096]{2,1,0:T(8,128)(2,1)} %q_ref.1, bf16[1,128,1024]{2,1,0:T(8,128)(2,1)} %k_ref.1, bf16[1,128,1024]{2,1,0:T(8,128)(2,1)} %v_ref.1, s32[1,128]{1,0:T(1,128)} %doc_ref.1), custom_call_target="tpu_custom_call" | custom-call | bytes 4194304 | tf_op jit(solution)/shard_map/pallas_call | solution.py:76
  60.9 37.1 %all_to_all.40.own_ref = bf16[32,272,128]{2,1,0:T(8,128)(2,1)S(1)} all-to-all(bf16[32,272,128]{2,1,0:T(8,128)(2,1)} %shard_map.91), channel_id=1, replica_groups=mesh['seq'=32,'dp'=8] {'seq'}, dimensions={0} | all-to-all | bytes 4456448 | tf_op jit(solution)/shard_map/all_to_all | solution.py:558
  98.0 0.0 copy-start.1
  98.0 1.4 copy-done.1
  99.4 1.1 slice.4
  100.5 0.4 collective-permute-start
  100.9 0.0 collective-permute-done.1.other_ref
  100.9 0.0 copy-start.2
  100.9 1.4 copy-done.2
  102.4 7.3 %shard_map.94 = f32[32,40,128]{2,1,0:T(8,128)} custom-call(s32[1]{0:T(128)} %bitcast.core_ref, bf16[1,128,8192]{2,1,0:T(8,128)(2,1)} %hid_ref.3, bf16[8,288,512]{2,1,0:T(8,128)(2,1)} %bitcast.12, bf16[8,288,512]{2,1,0:T(8,128)(2,1)} %copy-done.2), custom_call_target="tpu_custom_call" | custom-call | flops 603979776 | bytes 8388608 | tf_op jit(solution)/shard_map/pallas_call | solution.py:138
  109.7 3.7 %all-to-all-start.1 = ((f32[32,40,128]{2,1,0:T(8,128)}), f32[32,40,128]{2,1,0:T(8,128)S(1)}, u32[]{:S(2)}, u32[]{:S(2)}) async-start(f32[32,40,128]{2,1,0:T(8,128)} %shard_map.94), calls=%async_computation.1 | async-start | bytes 1310720 | tf_op jit(solution)/shard_map/all_to_all | solution.py:558
  113.4 3.4 %shard_map.93 = bf16[16,128,512]{2,1,0:T(8,128)(2,1)} custom-call(bf16[1,128,8192]{2,1,0:T(8,128)(2,1)} %hid_ref.3), custom_call_target="tpu_custom_call" | custom-call | bytes 4194304 | tf_op jit(solution)/shard_map/pallas_call | solution.py:101
  116.7 0.0 copy-start.4
  116.7 9.7 %all-to-all-done.1.refs_5_ = f32[32,40,128]{2,1,0:T(8,128)S(1)} async-done(((f32[32,40,128]{2,1,0:T(8,128)}), f32[32,40,128]{2,1,0:T(8,128)S(1)}, u32[]{:S(2)}, u32[]{:S(2)}) %all-to-all-start.1) | async-done | bytes 655392 | tf_op jit(solution)/shard_map/all_to_all | solution.py:558
  126.4 0.0 copy-start.3
  126.4 3.6 %all-to-all-start.2 = ((bf16[16,128,512]{2,1,0:T(8,128)(2,1)}), bf16[16,128,512]{2,1,0:T(8,128)(2,1)S(1)}, u32[]{:S(2)}, u32[]{:S(2)}) async-start(bf16[16,128,512]{2,1,0:T(8,128)(2,1)} %shard_map.93), calls=%async_computation.2 | async-start | bytes 4194304 | tf_op jit(solution)/shard_map/all_to_all | solution.py:558
  130.0 0.0 copy-done.4
  130.0 0.8 copy.10
  130.8 0.0 collective-permute-done.other_ref
  130.8 23.4 %shard_map.92 = (bf16[128,4096]{1,0:T(8,128)(2,1)}, bf16[4096,128]{1,0:T(8,128)(2,1)}, bf16[128,4096]{1,0:T(8,128)(2,1)}, s32[4]{0:T(128)}) custom-call(s32[1]{0:T(128)} %bitcast.core_ref, bf16[32,272,128]{2,1,0:T(8,128)(2,1)} %copy-done.1, bf16[32,128,128]{2,1,0:T(8,128)(2,1)} %collective-permute-done.other_ref), custom_call_target="tpu_custom_call" | custom-call | flops 8589934592 | bytes 8388608 | tf_op jit(solution)/shard_map/pallas_call | solution.py:240
  154.2 0.0 copy-done.3
  154.3 26.1 %shard_map.95 = f32[4,40,1024]{2,1,0:T(8,128)} custom-call(s32[1]{0:T(128)} %bitcast.2.refs_0_, s32[4]{0:T(128)} %get-tuple-element.15.refs_1_, f32[32]{0:T(128)} %refs_2_.1, f32[32]{0:T(128)} %refs_3_.1, f32[256,4]{1,0:T(8,128)} %bitcast.14, f32[32,40,128]{2,1,0:T(8,128)} %copy-done.3, bf16[128,4096]{1,0:T(8,128)(2,1)} %get-tuple-element.17.refs_6_, ...), custom_call_target="tpu_custom_call" | custom-call | flops 8589934592 | bytes 8388608 | tf_op jit(solution)/shard_map/pallas_call | solution.py:450
  180.3 0.0 all-to-all-done.2
  180.3 12.6 %all_to_all.41.in_ref = f32[4,40,1024]{2,1,0:T(8,128)S(1)} all-to-all(f32[4,40,1024]{2,1,0:T(8,128)} %shard_map.95), channel_id=1, replica_groups={{0,8,16,24},{32,40,48,56},{64,72,80,88},{96,104,112,120},{128,136,144,1..., dimensions={0} | all-to-all | bytes 1310720 | tf_op jit(solution)/shard_map/all_to_all | solution.py:558
  192.9 0.1 shard_map.96
  192.9 17.6 %all_to_all.42.own_ref = bf16[8,40,1024]{2,1,0:T(8,128)(2,1)S(1)} all-to-all(bf16[8,40,1024]{2,1,0:T(8,128)(2,1)S(1)} %shard_map.96), channel_id=1, replica_groups={{0,32,64,96,128,160,192,224},{8,40,72,104,136,168,200,232},{16,48,80,11..., dimensions={0} | all-to-all | bytes 1310720 | tf_op jit(solution)/shard_map/all_to_all | solution.py:558
  210.5 2.8 %collective-permute-start.2 = (bf16[8,40,1024]{2,1,0:T(8,128)(2,1)S(1)}, bf16[8,40,1024]{2,1,0:T(8,128)(2,1)}, u32[]{:S(2)}, u32[]{:S(2)}) collective-permute-start(bf16[8,40,1024]{2,1,0:T(8,128)(2,1)S(1)} %all_to_all.42.own_ref), channel_id=1, source_target_pairs={{0,8},{8,0},{16,24},{24,16},{32,40},{40,32},{48,56},{56,48},{64,72... | collective-permute-start | bytes 1966088 | tf_op jit(solution)/shard_map/ppermute | solution.py:595
  213.3 0.1 pad_add_fusion.place_ref
  213.4 1.8 collective-permute-done.2.other_ref
  215.2 2.0 shard_map.97
  217.2 0.1 collective-permute-start.3
  217.3 8.9 %collective-permute-done.3 = f32[2,4,80,128]{3,2,1,0:T(8,128)S(1)} collective-permute-done((f32[2,4,80,128]{3,2,1,0:T(8,128)S(1)}, f32[2,4,80,128]{3,2,1,0:T(8,128)S(1)}, u32[]{:S(2)}, u32[]{:S(2)}) %collective-permute-start.3) | collective-permute-done | bytes 327712 | tf_op jit(solution)/shard_map/ppermute | solution.py:597
  226.3 4.8 %all_to_all.43 = f32[2,4,80,128]{3,2,1,0:T(8,128)S(1)} all-to-all(f32[2,4,80,128]{3,2,1,0:T(8,128)S(1)} %add.7), channel_id=1, replica_groups={{0,8},{16,24},{32,40},{48,56},{64,72},{80,88},{96,104},{112,120},{128,1..., dimensions={0} | all-to-all | bytes 655360 | tf_op jit(solution)/shard_map/all_to_all | solution.py:558
  231.1 16.7 %all_to_all.44 = f32[8,80,128]{2,1,0:T(8,128)S(1)} all-to-all(f32[8,80,128]{2,1,0:T(8,128)S(1)} %bitcast.13), channel_id=1, replica_groups=mesh['seq'=32,'dp'=8] {'dp'}, dimensions={0} | all-to-all | bytes 655360 | tf_op jit(solution)/shard_map/all_to_all | solution.py:558
  247.9 13.4 %all_to_all.45.own_ref = f32[16,80,128]{2,1,0:T(8,128)S(1)} all-to-all(f32[16,80,128]{2,1,0:T(8,128)S(1)} %broadcast_in_dim.16), channel_id=1, replica_groups={{0,16,32,48,64,80,96,112,128,144,160,176,192,208,224,240},{8,24,40,56,7..., dimensions={0} | all-to-all | bytes 1310720 | tf_op jit(solution)/shard_map/all_to_all | solution.py:558
  261.3 2.9 %collective-permute-start.4 = (f32[16,80,128]{2,1,0:T(8,128)S(1)}, f32[16,80,128]{2,1,0:T(8,128)S(1)}, u32[]{:S(2)}, u32[]{:S(2)}) collective-permute-start(f32[16,80,128]{2,1,0:T(8,128)S(1)} %all_to_all.45.own_ref), channel_id=1, source_target_pairs={{0,8},{8,0},{16,24},{24,16},{32,40},{40,32},{48,56},{56,48},{64,72... | collective-permute-start | bytes 1966088 | tf_op jit(solution)/shard_map/ppermute | solution.py:602
  264.2 1.7 collective-permute-done.4.other_ref
  265.9 1.2 shard_map.98
  (3 shorter events, 0.1 us)
Async XLA Ops:
  6.5 1.1 copy-start
  6.5 45.1 %all-gather.3.cloned.1.call-start = ((), (), s32[]{:S(2)}) async-start(), calls=%async_computation.8 | async-start | bytes 2654208 | tf_op jit(solution)/shard_map/all_gather | solution.py:580
  51.6 49.3 %collective-permute-start.1 = (bf16[8,288,512]{2,1,0:T(8,128)(2,1)}, bf16[8,288,512]{2,1,0:T(8,128)(2,1)S(1)}, u32[]{:S(2)}, u32[]{:S(2)}) collective-permute-start(bf16[8,288,512]{2,1,0:T(8,128)(2,1)} %bitcast.11), channel_id=1, source_target_pairs={{0,8},{8,0},{16,24},{24,16},{32,40},{40,32},{48,56},{56,48},{64,72... | collective-permute-start | bytes 7077896 | tf_op jit(solution)/shard_map/ppermute | solution.py:581
  98.0 1.4 copy-start.1
  100.5 30.3 %collective-permute-start = (bf16[32,128,128]{2,1,0:T(8,128)(2,1)}, bf16[32,128,128]{2,1,0:T(8,128)(2,1)}, u32[]{:S(2)}, u32[]{:S(2)}) collective-permute-start(bf16[32,128,128]{2,1,0:T(8,128)(2,1)} %slice.4), channel_id=1, source_target_pairs={{0,8},{8,0},{16,24},{24,16},{32,40},{40,32},{48,56},{56,48},{64,72... | collective-permute-start | bytes 3145736 | tf_op jit(solution)/shard_map/ppermute | solution.py:584
  100.9 1.4 copy-start.2
  109.7 16.7 %all-to-all-start.1 = ((f32[32,40,128]{2,1,0:T(8,128)}), f32[32,40,128]{2,1,0:T(8,128)S(1)}, u32[]{:S(2)}, u32[]{:S(2)}) async-start(f32[32,40,128]{2,1,0:T(8,128)} %shard_map.94), calls=%async_computation.1 | async-start | bytes 1310720 | tf_op jit(solution)/shard_map/all_to_all | solution.py:558
  116.7 13.3 %copy-start.4 = (f32[4,256]{1,0:T(4,128)S(1)}, f32[4,256]{1,0:T(4,128)}, u32[]{:S(2)}) copy-start(f32[4,256]{1,0:T(4,128)} %param.15) | copy-start | bytes 12292
  126.4 27.9 %copy-start.3 = (f32[32,40,128]{2,1,0:T(8,128)}, f32[32,40,128]{2,1,0:T(8,128)S(1)}, u32[]{:S(2)}) copy-start(f32[32,40,128]{2,1,0:T(8,128)S(1)} %all-to-all-done.1.refs_5_) | copy-start | bytes 1966084
  126.4 53.9 %all-to-all-start.2 = ((bf16[16,128,512]{2,1,0:T(8,128)(2,1)}), bf16[16,128,512]{2,1,0:T(8,128)(2,1)S(1)}, u32[]{:S(2)}, u32[]{:S(2)}) async-start(bf16[16,128,512]{2,1,0:T(8,128)(2,1)} %shard_map.93), calls=%async_computation.2 | async-start | bytes 4194304 | tf_op jit(solution)/shard_map/all_to_all | solution.py:558
  210.5 4.7 %collective-permute-start.2 = (bf16[8,40,1024]{2,1,0:T(8,128)(2,1)S(1)}, bf16[8,40,1024]{2,1,0:T(8,128)(2,1)}, u32[]{:S(2)}, u32[]{:S(2)}) collective-permute-start(bf16[8,40,1024]{2,1,0:T(8,128)(2,1)S(1)} %all_to_all.42.own_ref), channel_id=1, source_target_pairs={{0,8},{8,0},{16,24},{24,16},{32,40},{40,32},{48,56},{56,48},{64,72... | collective-permute-start | bytes 1966088 | tf_op jit(solution)/shard_map/ppermute | solution.py:595
  217.2 9.0 %collective-permute-start.3 = (f32[2,4,80,128]{3,2,1,0:T(8,128)S(1)}, f32[2,4,80,128]{3,2,1,0:T(8,128)S(1)}, u32[]{:S(2)}, u32[]{:S(2)}) collective-permute-start(f32[2,4,80,128]{3,2,1,0:T(8,128)S(1)} %get-tuple-element.24), channel_id=1, source_target_pairs={{0,16},{8,24},{16,0},{24,8},{32,48},{40,56},{48,32},{56,40},{64,80... | collective-permute-start | bytes 983048 | tf_op jit(solution)/shard_map/ppermute | solution.py:597
  261.3 4.6 %collective-permute-start.4 = (f32[16,80,128]{2,1,0:T(8,128)S(1)}, f32[16,80,128]{2,1,0:T(8,128)S(1)}, u32[]{:S(2)}, u32[]{:S(2)}) collective-permute-start(f32[16,80,128]{2,1,0:T(8,128)S(1)} %all_to_all.45.own_ref), channel_id=1, source_target_pairs={{0,8},{8,0},{16,24},{24,16},{32,40},{40,32},{48,56},{56,48},{64,72... | collective-permute-start | bytes 1966088 | tf_op jit(solution)/shard_map/ppermute | solution.py:602
Sparse Core Ops, SparseCore 0:
  9.1 42.4 all-gather.2

commit v3 on v2

--- a/solution.py
+++ b/solution.py
@@ -18,14 +18,19 @@
 ROWS = 128
 BLOCKS = SEQ // ROWS
 PARTS = 8
+WIDTH = 288
 DOC_ROWS = 16
 TEACH_ROWS = 2 * ROWS + DOC_ROWS
 COLS = 40
 SPAN = 256
 CHUNKS = SEQ // SPAN
-KEYS = 512
-PAD = 256
-QUARTER = SEQ // SHARE
+KEYS = 1024
+HALF = KEYS // 2
+QUERIES = 512
+PAD = max(0, KEYS - QUERIES)
+UNROLL = 16
+PACK_STEPS = 2
+PROJECT_STEPS = 2
 
 F32 = jnp.float32
 BF16 = jnp.bfloat16
@@ -65,63 +70,70 @@
 
 def pack_teacher_kernel(q_ref, k_ref, v_ref, doc_ref, out_ref):
     docs = jnp.broadcast_to(doc_ref[...].astype(F32), (DOC_ROWS, ROWS)).astype(BF16)
-    for k in range(SHARE):
+    for k in range(q_ref.shape[2] // DIM):
+        g = k // SHARE
         out_ref[k, 0:ROWS, :] = q_ref[0, :, k * DIM : (k + 1) * DIM]
         source = k_ref if k % 2 == 0 else v_ref
-        out_ref[k, ROWS : 2 * ROWS, :] = source[0]
+        out_ref[k, ROWS : 2 * ROWS, :] = source[0, :, g * DIM : (g + 1) * DIM]
         out_ref[k, 2 * ROWS :, :] = docs
 
 
 def pack_teacher(q, k, v, docs):
+    many = GROUPS // PACK_STEPS
     return pl.pallas_call(
         pack_teacher_kernel,
         out_shape=jax.ShapeDtypeStruct((HEADS, TEACH_ROWS, DIM), BF16),
-        grid=(GROUPS,),
+        grid=(PACK_STEPS,),
         in_specs=[
-            pl.BlockSpec((1, ROWS, SHARE * DIM), lambda g: (0, 0, g)),
-            pl.BlockSpec((1, ROWS, DIM), lambda g: (0, 0, g)),
-            pl.BlockSpec((1, ROWS, DIM), lambda g: (0, 0, g)),
+            pl.BlockSpec((1, ROWS, many * SHARE * DIM), lambda g: (0, 0, g)),
+            pl.BlockSpec((1, ROWS, many * DIM), lambda g: (0, 0, g)),
+            pl.BlockSpec((1, ROWS, many * DIM), lambda g: (0, 0, g)),
             pl.BlockSpec((1, ROWS), lambda g: (0, 0)),
         ],
-        out_specs=pl.BlockSpec((SHARE, TEACH_ROWS, DIM), lambda g: (g, 0, 0)),
+        out_specs=pl.BlockSpec((many * SHARE, TEACH_ROWS, DIM), lambda g: (g, 0, 0)),
         compiler_params=params(60),
         cost_estimate=pl.CostEstimate(flops=0, bytes_accessed=4 << 20, transcendentals=0),
     )(q, k, v, docs)
 
 
-def pack_hidden_kernel(hid_ref, out_ref):
-    for g in range(GROUPS):
-        for c in range(2):
-            for i in range(PARTS // 2):
-                at = (4 * c + i) * 1024 + g * 128
-                out_ref[2 * g + c, :, i * 128 : (i + 1) * 128] = hid_ref[0, :, at : at + 128]
-
-
-def pack_hidden(hidden):
+def pack_hidden_kernel(part_ref, hid_ref, *out_refs):
+    width = out_refs[0].shape[1]
+    for k, ref in enumerate(out_refs):
+        block = lax.rem(part_ref[0] + k, PARTS)
+        ref[...] = hid_ref[0, :, pl.ds(pl.multiple_of(block * width, width), width)]
+
+
+def pack_hidden(part, hidden):
+    block = jax.ShapeDtypeStruct((ROWS, D // PARTS), BF16)
     return pl.pallas_call(
         pack_hidden_kernel,
-        out_shape=jax.ShapeDtypeStruct((2 * GROUPS, ROWS, D // 16), BF16),
-        in_specs=[VMEM],
-        out_specs=VMEM,
+        out_shape=(block,) * PARTS,
+        in_specs=[SMEM, VMEM],
+        out_specs=(VMEM,) * PARTS,
         compiler_params=params(60),
         cost_estimate=pl.CostEstimate(flops=0, bytes_accessed=4 << 20, transcendentals=0),
-    )(hidden)
+    )(part, hidden)
 
 
 def project_kernel(core_ref, hid_ref, own_ref, other_ref, out_ref, acc_ref):
     step = pl.program_id(0)
-    half = own_ref.shape[2]
-    mine = pl.multiple_of(core_ref[0] * half, half)
-    theirs = pl.multiple_of((1 - core_ref[0]) * half, half)
+    many, _, half = own_ref.shape
+    part = 0.0
+    for i in range(many):
+        mine = pl.multiple_of((2 * i + core_ref[0]) * half, half)
+        theirs = pl.multiple_of((2 * i + 1 - core_ref[0]) * half, half)
+        part = part + mm_nt(own_ref[i], hid_ref[0, :, pl.ds(mine, half)])
+        part = part + mm_nt(other_ref[i], hid_ref[0, :, pl.ds(theirs, half)])
 
     @pl.when(step == 0)
     def _():
-        acc_ref[...] = jnp.zeros_like(acc_ref)
-
-    part = mm_nt(own_ref[0], hid_ref[0, :, pl.ds(mine, half)])
-    acc_ref[...] += part + mm_nt(other_ref[0], hid_ref[0, :, pl.ds(theirs, half)])
-
-    @pl.when(step == PARTS - 1)
+        acc_ref[...] = part
+
+    @pl.when(step > 0)
+    def _():
+        acc_ref[...] += part
+
+    @pl.when(step == PROJECT_STEPS - 1)
     def _():
         for h in range(HEADS):
             g = h // SHARE
@@ -133,18 +145,18 @@
 
 
 def project(core, hidden, own, other):
-    width = own.shape[1]
-    half = own.shape[2]
+    _, width, half = own.shape
+    many = PARTS // PROJECT_STEPS
     return pl.pallas_call(
         project_kernel,
         out_shape=jax.ShapeDtypeStruct((HEADS, COLS, ROWS), F32),
         grid_spec=pltpu.PrefetchScalarGridSpec(
             num_scalar_prefetch=1,
-            grid=(PARTS,),
+            grid=(PROJECT_STEPS,),
             in_specs=[
-                pl.BlockSpec((1, ROWS, 2 * half), lambda i, c: (0, 0, i)),
-                pl.BlockSpec((1, width, half), lambda i, c: (i, 0, 0)),
-                pl.BlockSpec((1, width, half), lambda i, c: (i, 0, 0)),
+                pl.BlockSpec((1, ROWS, many * 2 * half), lambda i, c: (0, 0, i)),
+                pl.BlockSpec((many, width, half), lambda i, c: (i, 0, 0)),
+                pl.BlockSpec((many, width, half), lambda i, c: (i, 0, 0)),
             ],
             out_specs=pl.BlockSpec((HEADS, COLS, ROWS), lambda i, c: (0, 0, 0)),
             scratch_shapes=[pltpu.VMEM((width, ROWS), F32)],
@@ -163,8 +175,9 @@
     for d in range(3):
         n_ref[d] = jnp.sum((docs < d + 0.5).astype(F32)).astype(jnp.int32)
     n_ref[3] = 0
-    keys[0:PAD, :] = jnp.zeros((PAD, DIM), BF16)
-    turned[:, 0:PAD] = jnp.zeros((DIM, PAD), BF16)
+    if PAD:
+        keys[0:PAD, :] = jnp.zeros((PAD, DIM), BF16)
+        turned[:, 0:PAD] = jnp.zeros((DIM, PAD), BF16)
 
     @pl.when(core_ref[0] == 0)
     def _():
@@ -179,61 +192,71 @@
             v_ref[s * ROWS : (s + 1) * ROWS, :] = own_ref[s, ROWS : 2 * ROWS, :]
 
     for s in range(BLOCKS):
-        block = v_ref[s * ROWS : (s + 1) * ROWS, :].astype(F32).T.astype(BF16)
+        block = v_ref[s * ROWS : (s + 1) * ROWS, :].T
         turned[:, PAD + s * ROWS : PAD + (s + 1) * ROWS] = block
         vt_ref[:, s * ROWS : (s + 1) * ROWS] = block
 
     scale = DIM ** (-0.5) * math.log2(math.e)
 
     def rows(i, carry):
-        q0 = i * SPAN
-        query = jnp.concatenate([own_ref[2 * i, 0:ROWS, :], own_ref[2 * i + 1, 0:ROWS, :]], 0)
+        q0 = i * QUERIES
+        many = QUERIES // ROWS
+        query = jnp.concatenate([own_ref[many * i + k, 0:ROWS, :] for k in range(many)], 0)
         first = scalar_start(q0, n_ref)
-        last = scalar_start(q0 + SPAN - 1, n_ref)
-        count = (q0 + SPAN - first + KEYS - 1) // KEYS
-        q_at = q0 + lax.broadcasted_iota(jnp.int32, (1, SPAN), 1)
+        last = scalar_start(q0 + QUERIES - 1, n_ref)
+        need = q0 + QUERIES - first
+        rest = lax.rem(need, KEYS)
+        count = need // KEYS + (rest > HALF).astype(jnp.int32)
+        ends = ((rest > 0) & (rest <= HALF)).astype(jnp.int32)
+        q_at = q0 + lax.broadcasted_iota(jnp.int32, (1, QUERIES), 1)
         start = doc_start(q_at, n_ref)
 
-        def score(j, top):
-            low = q0 + SPAN - (j + 1) * KEYS
-            at = pl.multiple_of(low + PAD, SPAN)
-            s = mm_nt(keys[pl.ds(at, KEYS), :], query)
-            k_at = low + lax.broadcasted_iota(jnp.int32, (KEYS, SPAN), 0)
-            s = jnp.where((k_at <= q_at) & (k_at >= start), s, NEG)
-            scores[pl.ds(pl.multiple_of(j * KEYS, KEYS), KEYS), :] = s
-            return jnp.maximum(top, jnp.max(s.reshape(KEYS // 8, 8, SPAN), axis=0))
-
-        def score_plain(j, top):
-            low = q0 + SPAN - (j + 1) * KEYS
-            at = pl.multiple_of(low + PAD, SPAN)
-            s = mm_nt(keys[pl.ds(at, KEYS), :], query)
-            scores[pl.ds(pl.multiple_of(j * KEYS, KEYS), KEYS), :] = s
-            return jnp.maximum(top, jnp.max(s.reshape(KEYS // 8, 8, SPAN), axis=0))
-
-        top = score(0, jnp.full((8, SPAN), NEG, F32))
-        inner = jnp.clip((q0 + SPAN - last) // KEYS, 1, count)
-        top = lax.fori_loop(1, inner, score_plain, top)
-        top = lax.fori_loop(inner, count, score, top)
+        def tile(at, size):
+            low = q0 + QUERIES - at - size
+            return low, pl.multiple_of(low + PAD, HALF), pl.ds(pl.multiple_of(at, HALF), size)
+
+        def score(at, size, masked, top):
+            low, key_at, rows_at = tile(at, size)
+            s = mm_nt(keys[pl.ds(key_at, size), :], query)
+            if masked:
+                k_at = low + lax.broadcasted_iota(jnp.int32, (size, QUERIES), 0)
+                s = jnp.where((k_at <= q_at) & (k_at >= start), s, NEG)
+            scores[rows_at, :] = s
+            return jnp.maximum(top, jnp.max(s.reshape(size // 8, 8, QUERIES), axis=0))
+
+        def masked(j, top):
+            return score(j * KEYS, KEYS, True, top)
+
+        def plain(j, top):
+            return score(j * KEYS, KEYS, False, top)
+
+        def masked_half(j, top):
+            return score(count * KEYS, HALF, True, top)
+
+        one = jnp.minimum(count, 1)
+        inner = jnp.clip((q0 + QUERIES - last) // KEYS, one, count)
+        top = jnp.full((8, QUERIES), NEG, F32)
+        top = lax.fori_loop(0, one, masked, top)
+        top = lax.fori_loop(one, inner, plain, top)
+        top = lax.fori_loop(inner, count, masked, top)
+        top = lax.fori_loop(0, ends, masked_half, top)
         top = jnp.max(top, axis=0, keepdims=True)
 
-        def mix(j, state):
+        def mix(at, size, state):
             total, out = state
-            low = q0 + SPAN - (j + 1) * KEYS
-            at = pl.multiple_of(low + PAD, SPAN)
-            s = scores[pl.ds(pl.multiple_of(j * KEYS, KEYS), KEYS), :]
-            p = jnp.exp2((s - top) * scale)
-            total = total + jnp.sum(p.reshape(KEYS // 8, 8, SPAN), axis=0)
-            out = out + mm(turned[:, pl.ds(at, KEYS)], p.astype(BF16))
-            return total, out
-
-        total, out = lax.fori_loop(
-            0, count, mix, (jnp.zeros((8, SPAN), F32), jnp.zeros((DIM, SPAN), F32))
-        )
+            _, key_at, rows_at = tile(at, size)
+            p = jnp.exp2((scores[rows_at, :] - top) * scale)
+            total = total + jnp.sum(p.reshape(size // 8, 8, QUERIES), axis=0)
+            return total, out + mm(turned[:, pl.ds(key_at, size)], p.astype(BF16))
+
+        state = (jnp.zeros((8, QUERIES), F32), jnp.zeros((DIM, QUERIES), F32))
+        state = lax.fori_loop(0, count, lambda j, t: mix(j * KEYS, KEYS, t), state)
+        total, out = lax.fori_loop(0, ends, lambda j, t: mix(count * KEYS, HALF, t), state)
         total = jnp.sum(total, axis=0, keepdims=True)
-        teach_ref[:, pl.ds(pl.multiple_of(q0, SPAN), SPAN)] = (out / total).astype(BF16)
+        teach_ref[:, pl.ds(pl.multiple_of(q0, QUERIES), QUERIES)] = (out / total).astype(BF16)
         return carry
 
-    lax.fori_loop(0, CHUNKS, rows, 0)
+    lax.fori_loop(0, SEQ // QUERIES, rows, 0)
 
 
 def attend(core, own, other):
@@ -250,9 +273,9 @@
         scratch_shapes=[
             pltpu.VMEM((PAD + SEQ, DIM), BF16),
             pltpu.VMEM((DIM, PAD + SEQ), BF16),
-            pltpu.VMEM((SEQ + KEYS, SPAN), F32),
+            pltpu.VMEM((SEQ + KEYS, QUERIES), F32),
         ],
-        compiler_params=params(),
+        compiler_params=params(56),
         cost_estimate=pl.CostEstimate(
             flops=8 << 30, bytes_accessed=8 << 20, transcendentals=8 << 20
         ),
@@ -394,7 +417,7 @@
         keep = jnp.where(last < base, 1.0, 0.0) * jnp.exp(ended)
         return keep * state + new[:STATE] + new[STATE:]
 
-    final = lax.fori_loop(0, CHUNKS, forward, jnp.zeros((STATE, DIM), F32))
+    final = lax.fori_loop(0, CHUNKS, forward, jnp.zeros((STATE, DIM), F32), unroll=UNROLL)
     state_s[CHUNKS] = final
 
     def backward(k, carried):
@@ -424,14 +447,13 @@
         for j in range(1, TAPS):
             reach = jnp.where(at >= doc_start(at + j, n_ref), pltpu.roll(rows, SPAN + 128 - j, 1)[:, :SPAN], 0.0)
             back = back + taps[:, j : j + 1] * reach
-        column = pl.multiple_of((c // 2) * ROWS, ROWS)
-        out_ref[2 * (c % 2), 0 : 2 * STATE, pl.ds(column, ROWS)] = back[:, :ROWS]
-        out_ref[2 * (c % 2) + 1, 0 : 2 * STATE, pl.ds(column, ROWS)] = back[:, ROWS:]
+        out_ref[2 * c, 0 : 2 * STATE, :] = back[:, :ROWS]
+        out_ref[2 * c + 1, 0 : 2 * STATE, :] = back[:, ROWS:]
         keep = jnp.where(last < base, 1.0, 0.0) * jnp.exp(ended)
         return keep * dstate + dstate_s[c], dpre[:, :128]
 
     nothing = (jnp.zeros((STATE, DIM), F32), jnp.zeros((2 * STATE, 128), F32))
-    lax.fori_loop(0, CHUNKS, backward, nothing)
+    lax.fori_loop(0, CHUNKS, backward, nothing, unroll=UNROLL)
 
     at_all = lax.broadcasted_iota(jnp.int32, (CHUNKS, SPAN), 0) * SPAN
     at_all = at_all + lax.broadcasted_iota(jnp.int32, (CHUNKS, SPAN), 1)
@@ -441,15 +463,13 @@
     dstep = (direct - rate * dlog) * slope_all
     for s in range(BLOCKS):
         piece = dstep[s // 2 : s // 2 + 1, (s % 2) * ROWS : (s % 2 + 1) * ROWS]
-        out_ref[s % SHARE, 2 * STATE :, (s // SHARE) * ROWS : (s // SHARE + 1) * ROWS] = (
-            jnp.broadcast_to(piece, (COLS - 2 * STATE, ROWS))
-        )
+        out_ref[s, 2 * STATE :, :] = jnp.broadcast_to(piece, (COLS - 2 * STATE, ROWS))
 
 
 def student(head, counts, bias, rate, taps, proj, teach, v, vt, weight):
     return pl.pallas_call(
         lambda *refs: student_kernel(*refs, weight=weight),
-        out_shape=jax.ShapeDtypeStruct((SHARE, COLS, QUARTER), F32),
+        out_shape=jax.ShapeDtypeStruct((BLOCKS, COLS, ROWS), F32),
         in_specs=[SMEM, SMEM, SMEM, SMEM, VMEM, VMEM, VMEM, VMEM, VMEM],
         out_specs=VMEM,
         scratch_shapes=[
@@ -467,95 +487,95 @@
             pltpu.VMEM((CHUNKS + 1, STATE, DIM), F32),
             pltpu.VMEM((CHUNKS, STATE, DIM), F32),
         ],
-        compiler_params=params(),
+        compiler_params=params(56),
         cost_estimate=pl.CostEstimate(
             flops=8 << 30, bytes_accessed=8 << 20, transcendentals=4 << 20
         ),
     )(head, counts, bias, rate, taps, proj, teach, v, vt)
 
 
-def combine_kernel(in_ref, out_ref):
-    gates = in_ref[0, : 2 * STATE] + in_ref[1, : 2 * STATE]
-    gates = gates + in_ref[2, : 2 * STATE]
-    gates = gates + in_ref[3, : 2 * STATE]
-    steps = [in_ref[k, 2 * STATE : 2 * STATE + 1] for k in range(SHARE)]
-    rest = jnp.zeros((COLS - 2 * STATE - SHARE, QUARTER), F32)
-    rounded = jnp.concatenate([gates] + steps + [rest], 0).astype(BF16)
+def combine_kernel(in_ref, out_ref, rows):
     for g in range(GROUPS):
-        out_ref[g] = rounded
+        gates = in_ref[SHARE * g, : 2 * STATE]
+        for k in range(1, SHARE):
+            gates = gates + in_ref[SHARE * g + k, : 2 * STATE]
+        rows[g * STATE : (g + 1) * STATE] = gates[:STATE]
+        rows[128 + g * STATE : 128 + (g + 1) * STATE] = gates[STATE:]
+    for h in range(HEADS):
+        rows[256 + h : 257 + h] = in_ref[h, 2 * STATE : 2 * STATE + 1]
+    rounded = rows[...].astype(BF16)
+    for d in range(PARTS):
+        out_ref[d] = rounded
 
 
 def combine(parts):
     return pl.pallas_call(
         combine_kernel,
-        out_shape=jax.ShapeDtypeStruct((GROUPS, COLS, QUARTER), BF16),
+        out_shape=jax.ShapeDtypeStruct((PARTS, WIDTH, ROWS), BF16),
         in_specs=[VMEM],
         out_specs=VMEM,
-        compiler_params=params(32),
+        scratch_shapes=[pltpu.VMEM((WIDTH, ROWS), F32)],
+        compiler_params=params(16),
     )(parts)
 
 
-def product_kernel(place_ref, own_ref, other_ref, hid_ref, keep_ref, send_ref, left):
-    core = place_ref[0]
-    pair = place_ref[1]
-    for k, ref in enumerate((own_ref, other_ref)):
-        for half in range(2):
-            rows = [ref[4 * half + i].astype(F32) for i in range(4)]
-            left[k, half] = jnp.concatenate(rows, 0).astype(BF16)
-    own_hid = hid_ref[:, core].reshape(QUARTER, 512)
-    other_hid = hid_ref[:, 1 - core].reshape(QUARTER, 512)
-    for ref, half in ((send_ref, 1 - pair), (keep_ref, pair)):
-        part = mm(left[0, half], own_hid) + mm(left[1, half], other_hid)
-        for i in range(4):
-            for r in range(2):
-                ref[r, i] = part[r * 80 : (r + 1) * 80, i * 128 : (i + 1) * 128]
-
-
-def product(place, own, other, hidden):
-    shape = jax.ShapeDtypeStruct((2, PARTS // 2, 2 * COLS, 128), F32)
+def product_kernel(core_ref, part_ref, grad_ref, *refs):
+    blocks, (keep_ref, send_ref) = refs[:PARTS], refs[PARTS:]
+    left = jnp.concatenate(
+        [grad_ref[lax.rem(part_ref[0] + PARTS - k, PARTS)] for k in range(PARTS)], 1
+    )
+    half = blocks[0].shape[1] // 2
+    for ref, core in ((send_ref, 1 - core_ref[0]), (keep_ref, core_ref[0])):
+        lanes = pl.ds(pl.multiple_of(core * half, half), half)
+        part = mm(left, jnp.concatenate([block[:, lanes] for block in blocks], 0))
+        for r in range(4):
+            for q in range(4):
+                ref[4 * r + q] = part[r * 72 : (r + 1) * 72, q * 128 : (q + 1) * 128]
+
+
+def product(core, part, grads, blocks):
+    shape = jax.ShapeDtypeStruct((16, WIDTH // 4, 128), F32)
     return pl.pallas_call(
         product_kernel,
         out_shape=(shape, shape),
-        in_specs=[SMEM, VMEM, VMEM, VMEM],
+        in_specs=[SMEM, SMEM, VMEM] + [VMEM] * PARTS,
         out_specs=(VMEM, VMEM),
-        scratch_shapes=[pltpu.VMEM((2, 2, 4 * COLS, QUARTER), BF16)],
-        compiler_params=params(32),
+        compiler_params=params(24),
         cost_estimate=pl.CostEstimate(
-            flops=2 * 320 * 1024 * 1024, bytes_accessed=4 << 20, transcendentals=0
+            flops=2 * WIDTH * 1024 * 1024, bytes_accessed=4 << 20, transcendentals=0
         ),
-    )(place, own, other, hidden.reshape(GROUPS, 2, ROWS, 512))
+    )(core, part, grads, *blocks)
 
 
 def arrange_kernel(core_ref, own_ref, other_ref, out_ref):
-    first = core_ref[0] == 0
-    for g in range(GROUPS):
-        lanes = slice(g * 128, (g + 1) * 128)
-        for k in range(GROUPS):
-            at = 2 * g + k // 4
-            mine, theirs = own_ref[at], other_ref[at]
-            rows = slice((k % 2) * COLS, (k % 2 + 1) * COLS)
-            if (k // 2) % 2 == 0:
-                block = jnp.where(first, mine[rows], theirs[rows])
-            else:
-                block = jnp.where(first, theirs[rows], mine[rows])
-            out_ref[k * STATE : (k + 1) * STATE, lanes] = block[:STATE]
-            out_ref[128 + k * STATE : 128 + (k + 1) * STATE, lanes] = block[STATE : 2 * STATE]
-            steps = block[2 * STATE : 2 * STATE + SHARE]
-            out_ref[256 + k * SHARE : 256 + (k + 1) * SHARE, lanes] = steps
+    half = out_ref.shape[1] // 2
+    for ref, core in ((own_ref, core_ref[0]), (other_ref, 1 - core_ref[0])):
+        for r in range(4):
+            for q in range(4):
+                lanes = pl.ds(pl.multiple_of(core * half + q * 128, 128), 128)
+                out_ref[r * 72 : (r + 1) * 72, lanes] = ref[4 * r + q]
 
 
 def arrange(core, own, other):
     return pl.pallas_call(
         arrange_kernel,
-        out_shape=jax.ShapeDtypeStruct((288, 1024), F32),
+        out_shape=jax.ShapeDtypeStruct((WIDTH, D // PARTS), F32),
         in_specs=[SMEM, VMEM, VMEM],
         out_specs=VMEM,
-        compiler_params=params(32),
+        compiler_params=params(16),
     )(core, own, other)
 
 
 def swap_all(x, axis, groups=None):
     return lax.all_to_all(x, axis, 0, 0, tiled=True, axis_index_groups=groups)
+
+
+def spread_hidden(blocks, distances):
+    moved = []
+    for k in distances:
+        route = [(i, (i + k) % PARTS) for i in range(PARTS)]
+        moved.append(lax.ppermute(blocks[k], "dp", route))
+    return moved
 
 
 def local(hidden, queries, keys, values, docs, w_proj, conv_weight, dt_bias, decay_rate):
@@ -564,43 +584,37 @@
     seq_len = hidden.shape[1] * seq_devices
     weight = 1.0 / math.sqrt(HEADS * DIM * data_devices * seq_len)
     head = lax.axis_index("seq").astype(jnp.int32)
-    core = lax.rem(head, 2)
-    pair = lax.rem(lax.div(head, 2), 2)
-    twos = [[2 * i, 2 * i + 1] for i in range(seq_devices // 2)]
-    fours = [[SHARE * g + j for j in range(SHARE)] for g in range(GROUPS)]
-    eights = [[SHARE * g + j for g in range(GROUPS)] for j in range(SHARE)]
-    halves = [[SHARE * g + 2 * y + c for g in range(GROUPS) for c in range(2)] for y in range(2)]
-    same_core = [[SHARE * g + 2 * y + c for g in range(GROUPS) for y in range(2)] for c in range(2)]
+    core = lax.rem(head, 2)[None]
+    part = lax.axis_index("dp").astype(jnp.int32)[None]
+    same_core = [[2 * i + c for i in range(seq_devices // 2)] for c in range(2)]
     partner = [(i, i ^ 1) for i in range(seq_devices)]
-    across = [(i, i ^ 2) for i in range(seq_devices)]
 
     turned_w = w_proj.T
     half = turned_w.shape[1] // 2
-    own_w = lax.dynamic_slice_in_dim(turned_w, core * half, half, 1)
+    own_w = lax.dynamic_slice_in_dim(turned_w, core[0] * half, half, 1)
     own_w = lax.all_gather(own_w, "dp", axis=0)
+    own = swap_all(pack_teacher(queries, keys, values, docs), "seq")
+    own, own_w, taps, blocks = lax.optimization_barrier(
+        (own, own_w, conv_weight.T, pack_hidden(part, hidden))
+    )
+    order = (4, 5, 3, 6, 2, 1, 7)
+    moved = {0: blocks[0]} | dict(zip(order, spread_hidden(blocks, order)))
     other_w = lax.ppermute(own_w, "seq", partner)
-
-    own = swap_all(pack_teacher(queries, keys, values, docs), "seq")
     other = lax.ppermute(own[:, ROWS : 2 * ROWS, :], "seq", partner)
-    proj = swap_all(project(core[None], hidden, own_w, other_w), "seq")
-    teach, v, vt, counts = attend(core[None], own, other)
-    hidden_packed = pack_hidden(hidden)
-    hidden_packed, proj = lax.optimization_barrier((hidden_packed, proj))
-    hidden_part = swap_all(hidden_packed, "seq", halves)
+    proj = swap_all(project(core, hidden, own_w, other_w), "seq")
+    teach, v, vt, counts = attend(core, own, other)
     grads = student(
-        head[None], counts, dt_bias, decay_rate, conv_weight.T, proj, teach, v, vt, weight
+        head[None], counts, dt_bias, decay_rate, taps, proj, teach, v, vt, weight
     )
-    grads, hidden_part = lax.optimization_barrier((grads, hidden_part))
-    own_grads = swap_all(combine(swap_all(grads, "seq", fours)), "seq", eights)
-    other_grads = lax.ppermute(own_grads, "seq", partner)
-    keep, send = product(jnp.stack([core, pair]), own_grads, other_grads, hidden_part)
-    summed = keep + lax.ppermute(send, "seq", across)
-    rows = swap_all(summed, "seq", twos).reshape(PARTS, 2 * COLS, 128)
-    total = jnp.sum(swap_all(rows, "dp"), axis=0)
-    spread = jnp.broadcast_to(total[None], (seq_devices // 2, 2 * COLS, 128))
+    grads, moved = lax.optimization_barrier((grads, moved))
+    rounded = swap_all(combine(swap_all(grads, "seq")), "dp")
+    keep, send = product(core, part, rounded, [moved[k] for k in range(PARTS)])
+    partial = keep + lax.ppermute(send, "seq", partner)
+    total = jnp.sum(swap_all(partial, "seq", same_core), axis=0)
+    spread = jnp.broadcast_to(total[None], partial.shape)
     own_blocks = swap_all(spread, "seq", same_core)
     other_blocks = lax.ppermute(own_blocks, "seq", partner)
-    return arrange(core[None], own_blocks, other_blocks).T
+    return arrange(core, own_blocks, other_blocks).T
 
 
 def solution(mesh):

time: 275 us -> 205 us (0.75)
  waiting for transfers between devices: 65.4 us -> 31.2 us
  blocking collectives: 102 us -> 72.9 us
  Pallas kernels: 69 us -> 44.2 us
  starting transfers between devices: 17.1 us -> 37.6 us
    all_gather x1, waiting for transfers between devices: 43.3 us -> 2.12 us  [local(): own_w = lax.all_gather(own_w, 'dp', axis=0)]
    all_to_all x6 -> x4, blocking collectives: 102 us -> 72.9 us  [swap_all(): return lax.all_to_all(x, axis, 0, 0, tiled=True, axis_index_groups=groups)]
    all_to_all x2, waiting for transfers between devices: 9.68 us -> 25.8 us  [swap_all(): return lax.all_to_all(x, axis, 0, 0, tiled=True, axis_index_groups=groups)]
    ppermute x2 -> x8, starting transfers between devices: 2.91 us -> 13.8 us  [the longest x7 13.3 us: spread_hidden(): moved.append(lax.ppermute(blocks[k], 'dp', route))]
    all_to_all x2, starting transfers between devices: 7.3 us -> 17.2 us  [swap_all(): return lax.all_to_all(x, axis, 0, 0, tiled=True, axis_index_groups=groups)]
    pallas_call x1, Pallas kernels: 26.1 us -> 17 us  [student(): pl.pallas_call(lambda *refs: student_kernel(*refs, weight=weight), out_sh...]
    ppermute x2 -> x8, waiting for transfers between devices: 10.7 us -> 1.65 us  [the longest x1 1.63 us: local(): partial = keep + lax.ppermute(send, 'seq', partner)]
    pallas_call x1, Pallas kernels: 23.4 us -> 14.8 us  [attend(): pl.pallas_call(attend_kernel, out_shape=(jax.ShapeDtypeStruct((DIM, SEQ),...]
  transfers between devices with their start and end apart: 8 -> 14, of which waited for: 5 -> 4; matrix products, arithmetic and copies ran while one was open for 1% -> 1% of each run, Pallas kernels for 24% -> 21%
where the time goes in v3:
time: 205 us; the launch traced here: 204 us
  blocking collectives  72.9 us (36%)
  Pallas kernels  44.2 us (22%)
  starting transfers between devices  37.6 us (18%)
  waiting for transfers between devices  31.2 us (15%)
  between operations  13.5 us (7%)
  local copies, waits for them, and re-layouts  4.6 us (2%)
    all_to_all x4, blocking collectives, swap_all(): return lax.all_to_all(x, axis, 0, 0, tiled=True, axis_index_groups=groups)  72.9 us
    all_to_all x2, waiting for transfers between devices, swap_all(): return lax.all_to_all(x, axis, 0, 0, tiled=True, axis_index_groups=groups)  25.8 us
    all_to_all x2, starting transfers between devices, swap_all(): return lax.all_to_all(x, axis, 0, 0, tiled=True, axis_index_groups=groups)  17.2 us
    pallas_call x1, Pallas kernels, student(): pl.pallas_call(lambda *refs: student_kernel(*refs, weight=weight), out_sh...  17 us
    pallas_call x1, Pallas kernels, attend(): pl.pallas_call(attend_kernel, out_shape=(jax.ShapeDtypeStruct((DIM, SEQ),...  14.8 us
    ppermute x7, starting transfers between devices, spread_hidden(): moved.append(lax.ppermute(blocks[k], 'dp', route))  13.3 us
    pallas_call x1, Pallas kernels, project(): pl.pallas_call(project_kernel, out_shape=jax.ShapeDtypeStruct((HEADS, COL...  4.69 us
  transfers between devices with their start and end apart: 14, of which 4 were waited for; matrix products, arithmetic and copies ran while one was open for 1% of the time, Pallas kernels for 21%

profile of v3, /device:TPU:1, one launch (start us, length us, event | category | flops | bytes accessed | tf_op | source)
XLA Modules:
  0.0 204.1 jit_solution(3856166307410377497)
XLA Ops:
  6.5 0.0 copy-start
  6.5 0.0 all-gather.3.cloned.1.call-start
  6.5 1.1 copy-done
  7.6 0.7 dynamic-slice_bitcast_fusion
  8.3 0.0 all-gather.3.cloned.1.call-update
  8.4 2.7 %shard_map.91 = bf16[32,272,128]{2,1,0:T(8,128)(2,1)} custom-call(bf16[1,128,4096]{2,1,0:T(8,128)(2,1)} %q_ref.1, bf16[1,128,1024]{2,1,0:T(8,128)(2,1)} %k_ref.1, bf16[1,128,1024]{2,1,0:T(8,128)(2,1)} %v_ref.1, s32[1,128]{1,0:T(1,128)} %doc_ref.1), custom_call_target="tpu_custom_call" | custom-call | bytes 4194304 | tf_op jit(solution)/shard_map/pallas_call | solution.py:83
  11.0 0.0 copy-start.4
  11.1 8.7 %all-to-all-start = ((bf16[32,272,128]{2,1,0:T(8,128)(2,1)}), bf16[32,272,128]{2,1,0:T(8,128)(2,1)S(1)}, u32[]{:S(2)}, u32[]{:S(2)}) async-start(bf16[32,272,128]{2,1,0:T(8,128)(2,1)} %shard_map.91), calls=%async_computation | async-start | bytes 4456448 | tf_op jit(solution)/shard_map/all_to_all | solution.py:570
  19.8 0.0 copy-done.4
  19.8 0.8 copy.10
  20.6 3.1 %shard_map.92 = (bf16[128,1024]{1,0:T(8,128)(2,1)}, bf16[128,1024]{1,0:T(8,128)(2,1)}, bf16[128,1024]{1,0:T(8,128)(2,1)}, bf16[128,1024]{1,0:T(8,128)(2,1)}, bf1...) custom-call(s32[1]{0:T(128)} %bitcast.1.part_ref, ...), custom_call_target="tpu_custom_call" | custom-call | bytes 4194304 | tf_op jit(solution)/shard_map/pallas_call | solution.py:108
  23.7 25.8 %all-to-all-done.own_ref = bf16[32,272,128]{2,1,0:T(8,128)(2,1)S(1)} async-done(((bf16[32,272,128]{2,1,0:T(8,128)(2,1)}), bf16[32,272,128]{2,1,0:T(8,128)(2,1)S(1)}, u32[]{:S(2)}, u32[]{:S(2)}) %all-to-all-start) | async-done | bytes 2228256 | tf_op jit(solution)/shard_map/all_to_all | solution.py:570
  49.5 0.0 copy-start.2
  49.5 2.1 %all-gather.3.cloned.1.call-done = bf16[2304,512]{1,0:T(8,128)(2,1)} async-done(((bf16[288,512]{1,0:T(8,128)(2,1)}), bf16[2304,512]{1,0:T(8,128)(2,1)}) %all-gather.3.cloned.1.call-update) | async-done | bytes 2359312 | tf_op jit(solution)/shard_map/all_gather | solution.py:595
  51.6 3.6 %collective-permute-start.1 = (bf16[8,288,512]{2,1,0:T(8,128)(2,1)}, bf16[8,288,512]{2,1,0:T(8,128)(2,1)}, u32[]{:S(2)}, u32[]{:S(2)}) collective-permute-start(bf16[8,288,512]{2,1,0:T(8,128)(2,1)} %bitcast.8), channel_id=1, source_target_pairs={{0,8},{8,0},{16,24},{24,16},{32,40},{40,32},{48,56},{56,48},{64,72... | collective-permute-start | bytes 7077896 | tf_op jit(solution)/shard_map/ppermute | solution.py:602
  55.2 1.1 slice.3
  56.3 0.0 copy-done.2
  56.3 0.0 collective-permute-start
  56.3 0.8 collective-permute-start.2
  57.2 1.8 collective-permute-start.3
  59.0 1.8 collective-permute-start.4
  60.8 0.0 collective-permute-done.1.other_ref
  60.8 2.8 %collective-permute-start.5 = (bf16[128,1024]{1,0:T(8,128)(2,1)}, bf16[128,1024]{1,0:T(8,128)(2,1)S(1)}, u32[]{:S(2)}, u32[]{:S(2)}) collective-permute-start(bf16[128,1024]{1,0:T(8,128)(2,1)} %get-tuple-element.58), channel_id=1, source_target_pairs={{0,4},{1,5},{2,6},{3,7},{4,0},{5,1},{6,2},{7,3},{8,12},{9,13},{10,... | collective-permute-start | bytes 786440 | tf_op jit(solution)/shard_map/ppermute | solution.py:577
  63.6 4.7 %shard_map.94 = f32[32,40,128]{2,1,0:T(8,128)} custom-call(s32[1]{0:T(128)} %bitcast.core_ref, bf16[1,128,8192]{2,1,0:T(8,128)(2,1)} %hid_ref.3, bf16[8,288,512]{2,1,0:T(8,128)(2,1)} %bitcast.9, bf16[8,288,512]{2,1,0:T(8,128)(2,1)} %collective-permute-done.1.other_ref), custom_call_target="tpu_custom_call" | custom-call | flops 603979776 | bytes 8388608 | tf_op jit(solution)/shard_map/pallas_call | solution.py:150
  68.3 8.5 %all-to-all-start.1 = ((f32[32,40,128]{2,1,0:T(8,128)}), f32[32,40,128]{2,1,0:T(8,128)S(1)}, u32[]{:S(2)}, u32[]{:S(2)}) async-start(f32[32,40,128]{2,1,0:T(8,128)} %shard_map.94), calls=%async_computation.1 | async-start | bytes 1310720 | tf_op jit(solution)/shard_map/all_to_all | solution.py:570
  76.8 0.0 copy-start.5
  76.8 0.0 collective-permute-done.other_ref
  76.8 2.6 %collective-permute-start.6 = (bf16[128,1024]{1,0:T(8,128)(2,1)}, bf16[128,1024]{1,0:T(8,128)(2,1)S(1)}, u32[]{:S(2)}, u32[]{:S(2)}) collective-permute-start(bf16[128,1024]{1,0:T(8,128)(2,1)} %get-tuple-element.59), channel_id=1, source_target_pairs={{0,5},{1,6},{2,7},{3,0},{4,1},{5,2},{6,3},{7,4},{8,13},{9,14},{10,... | collective-permute-start | bytes 786440 | tf_op jit(solution)/shard_map/ppermute | solution.py:577
  79.4 14.8 %shard_map.93 = (bf16[128,4096]{1,0:T(8,128)(2,1)}, bf16[4096,128]{1,0:T(8,128)(2,1)}, bf16[128,4096]{1,0:T(8,128)(2,1)}, s32[4]{0:T(128)}) custom-call(s32[1]{0:T(128)} %bitcast.core_ref, bf16[32,272,128]{2,1,0:T(8,128)(2,1)} %copy-done.2, bf16[32,128,128]{2,1,0:T(8,128)(2,1)} %collective-permute-done.other_ref), custom_call_target="tpu_custom_call" | custom-call | flops 8589934592 | bytes 8388608 | tf_op jit(solution)/shard_map/pallas_call | solution.py:263
  94.2 0.0 collective-permute-done.2.refs_1_
  94.2 2.6 %collective-permute-start.7 = (bf16[128,1024]{1,0:T(8,128)(2,1)}, bf16[128,1024]{1,0:T(8,128)(2,1)S(1)}, u32[]{:S(2)}, u32[]{:S(2)}) collective-permute-start(bf16[128,1024]{1,0:T(8,128)(2,1)} %get-tuple-element.60), channel_id=1, source_target_pairs={{0,6},{1,7},{2,0},{3,1},{4,2},{5,3},{6,4},{7,5},{8,14},{9,15},{10,... | collective-permute-start | bytes 786440 | tf_op jit(solution)/shard_map/ppermute | solution.py:577
  96.8 0.0 collective-permute-done.3.refs_2_
  96.8 0.0 copy-done.5
  96.8 0.8 collective-permute-start.8
  97.6 0.0 all-to-all-done.1.refs_5_
  97.6 0.0 copy-start.3
  97.6 0.8 copy-done.3
  98.5 17.0 %shard_map.95 = f32[32,40,128]{2,1,0:T(8,128)} custom-call(s32[1]{0:T(128)} %bitcast.2.refs_0_, s32[4]{0:T(128)} %get-tuple-element.48.refs_1_, f32[32]{0:T(128)} %refs_2_.1, f32[32]{0:T(128)} %refs_3_.1, f32[256,4]{1,0:T(8,128)} %bitcast.10, f32[32,40,128]{2,1,0:T(8,128)} %copy-done.3, bf16[128,4096]{1,0:T(8,128)(2,1)} %get-tuple-element.51.refs_6_, ...), custom_call_target="tpu_custom_call" | custom-call | flops 8589934592 | bytes 8388608 | tf_op jit(solution)/shard_map/pallas_call | solution.py:470
  115.4 0.0 copy-start.1
  115.4 0.0 collective-permute-done.4.refs_3_
  115.4 0.0 collective-permute-done.5.refs_4_
  115.4 0.0 collective-permute-done.6.refs_5_
  115.5 0.0 collective-permute-done.7.refs_6_
  115.5 0.0 collective-permute-done.8.refs_7_
  115.5 21.2 %all_to_all.30.in_ref = f32[32,40,128]{2,1,0:T(8,128)S(1)} all-to-all(f32[32,40,128]{2,1,0:T(8,128)} %shard_map.95), channel_id=1, replica_groups=mesh['seq'=32,'dp'=8] {'seq'}, dimensions={0} | all-to-all | bytes 1310720 | tf_op jit(solution)/shard_map/all_to_all | solution.py:570
  136.7 0.1 shard_map.96
  136.7 24.0 %all_to_all.31.grad_ref = bf16[8,288,128]{2,1,0:T(8,128)(2,1)S(1)} all-to-all(bf16[8,288,128]{2,1,0:T(8,128)(2,1)S(1)} %shard_map.96), channel_id=1, replica_groups=mesh['seq'=32,'dp'=8] {'dp'}, dimensions={0} | all-to-all | bytes 1179648 | tf_op jit(solution)/shard_map/all_to_all | solution.py:570
  160.8 0.0 copy-done.1
  160.8 0.8 shard_map.97
  161.6 0.5 collective-permute-start.9
  162.1 1.6 collective-permute-done.9
  163.7 0.1 add.7
  163.8 14.4 %all_to_all.32 = f32[16,72,128]{2,1,0:T(8,128)S(1)} all-to-all(f32[16,72,128]{2,1,0:T(8,128)S(1)} %add.7), channel_id=1, replica_groups={{0,16,32,48,64,80,96,112,128,144,160,176,192,208,224,240},{8,24,40,56,7..., dimensions={0} | all-to-all | bytes 1179648 | tf_op jit(solution)/shard_map/all_to_all | solution.py:570
  178.2 13.3 %all_to_all.33.own_ref = f32[16,72,128]{2,1,0:T(8,128)S(1)} all-to-all(f32[16,72,128]{2,1,0:T(8,128)S(1)} %broadcast_in_dim.18), channel_id=1, replica_groups={{0,16,32,48,64,80,96,112,128,144,160,176,192,208,224,240},{8,24,40,56,7..., dimensions={0} | all-to-all | bytes 1179648 | tf_op jit(solution)/shard_map/all_to_all | solution.py:570
  191.6 2.9 %collective-permute-start.10 = (f32[16,72,128]{2,1,0:T(8,128)S(1)}, f32[16,72,128]{2,1,0:T(8,128)S(1)}, u32[]{:S(2)}, u32[]{:S(2)}) collective-permute-start(f32[16,72,128]{2,1,0:T(8,128)S(1)} %all_to_all.33.own_ref), channel_id=1, source_target_pairs={{0,8},{8,0},{16,24},{24,16},{32,40},{40,32},{48,56},{56,48},{64,72... | collective-permute-start | bytes 1769480 | tf_op jit(solution)/shard_map/ppermute | solution.py:616
  194.5 1.6 collective-permute-done.10.other_ref
  196.1 1.1 shard_map.98
  (2 shorter events, 0.1 us)
Async XLA Ops:
  6.5 1.1 copy-start
  6.5 45.1 %all-gather.3.cloned.1.call-start = ((), (), s32[]{:S(2)}) async-start(), calls=%async_computation.6 | async-start | bytes 2654208 | tf_op jit(solution)/shard_map/all_gather | solution.py:595
  11.0 8.7 %copy-start.4 = (f32[4,256]{1,0:T(4,128)S(1)}, f32[4,256]{1,0:T(4,128)}, u32[]{:S(2)}) copy-start(f32[4,256]{1,0:T(4,128)} %param.15) | copy-start | bytes 12292
  11.1 38.4 %all-to-all-start = ((bf16[32,272,128]{2,1,0:T(8,128)(2,1)}), bf16[32,272,128]{2,1,0:T(8,128)(2,1)S(1)}, u32[]{:S(2)}, u32[]{:S(2)}) async-start(bf16[32,272,128]{2,1,0:T(8,128)(2,1)} %shard_map.91), calls=%async_computation | async-start | bytes 4456448 | tf_op jit(solution)/shard_map/all_to_all | solution.py:570
  49.5 6.9 %copy-start.2 = (bf16[32,272,128]{2,1,0:T(8,128)(2,1)}, bf16[32,272,128]{2,1,0:T(8,128)(2,1)S(1)}, u32[]{:S(2)}) copy-start(bf16[32,272,128]{2,1,0:T(8,128)(2,1)S(1)} %all-to-all-done.own_ref) | copy-start | bytes 6684676
  51.6 9.2 %collective-permute-start.1 = (bf16[8,288,512]{2,1,0:T(8,128)(2,1)}, bf16[8,288,512]{2,1,0:T(8,128)(2,1)}, u32[]{:S(2)}, u32[]{:S(2)}) collective-permute-start(bf16[8,288,512]{2,1,0:T(8,128)(2,1)} %bitcast.8), channel_id=1, source_target_pairs={{0,8},{8,0},{16,24},{24,16},{32,40},{40,32},{48,56},{56,48},{64,72... | collective-permute-start | bytes 7077896 | tf_op jit(solution)/shard_map/ppermute | solution.py:602
  56.3 20.4 %collective-permute-start = (bf16[32,128,128]{2,1,0:T(8,128)(2,1)}, bf16[32,128,128]{2,1,0:T(8,128)(2,1)}, u32[]{:S(2)}, u32[]{:S(2)}) collective-permute-start(bf16[32,128,128]{2,1,0:T(8,128)(2,1)} %slice.3), channel_id=1, source_target_pairs={{0,8},{8,0},{16,24},{24,16},{32,40},{40,32},{48,56},{56,48},{64,72... | collective-permute-start | bytes 3145736 | tf_op jit(solution)/shard_map/ppermute | solution.py:603
  56.3 37.8 %collective-permute-start.2 = (bf16[128,1024]{1,0:T(8,128)(2,1)}, bf16[128,1024]{1,0:T(8,128)(2,1)S(1)}, u32[]{:S(2)}, u32[]{:S(2)}) collective-permute-start(bf16[128,1024]{1,0:T(8,128)(2,1)} %get-tuple-element.55), channel_id=1, source_target_pairs={{0,1},{1,2},{2,3},{3,4},{4,5},{5,6},{6,7},{7,0},{8,9},{9,10},{10,1... | collective-permute-start | bytes 786440 | tf_op jit(solution)/shard_map/ppermute | solution.py:577
  57.2 39.6 %collective-permute-start.3 = (bf16[128,1024]{1,0:T(8,128)(2,1)}, bf16[128,1024]{1,0:T(8,128)(2,1)S(1)}, u32[]{:S(2)}, u32[]{:S(2)}) collective-permute-start(bf16[128,1024]{1,0:T(8,128)(2,1)} %get-tuple-element.56), channel_id=1, source_target_pairs={{0,2},{1,3},{2,4},{3,5},{4,6},{5,7},{6,0},{7,1},{8,10},{9,11},{10,... | collective-permute-start | bytes 786440 | tf_op jit(solution)/shard_map/ppermute | solution.py:577
  59.0 56.4 %collective-permute-start.4 = (bf16[128,1024]{1,0:T(8,128)(2,1)}, bf16[128,1024]{1,0:T(8,128)(2,1)S(1)}, u32[]{:S(2)}, u32[]{:S(2)}) collective-permute-start(bf16[128,1024]{1,0:T(8,128)(2,1)} %get-tuple-element.57), channel_id=1, source_target_pairs={{0,3},{1,4},{2,5},{3,6},{4,7},{5,0},{6,1},{7,2},{8,11},{9,12},{10,... | collective-permute-start | bytes 786440 | tf_op jit(solution)/shard_map/ppermute | solution.py:577
  60.8 54.6 %collective-permute-start.5 = (bf16[128,1024]{1,0:T(8,128)(2,1)}, bf16[128,1024]{1,0:T(8,128)(2,1)S(1)}, u32[]{:S(2)}, u32[]{:S(2)}) collective-permute-start(bf16[128,1024]{1,0:T(8,128)(2,1)} %get-tuple-element.58), channel_id=1, source_target_pairs={{0,4},{1,5},{2,6},{3,7},{4,0},{5,1},{6,2},{7,3},{8,12},{9,13},{10,... | collective-permute-start | bytes 786440 | tf_op jit(solution)/shard_map/ppermute | solution.py:577
  68.3 29.3 %all-to-all-start.1 = ((f32[32,40,128]{2,1,0:T(8,128)}), f32[32,40,128]{2,1,0:T(8,128)S(1)}, u32[]{:S(2)}, u32[]{:S(2)}) async-start(f32[32,40,128]{2,1,0:T(8,128)} %shard_map.94), calls=%async_computation.1 | async-start | bytes 1310720 | tf_op jit(solution)/shard_map/all_to_all | solution.py:570
  76.8 20.0 %copy-start.5 = (bf16[128,1024]{1,0:T(8,128)(2,1)S(1)}, bf16[128,1024]{1,0:T(8,128)(2,1)}, u32[]{:S(2)}) copy-start(bf16[128,1024]{1,0:T(8,128)(2,1)} %get-tuple-element.61) | copy-start | bytes 786436
  76.8 38.7 %collective-permute-start.6 = (bf16[128,1024]{1,0:T(8,128)(2,1)}, bf16[128,1024]{1,0:T(8,128)(2,1)S(1)}, u32[]{:S(2)}, u32[]{:S(2)}) collective-permute-start(bf16[128,1024]{1,0:T(8,128)(2,1)} %get-tuple-element.59), channel_id=1, source_target_pairs={{0,5},{1,6},{2,7},{3,0},{4,1},{5,2},{6,3},{7,4},{8,13},{9,14},{10,... | collective-permute-start | bytes 786440 | tf_op jit(solution)/shard_map/ppermute | solution.py:577
  94.2 21.3 %collective-permute-start.7 = (bf16[128,1024]{1,0:T(8,128)(2,1)}, bf16[128,1024]{1,0:T(8,128)(2,1)S(1)}, u32[]{:S(2)}, u32[]{:S(2)}) collective-permute-start(bf16[128,1024]{1,0:T(8,128)(2,1)} %get-tuple-element.60), channel_id=1, source_target_pairs={{0,6},{1,7},{2,0},{3,1},{4,2},{5,3},{6,4},{7,5},{8,14},{9,15},{10,... | collective-permute-start | bytes 786440 | tf_op jit(solution)/shard_map/ppermute | solution.py:577
  96.8 18.7 %collective-permute-start.8 = (bf16[128,1024]{1,0:T(8,128)(2,1)S(1)}, bf16[128,1024]{1,0:T(8,128)(2,1)S(1)}, u32[]{:S(2)}, u32[]{:S(2)}) collective-permute-start(bf16[128,1024]{1,0:T(8,128)(2,1)S(1)} %copy-done.5), channel_id=1, source_target_pairs={{0,7},{1,0},{2,1},{3,2},{4,3},{5,4},{6,5},{7,6},{8,15},{9,8},{10,9... | collective-permute-start | bytes 786440 | tf_op jit(solution)/shard_map/ppermute | solution.py:577
  97.6 0.8 copy-start.3
  115.4 45.3 %copy-start.1 = (bf16[128,1024]{1,0:T(8,128)(2,1)S(1)}, bf16[128,1024]{1,0:T(8,128)(2,1)}, u32[]{:S(2)}) copy-start(bf16[128,1024]{1,0:T(8,128)(2,1)} %get-tuple-element.63.refs_0_) | copy-start | bytes 786436
  161.6 2.2 %collective-permute-start.9 = (f32[16,72,128]{2,1,0:T(8,128)S(1)}, f32[16,72,128]{2,1,0:T(8,128)S(1)}, u32[]{:S(2)}, u32[]{:S(2)}) collective-permute-start(f32[16,72,128]{2,1,0:T(8,128)S(1)} %get-tuple-element.72), channel_id=1, source_target_pairs={{0,8},{8,0},{16,24},{24,16},{32,40},{40,32},{48,56},{56,48},{64,72... | collective-permute-start | bytes 1769480 | tf_op jit(solution)/shard_map/ppermute | solution.py:612
  191.6 4.6 %collective-permute-start.10 = (f32[16,72,128]{2,1,0:T(8,128)S(1)}, f32[16,72,128]{2,1,0:T(8,128)S(1)}, u32[]{:S(2)}, u32[]{:S(2)}) collective-permute-start(f32[16,72,128]{2,1,0:T(8,128)S(1)} %all_to_all.33.own_ref), channel_id=1, source_target_pairs={{0,8},{8,0},{16,24},{24,16},{32,40},{40,32},{48,56},{56,48},{64,72... | collective-permute-start | bytes 1769480 | tf_op jit(solution)/shard_map/ppermute | solution.py:616
Sparse Core Ops, SparseCore 0:
  9.1 42.4 all-gather.2

commit v4 on v3

--- a/solution.py
+++ b/solution.py
@@ -37,6 +37,7 @@
 NEG = -1e30
 VMEM = pl.BlockSpec(memory_space=pltpu.VMEM)
 SMEM = pl.BlockSpec(memory_space=pltpu.SMEM)
+ANY = pl.BlockSpec(memory_space=pl.ANY)
 
 NT = (((1,), (1,)), ((), ()))
 
@@ -161,7 +162,7 @@
             out_specs=pl.BlockSpec((HEADS, COLS, ROWS), lambda i, c: (0, 0, 0)),
             scratch_shapes=[pltpu.VMEM((width, ROWS), F32)],
         ),
-        compiler_params=params(60),
+        compiler_params=params(24),
         cost_estimate=pl.CostEstimate(
             flops=2 * ROWS * D * 288, bytes_accessed=8 << 20, transcendentals=0
         ),
@@ -169,39 +170,65 @@
 
 
 def attend_kernel(
-    core_ref, own_ref, other_ref, teach_ref, v_ref, vt_ref, n_ref, keys, turned, scores
+    core_ref,
+    own_ref,
+    other_ref,
+    teach_ref,
+    v_ref,
+    vt_ref,
+    n_ref,
+    queries,
+    labels,
+    keys,
+    values,
+    turned,
+    mixed,
+    scores,
+    sems,
+    out_sems,
 ):
-    docs = jnp.max(own_ref[:, 2 * ROWS :, :].astype(F32), axis=1)
+    first = PAD // ROWS
+    key_part = keys.at[pl.ds(first, BLOCKS)]
+    docs_in = pltpu.make_async_copy(own_ref.at[:, pl.ds(2 * ROWS, DOC_ROWS)], labels, sems.at[0])
+    query_in = pltpu.make_async_copy(own_ref.at[:, pl.ds(0, ROWS)], queries, sems.at[1])
+    own_kv = own_ref.at[:, pl.ds(ROWS, ROWS)]
+    is_key = core_ref[0] == 0
+
+    @pl.when(is_key)
+    def _():
+        pltpu.make_async_copy(other_ref, values, sems.at[2]).start()
+        pltpu.make_async_copy(own_kv, key_part, sems.at[3]).start()
+
+    @pl.when(jnp.logical_not(is_key))
+    def _():
+        pltpu.make_async_copy(own_kv, values, sems.at[2]).start()
+        pltpu.make_async_copy(other_ref, key_part, sems.at[3]).start()
+
+    docs_in.start()
+    query_in.start()
+    keys[0:first] = jnp.zeros((first, ROWS, DIM), BF16)
+    turned[:, 0:PAD] = jnp.zeros((DIM, PAD), BF16)
+    pltpu.make_async_copy(other_ref, values, sems.at[2]).wait()
+    v_out = pltpu.make_async_copy(values, v_ref, out_sems.at[0])
+    v_out.start()
+    for s in range(BLOCKS):
+        turned[:, PAD + s * ROWS : PAD + (s + 1) * ROWS] = values[s].T
+    vt_out = pltpu.make_async_copy(turned.at[:, pl.ds(PAD, SEQ)], vt_ref, out_sems.at[1])
+    vt_out.start()
+    docs_in.wait()
+    docs = jnp.max(labels[...].astype(F32), axis=1)
     for d in range(3):
         n_ref[d] = jnp.sum((docs < d + 0.5).astype(F32)).astype(jnp.int32)
     n_ref[3] = 0
-    if PAD:
-        keys[0:PAD, :] = jnp.zeros((PAD, DIM), BF16)
-        turned[:, 0:PAD] = jnp.zeros((DIM, PAD), BF16)
-
-    @pl.when(core_ref[0] == 0)
-    def _():
-        for s in range(BLOCKS):
-            keys[PAD + s * ROWS : PAD + (s + 1) * ROWS, :] = own_ref[s, ROWS : 2 * ROWS, :]
-            v_ref[s * ROWS : (s + 1) * ROWS, :] = other_ref[s]
-
-    @pl.when(core_ref[0] != 0)
-    def _():
-        for s in range(BLOCKS):
-            keys[PAD + s * ROWS : PAD + (s + 1) * ROWS, :] = other_ref[s]
-            v_ref[s * ROWS : (s + 1) * ROWS, :] = own_ref[s, ROWS : 2 * ROWS, :]
-
-    for s in range(BLOCKS):
-        block = v_ref[s * ROWS : (s + 1) * ROWS, :].T
-        turned[:, PAD + s * ROWS : PAD + (s + 1) * ROWS] = block
-        vt_ref[:, s * ROWS : (s + 1) * ROWS] = block
+    query_in.wait()
+    pltpu.make_async_copy(other_ref, key_part, sems.at[3]).wait()
 
     scale = DIM ** (-0.5) * math.log2(math.e)
 
     def rows(i, carry):
         q0 = i * QUERIES
         many = QUERIES // ROWS
-        query = jnp.concatenate([own_ref[many * i + k, 0:ROWS, :] for k in range(many)], 0)
+        query = queries[pl.ds(many * i, many)].reshape(QUERIES, DIM)
         first = scalar_start(q0, n_ref)
         last = scalar_start(q0 + QUERIES - 1, n_ref)
         need = q0 + QUERIES - first
@@ -213,11 +240,12 @@
 
         def tile(at, size):
             low = q0 + QUERIES - at - size
-            return low, pl.multiple_of(low + PAD, HALF), pl.ds(pl.multiple_of(at, HALF), size)
+            return low, low + PAD, pl.ds(pl.multiple_of(at, HALF), size)
 
         def score(at, size, masked, top):
             low, key_at, rows_at = tile(at, size)
-            s = mm_nt(keys[pl.ds(key_at, size), :], query)
+            block = keys[pl.ds(key_at // ROWS, size // ROWS)].reshape(size, DIM)
+            s = mm_nt(block, query)
             if masked:
                 k_at = low + lax.broadcasted_iota(jnp.int32, (size, QUERIES), 0)
                 s = jnp.where((k_at <= q_at) & (k_at >= start), s, NEG)
@@ -247,35 +275,53 @@
             _, key_at, rows_at = tile(at, size)
             p = jnp.exp2((scores[rows_at, :] - top) * scale)
             total = total + jnp.sum(p.reshape(size // 8, 8, QUERIES), axis=0)
-            return total, out + mm(turned[:, pl.ds(key_at, size)], p.astype(BF16))
+            return total, out + mm(
+                turned[:, pl.ds(pl.multiple_of(key_at, HALF), size)], p.astype(BF16)
+            )
 
         state = (jnp.zeros((8, QUERIES), F32), jnp.zeros((DIM, QUERIES), F32))
         state = lax.fori_loop(0, count, lambda j, t: mix(j * KEYS, KEYS, t), state)
         total, out = lax.fori_loop(0, ends, lambda j, t: mix(count * KEYS, HALF, t), state)
         total = jnp.sum(total, axis=0, keepdims=True)
-        teach_ref[:, pl.ds(pl.multiple_of(q0, QUERIES), QUERIES)] = (out / total).astype(BF16)
+        mixed[i] = (out / total).astype(BF16)
+        teach_out(i).start()
         return carry
 
+    def teach_out(i):
+        lanes = pl.ds(pl.multiple_of(i * QUERIES, QUERIES), QUERIES)
+        return pltpu.make_async_copy(mixed.at[i], teach_ref.at[:, lanes], out_sems.at[2 + i])
+
     lax.fori_loop(0, SEQ // QUERIES, rows, 0)
+    v_out.wait()
+    vt_out.wait()
+    for i in range(SEQ // QUERIES):
+        teach_out(i).wait()
 
 
 def attend(core, own, other):
+    many = SEQ // QUERIES
     return pl.pallas_call(
         attend_kernel,
         out_shape=(
             jax.ShapeDtypeStruct((DIM, SEQ), BF16),
-            jax.ShapeDtypeStruct((SEQ, DIM), BF16),
+            jax.ShapeDtypeStruct((BLOCKS, ROWS, DIM), BF16),
             jax.ShapeDtypeStruct((DIM, SEQ), BF16),
             jax.ShapeDtypeStruct((4,), jnp.int32),
         ),
-        in_specs=[SMEM, VMEM, VMEM],
-        out_specs=(VMEM, VMEM, VMEM, SMEM),
+        in_specs=[SMEM, ANY, ANY],
+        out_specs=(ANY, ANY, ANY, SMEM),
         scratch_shapes=[
-            pltpu.VMEM((PAD + SEQ, DIM), BF16),
+            pltpu.VMEM((BLOCKS, ROWS, DIM), BF16),
+            pltpu.VMEM((BLOCKS, DOC_ROWS, DIM), BF16),
+            pltpu.VMEM((BLOCKS + PAD // ROWS, ROWS, DIM), BF16),
+            pltpu.VMEM((BLOCKS, ROWS, DIM), BF16),
             pltpu.VMEM((DIM, PAD + SEQ), BF16),
+            pltpu.VMEM((many, DIM, QUERIES), BF16),
             pltpu.VMEM((SEQ + KEYS, QUERIES), F32),
+            pltpu.SemaphoreType.DMA((4,)),
+            pltpu.SemaphoreType.DMA((2 + many,)),
         ],
-        compiler_params=params(56),
+        compiler_params=params(),
         cost_estimate=pl.CostEstimate(
             flops=8 << 30, bytes_accessed=8 << 20, transcendentals=8 << 20
         ),
@@ -383,7 +429,7 @@
         fade = jnp.exp(jnp.where(allowed, cum - columns[c], NEG))
         mixing = fade * inner
         mix_high, mix_low = split(mixing)
-        values = v_ref[pl.ds(wide, SPAN), :]
+        values = v_ref[pl.ds(2 * c, 2)].reshape(SPAN, DIM)
         turned = vt_ref[:, pl.ds(wide, SPAN)]
         enter = jnp.where(start < base, jnp.exp(cum), 0.0)
         entered = gate_c * enter
@@ -503,15 +549,13 @@
         rows[128 + g * STATE : 128 + (g + 1) * STATE] = gates[STATE:]
     for h in range(HEADS):
         rows[256 + h : 257 + h] = in_ref[h, 2 * STATE : 2 * STATE + 1]
-    rounded = rows[...].astype(BF16)
-    for d in range(PARTS):
-        out_ref[d] = rounded
+    out_ref[...] = rows[...].astype(BF16)
 
 
 def combine(parts):
     return pl.pallas_call(
         combine_kernel,
-        out_shape=jax.ShapeDtypeStruct((PARTS, WIDTH, ROWS), BF16),
+        out_shape=jax.ShapeDtypeStruct((WIDTH, ROWS), BF16),
         in_specs=[VMEM],
         out_specs=VMEM,
         scratch_shapes=[pltpu.VMEM((WIDTH, ROWS), F32)],
@@ -519,11 +563,9 @@
     )(parts)
 
 
-def product_kernel(core_ref, part_ref, grad_ref, *refs):
-    blocks, (keep_ref, send_ref) = refs[:PARTS], refs[PARTS:]
-    left = jnp.concatenate(
-        [grad_ref[lax.rem(part_ref[0] + PARTS - k, PARTS)] for k in range(PARTS)], 1
-    )
+def product_kernel(core_ref, *refs):
+    grads, blocks, (keep_ref, send_ref) = refs[:PARTS], refs[PARTS : 2 * PARTS], refs[2 * PARTS :]
+    left = jnp.concatenate([grad[...] for grad in grads], 1)
     half = blocks[0].shape[1] // 2
     for ref, core in ((send_ref, 1 - core_ref[0]), (keep_ref, core_ref[0])):
         lanes = pl.ds(pl.multiple_of(core * half, half), half)
@@ -533,18 +575,18 @@
                 ref[4 * r + q] = part[r * 72 : (r + 1) * 72, q * 128 : (q + 1) * 128]
 
 
-def product(core, part, grads, blocks):
+def product(core, grads, blocks):
     shape = jax.ShapeDtypeStruct((16, WIDTH // 4, 128), F32)
     return pl.pallas_call(
         product_kernel,
         out_shape=(shape, shape),
-        in_specs=[SMEM, SMEM, VMEM] + [VMEM] * PARTS,
+        in_specs=[SMEM] + [VMEM] * (2 * PARTS),
         out_specs=(VMEM, VMEM),
         compiler_params=params(24),
         cost_estimate=pl.CostEstimate(
             flops=2 * WIDTH * 1024 * 1024, bytes_accessed=4 << 20, transcendentals=0
         ),
-    )(core, part, grads, *blocks)
+    )(core, *grads, *blocks)
 
 
 def arrange_kernel(core_ref, own_ref, other_ref, out_ref):
@@ -594,21 +636,30 @@
     own_w = lax.dynamic_slice_in_dim(turned_w, core[0] * half, half, 1)
     own_w = lax.all_gather(own_w, "dp", axis=0)
     own = swap_all(pack_teacher(queries, keys, values, docs), "seq")
-    own, own_w, taps, blocks = lax.optimization_barrier(
-        (own, own_w, conv_weight.T, pack_hidden(part, hidden))
+    other = lax.ppermute(own[:, ROWS : 2 * ROWS, :], "seq", partner)
+    own, other, own_w, taps, blocks = lax.optimization_barrier(
+        (own, other, own_w, conv_weight.T, pack_hidden(part, hidden))
     )
-    order = (4, 5, 3, 6, 2, 1, 7)
+    order, last = (4, 5, 3, 6, 2), (1, 7)
     moved = {0: blocks[0]} | dict(zip(order, spread_hidden(blocks, order)))
+    waiting = {k: blocks[k] for k in last}
     other_w = lax.ppermute(own_w, "seq", partner)
-    other = lax.ppermute(own[:, ROWS : 2 * ROWS, :], "seq", partner)
     proj = swap_all(project(core, hidden, own_w, other_w), "seq")
     teach, v, vt, counts = attend(core, own, other)
     grads = student(
         head[None], counts, dt_bias, decay_rate, taps, proj, teach, v, vt, weight
     )
-    grads, moved = lax.optimization_barrier((grads, moved))
-    rounded = swap_all(combine(swap_all(grads, "seq")), "dp")
-    keep, send = product(core, part, rounded, [moved[k] for k in range(PARTS)])
+    grads, moved, waiting = lax.optimization_barrier((grads, moved, waiting))
+    rounded, nearby = lax.optimization_barrier(
+        (combine(swap_all(grads, "seq")), spread_hidden(waiting, last))
+    )
+    moved.update(zip(last, nearby))
+    far_first = (4, 5, 3, 6, 2, 7, 1)
+    copies = {k: rounded for k in far_first}
+    spread_grads = {0: rounded} | dict(zip(far_first, spread_hidden(copies, far_first)))
+    keep, send = product(
+        core, [spread_grads[k] for k in range(PARTS)], [moved[k] for k in range(PARTS)]
+    )
     partial = keep + lax.ppermute(send, "seq", partner)
     total = jnp.sum(swap_all(partial, "seq", same_core), axis=0)
     spread = jnp.broadcast_to(total[None], partial.shape)

time: 205 us -> 200 us (0.976)
  waiting for transfers between devices: 31.2 us -> 21 us
  starting transfers between devices: 37.6 us -> 47 us
  blocking collectives: 72.9 us -> 67.4 us
  local copies, waits for them, and re-layouts: 4.6 us -> 7.63 us
    ppermute x7 -> x14, starting transfers between devices: 13.3 us -> 29.5 us  [spread_hidden(): moved.append(lax.ppermute(blocks[k], 'dp', route))]
    all_to_all x2, waiting for transfers between devices: 25.8 us -> 10.2 us  [swap_all(): return lax.all_to_all(x, axis, 0, 0, tiled=True, axis_index_groups=groups)]
    ppermute x7 -> x14, waiting for transfers between devices: 0.02 us -> 7.54 us  [spread_hidden(): moved.append(lax.ppermute(blocks[k], 'dp', route))]
    all_to_all x4 -> x3, blocking collectives: 72.9 us -> 67.4 us  [swap_all(): return lax.all_to_all(x, axis, 0, 0, tiled=True, axis_index_groups=groups)]
    all_to_all x2, starting transfers between devices: 17.2 us -> 12.9 us  [swap_all(): return lax.all_to_all(x, axis, 0, 0, tiled=True, axis_index_groups=groups)]
    ppermute x1, starting transfers between devices: 3.64 us -> 0.2 us  [local(): other_w = lax.ppermute(own_w, 'seq', partner)]
    unnamed x13 -> x19, local copies, waits for them, and re-layouts: 2.73 us -> 5.77 us
    all_gather x1, waiting for transfers between devices: 2.12 us -> 0.01 us  [local(): own_w = lax.all_gather(own_w, 'dp', axis=0)]
  transfers between devices with their start and end apart: 14 -> 21, of which waited for: 4 -> 7; matrix products, arithmetic and copies ran while one was open for 1% -> 1% of each run, Pallas kernels for 21% -> 20%
where the time goes in v4:
time: 200 us
  blocking collectives  67.4 us (34%)
  starting transfers between devices  47 us (24%)
  Pallas kernels  43 us (22%)
  waiting for transfers between devices  21 us (10%)
  between operations  13.6 us (7%)
  local copies, waits for them, and re-layouts  7.63 us (4%)
    all_to_all x3, blocking collectives, swap_all(): return lax.all_to_all(x, axis, 0, 0, tiled=True, axis_index_groups=groups)  67.4 us
    ppermute x14, starting transfers between devices, spread_hidden(): moved.append(lax.ppermute(blocks[k], 'dp', route))  29.5 us
    pallas_call x1, Pallas kernels, student(): pl.pallas_call(lambda *refs: student_kernel(*refs, weight=weight), out_sh...  17 us
    pallas_call x1, Pallas kernels, attend(): pl.pallas_call(attend_kernel, out_shape=(jax.ShapeDtypeStruct((DIM, SEQ),...  14.6 us
    all_to_all x2, starting transfers between devices, swap_all(): return lax.all_to_all(x, axis, 0, 0, tiled=True, axis_index_groups=groups)  12.9 us
    all_to_all x2, waiting for transfers between devices, swap_all(): return lax.all_to_all(x, axis, 0, 0, tiled=True, axis_index_groups=groups)  10.2 us
    ppermute x14, waiting for transfers between devices, spread_hidden(): moved.append(lax.ppermute(blocks[k], 'dp', route))  7.54 us
    unnamed x19, local copies, waits for them, and re-layouts  5.77 us
  transfers between devices with their start and end apart: 21, of which 7 were waited for; matrix products, arithmetic and copies ran while one was open for 1% of the time, Pallas kernels for 20%

profile of v4, /device:TPU:1, one launch (start us, length us, event | category | flops | bytes accessed | tf_op | source)
XLA Modules:
  0.0 199.7 jit_solution(3854653982980981928)
XLA Ops:
  6.5 0.0 copy-start
  6.5 0.0 all-gather.3.cloned.1.call-start
  6.5 1.1 copy-done
  7.6 0.7 dynamic-slice_bitcast_fusion
  8.3 0.0 all-gather.3.cloned.1.call-update
  8.4 2.7 %shard_map.91 = bf16[32,272,128]{2,1,0:T(8,128)(2,1)} custom-call(bf16[1,128,4096]{2,1,0:T(8,128)(2,1)} %q_ref.1, bf16[1,128,1024]{2,1,0:T(8,128)(2,1)} %k_ref.1, bf16[1,128,1024]{2,1,0:T(8,128)(2,1)} %v_ref.1, s32[1,128]{1,0:T(1,128)} %doc_ref.1), custom_call_target="tpu_custom_call" | custom-call | bytes 4194304 | tf_op jit(solution)/shard_map/pallas_call | solution.py:84
  11.1 38.9 %all_to_all.25.own_ref = bf16[32,272,128]{2,1,0:T(8,128)(2,1)S(1)} all-to-all(bf16[32,272,128]{2,1,0:T(8,128)(2,1)} %shard_map.91), channel_id=1, replica_groups=mesh['seq'=32,'dp'=8] {'seq'}, dimensions={0} | all-to-all | bytes 4456448 | tf_op jit(solution)/shard_map/all_to_all | solution.py:612
  50.0 1.4 copy-done.4
  51.4 1.1 slice.4
  52.5 0.4 collective-permute-start
  52.9 0.0 copy-done.6
  52.9 0.8 copy.10
  53.7 3.0 %shard_map.92 = (bf16[128,1024]{1,0:T(8,128)(2,1)}, bf16[128,1024]{1,0:T(8,128)(2,1)}, bf16[128,1024]{1,0:T(8,128)(2,1)}, bf16[128,1024]{1,0:T(8,128)(2,1)}, bf1...) custom-call(s32[1]{0:T(128)} %bitcast.5.part_ref, ...), custom_call_target="tpu_custom_call" | custom-call | bytes 4194304 | tf_op jit(solution)/shard_map/pallas_call | solution.py:109
  56.7 0.0 collective-permute-done.other_ref
  56.7 0.2 collective-permute-start.1
  56.9 3.0 %collective-permute-start.2 = (bf16[128,1024]{1,0:T(8,128)(2,1)}, bf16[128,1024]{1,0:T(8,128)(2,1)S(1)}, u32[]{:S(2)}, u32[]{:S(2)}) collective-permute-start(bf16[128,1024]{1,0:T(8,128)(2,1)} %get-tuple-element.60), channel_id=1, source_target_pairs={{0,2},{1,3},{2,4},{3,5},{4,6},{5,7},{6,0},{7,1},{8,10},{9,11},{10,... | collective-permute-start | bytes 786440 | tf_op jit(solution)/shard_map/ppermute | solution.py:619
  59.9 4.7 %collective-permute-start.3 = (bf16[128,1024]{1,0:T(8,128)(2,1)}, bf16[128,1024]{1,0:T(8,128)(2,1)S(1)}, u32[]{:S(2)}, u32[]{:S(2)}) collective-permute-start(bf16[128,1024]{1,0:T(8,128)(2,1)} %get-tuple-element.61), channel_id=1, source_target_pairs={{0,3},{1,4},{2,5},{3,6},{4,7},{5,0},{6,1},{7,2},{8,11},{9,12},{10,... | collective-permute-start | bytes 786440 | tf_op jit(solution)/shard_map/ppermute | solution.py:619
  64.6 1.0 collective-permute-start.4
  65.5 4.0 %collective-permute-start.5 = (bf16[128,1024]{1,0:T(8,128)(2,1)}, bf16[128,1024]{1,0:T(8,128)(2,1)}, u32[]{:S(2)}, u32[]{:S(2)}) collective-permute-start(bf16[128,1024]{1,0:T(8,128)(2,1)} %get-tuple-element.63), channel_id=1, source_target_pairs={{0,5},{1,6},{2,7},{3,0},{4,1},{5,2},{6,3},{7,4},{8,13},{9,14},{10,... | collective-permute-start | bytes 786440 | tf_op jit(solution)/shard_map/ppermute | solution.py:619
  69.5 0.0 collective-permute-done.1.other_ref
  69.5 2.4 %collective-permute-start.6 = (bf16[128,1024]{1,0:T(8,128)(2,1)}, bf16[128,1024]{1,0:T(8,128)(2,1)}, u32[]{:S(2)}, u32[]{:S(2)}) collective-permute-start(bf16[128,1024]{1,0:T(8,128)(2,1)} %get-tuple-element.64), channel_id=1, source_target_pairs={{0,6},{1,7},{2,0},{3,1},{4,2},{5,3},{6,4},{7,5},{8,14},{9,15},{10,... | collective-permute-start | bytes 786440 | tf_op jit(solution)/shard_map/ppermute | solution.py:619
  71.9 0.0 copy-done.1
  71.9 1.7 copy-done.2
  73.6 2.7 %shard_map.94 = f32[32,40,128]{2,1,0:T(8,128)} custom-call(s32[1]{0:T(128)} %bitcast.core_ref, bf16[1,128,8192]{2,1,0:T(8,128)(2,1)S(1)} %copy-done.1, bf16[8,288,512]{2,1,0:T(8,128)(2,1)S(1)} %bitcast.9, bf16[8,288,512]{2,1,0:T(8,128)(2,1)S(1)} %collective-permute-done.1.other_ref), custom_call_target="tpu_custom_call" | custom-call | flops 603979776 | bytes 8388608 | tf_op jit(solution)/shard_map/pallas_call | solution.py:151
  76.3 5.3 %all-to-all-start.1 = ((f32[32,40,128]{2,1,0:T(8,128)}), f32[32,40,128]{2,1,0:T(8,128)S(1)}, u32[]{:S(2)}, u32[]{:S(2)}) async-start(f32[32,40,128]{2,1,0:T(8,128)} %shard_map.94), calls=%async_computation.1 | async-start | bytes 1310720 | tf_op jit(solution)/shard_map/all_to_all | solution.py:612
  81.6 14.6 %shard_map.93 = (bf16[128,4096]{1,0:T(8,128)(2,1)}, bf16[32,128,128]{2,1,0:T(8,128)(2,1)}, bf16[128,4096]{1,0:T(8,128)(2,1)}, s32[4]{0:T(128)}) custom-call(s32[1]{0:T(128)} %bitcast.core_ref, bf16[32,272,128]{2,1,0:T(8,128)(2,1)} %copy-done.4, bf16[32,128,128]{2,1,0:T(8,128)(2,1)} %collective-permute-done.other_ref), custom_call_target="tpu_custom_call" | custom-call | flops 8589934592 | bytes 8388608 | tf_op jit(solution)/shard_map/pallas_call | solution.py:303
  96.2 0.0 all-to-all-done.1.refs_5_
  96.2 0.0 copy-start.5
  96.2 0.8 copy-done.5
  97.0 17.0 %shard_map.95 = f32[32,40,128]{2,1,0:T(8,128)} custom-call(s32[1]{0:T(128)} %bitcast.1.refs_0_, s32[4]{0:T(128)} %get-tuple-element.53.refs_1_, f32[32]{0:T(128)} %refs_2_.1, f32[32]{0:T(128)} %refs_3_.1, f32[256,4]{1,0:T(8,128)} %bitcast.10, f32[32,40,128]{2,1,0:T(8,128)} %copy-done.5, bf16[128,4096]{1,0:T(8,128)(2,1)} %get-tuple-element.56.refs_6_, ...), custom_call_target="tpu_custom_call" | custom-call | flops 8589934592 | bytes 8388608 | tf_op jit(solution)/shard_map/pallas_call | solution.py:516
  114.1 0.0 collective-permute-done.2.refs_10_
  114.1 0.0 collective-permute-done.3.refs_11_
  114.1 0.0 collective-permute-done.4.refs_12_
  114.1 0.0 collective-permute-done.5.refs_13_
  114.1 0.0 collective-permute-done.6.refs_14_
  114.1 7.5 %all-to-all-start.2 = ((f32[32,40,128]{2,1,0:T(8,128)}), f32[32,40,128]{2,1,0:T(8,128)S(1)}, u32[]{:S(2)}, u32[]{:S(2)}) async-start(f32[32,40,128]{2,1,0:T(8,128)} %shard_map.95), calls=%async_computation.2 | async-start | bytes 1310720 | tf_op jit(solution)/shard_map/all_to_all | solution.py:612
  121.6 0.1 collective-permute-start.7
  121.7 2.7 %collective-permute-start.8 = (bf16[128,1024]{1,0:T(8,128)(2,1)S(1)}, bf16[128,1024]{1,0:T(8,128)(2,1)S(1)}, u32[]{:S(2)}, u32[]{:S(2)}) collective-permute-start(bf16[128,1024]{1,0:T(8,128)(2,1)S(1)} %copy-done.7), channel_id=1, source_target_pairs={{0,7},{1,0},{2,1},{3,2},{4,3},{5,4},{6,5},{7,6},{8,15},{9,8},{10,9... | collective-permute-start | bytes 786440 | tf_op jit(solution)/shard_map/ppermute | solution.py:619
  124.4 10.2 %all-to-all-done.2.in_ref = f32[32,40,128]{2,1,0:T(8,128)S(1)} async-done(((f32[32,40,128]{2,1,0:T(8,128)}), f32[32,40,128]{2,1,0:T(8,128)S(1)}, u32[]{:S(2)}, u32[]{:S(2)}) %all-to-all-start.2) | async-done | bytes 655392 | tf_op jit(solution)/shard_map/all_to_all | solution.py:612
  134.6 0.0 collective-permute-done.7.refs_9_
  134.6 0.0 collective-permute-done.8.refs_15_
  134.6 0.3 collective-permute-start.10
  134.9 3.2 %collective-permute-start.11 = (bf16[288,128]{1,0:T(8,128)(2,1)S(1)}, bf16[288,128]{1,0:T(8,128)(2,1)S(1)}, u32[]{:S(2)}, u32[]{:S(2)}) collective-permute-start(bf16[288,128]{1,0:T(8,128)(2,1)S(1)} %shard_map.96.refs_0_), channel_id=1, source_target_pairs={{0,3},{1,4},{2,5},{3,6},{4,7},{5,0},{6,1},{7,2},{8,11},{9,12},{10,... | collective-permute-start | bytes 221192 | tf_op jit(solution)/shard_map/ppermute | solution.py:619
  138.1 1.0 collective-permute-start.12
  139.1 4.4 %collective-permute-start.13 = (bf16[288,128]{1,0:T(8,128)(2,1)S(1)}, bf16[288,128]{1,0:T(8,128)(2,1)S(1)}, u32[]{:S(2)}, u32[]{:S(2)}) collective-permute-start(bf16[288,128]{1,0:T(8,128)(2,1)S(1)} %shard_map.96.refs_0_), channel_id=1, source_target_pairs={{0,5},{1,6},{2,7},{3,0},{4,1},{5,2},{6,3},{7,4},{8,13},{9,14},{10,... | collective-permute-start | bytes 221192 | tf_op jit(solution)/shard_map/ppermute | solution.py:619
  143.5 0.1 collective-permute-start.14
  143.6 1.3 collective-permute-done.10.refs_2_
  145.0 0.0 collective-permute-start.15
  145.0 0.0 collective-permute-done.11.refs_3_
  145.0 2.8 %collective-permute-start.9 = (bf16[288,128]{1,0:T(8,128)(2,1)S(1)}, bf16[288,128]{1,0:T(8,128)(2,1)S(1)}, u32[]{:S(2)}, u32[]{:S(2)}) collective-permute-start(bf16[288,128]{1,0:T(8,128)(2,1)S(1)} %shard_map.96.refs_0_), channel_id=1, source_target_pairs={{0,1},{1,2},{2,3},{3,4},{4,5},{5,6},{6,7},{7,0},{8,9},{9,10},{10,1... | collective-permute-start | bytes 221192 | tf_op jit(solution)/shard_map/ppermute | solution.py:619
  147.8 1.6 collective-permute-done.12.refs_4_
  149.4 0.0 collective-permute-done.13.refs_5_
  149.5 3.5 %collective-permute-done.14.refs_6_ = bf16[288,128]{1,0:T(8,128)(2,1)S(1)} collective-permute-done((bf16[288,128]{1,0:T(8,128)(2,1)S(1)}, bf16[288,128]{1,0:T(8,128)(2,1)S(1)}, u32[]{:S(2)}, u32[]{:S(2)}) %collective-permute-start.14) | collective-permute-done | bytes 73760 | tf_op jit(solution)/shard_map/ppermute | solution.py:619
  152.9 1.1 collective-permute-done.15.refs_7_
  154.0 0.0 collective-permute-done.9.refs_1_
  154.0 1.8 shard_map.97
  155.8 1.1 collective-permute-start.16
  156.9 1.6 collective-permute-done.16
  158.5 0.1 add.7
  158.6 15.2 %all_to_all.26 = f32[16,72,128]{2,1,0:T(8,128)S(1)} all-to-all(f32[16,72,128]{2,1,0:T(8,128)S(1)} %add.7), channel_id=1, replica_groups={{0,16,32,48,64,80,96,112,128,144,160,176,192,208,224,240},{8,24,40,56,7..., dimensions={0} | all-to-all | bytes 1179648 | tf_op jit(solution)/shard_map/all_to_all | solution.py:612
  173.9 13.3 %all_to_all.27.own_ref = f32[16,72,128]{2,1,0:T(8,128)S(1)} all-to-all(f32[16,72,128]{2,1,0:T(8,128)S(1)} %broadcast_in_dim.18), channel_id=1, replica_groups={{0,16,32,48,64,80,96,112,128,144,160,176,192,208,224,240},{8,24,40,56,7..., dimensions={0} | all-to-all | bytes 1179648 | tf_op jit(solution)/shard_map/all_to_all | solution.py:612
  187.2 2.9 %collective-permute-start.17 = (f32[16,72,128]{2,1,0:T(8,128)S(1)}, f32[16,72,128]{2,1,0:T(8,128)S(1)}, u32[]{:S(2)}, u32[]{:S(2)}) collective-permute-start(f32[16,72,128]{2,1,0:T(8,128)S(1)} %all_to_all.27.own_ref), channel_id=1, source_target_pairs={{0,8},{8,0},{16,24},{24,16},{32,40},{40,32},{48,56},{56,48},{64,72... | collective-permute-start | bytes 1769480 | tf_op jit(solution)/shard_map/ppermute | solution.py:667
  190.2 1.6 collective-permute-done.17.other_ref
  191.8 1.1 shard_map.98
  (14 shorter events, 0.1 us)
Async XLA Ops:
  6.5 1.1 copy-start
  6.5 50.2 %all-gather.3.cloned.1.call-start = ((), (), s32[]{:S(2)}) async-start(), calls=%async_computation.5 | async-start | bytes 2654208 | tf_op jit(solution)/shard_map/all_gather | solution.py:637
  11.1 41.8 %copy-start.6 = (f32[4,256]{1,0:T(4,128)S(1)}, f32[4,256]{1,0:T(4,128)}, u32[]{:S(2)}) copy-start(f32[4,256]{1,0:T(4,128)} %param.15) | copy-start | bytes 12292
  50.0 1.4 copy-start.4
  51.4 20.5 %copy-start.1 = (bf16[1,128,8192]{2,1,0:T(8,128)(2,1)S(1)}, bf16[1,128,8192]{2,1,0:T(8,128)(2,1)}, u32[]{:S(2)}) copy-start(bf16[1,128,8192]{2,1,0:T(8,128)(2,1)} %hid_ref.3) | copy-start | bytes 6291460
  52.5 4.2 %collective-permute-start = (bf16[32,128,128]{2,1,0:T(8,128)(2,1)}, bf16[32,128,128]{2,1,0:T(8,128)(2,1)}, u32[]{:S(2)}, u32[]{:S(2)}) collective-permute-start(bf16[32,128,128]{2,1,0:T(8,128)(2,1)} %slice.4), channel_id=1, source_target_pairs={{0,8},{8,0},{16,24},{24,16},{32,40},{40,32},{48,56},{56,48},{64,72... | collective-permute-start | bytes 3145736 | tf_op jit(solution)/shard_map/ppermute | solution.py:639
  56.7 12.8 %collective-permute-start.1 = (bf16[8,288,512]{2,1,0:T(8,128)(2,1)}, bf16[8,288,512]{2,1,0:T(8,128)(2,1)S(1)}, u32[]{:S(2)}, u32[]{:S(2)}) collective-permute-start(bf16[8,288,512]{2,1,0:T(8,128)(2,1)} %bitcast.8), channel_id=1, source_target_pairs={{0,8},{8,0},{16,24},{24,16},{32,40},{40,32},{48,56},{56,48},{64,72... | collective-permute-start | bytes 7077896 | tf_op jit(solution)/shard_map/ppermute | solution.py:646
  56.9 57.1 %collective-permute-start.2 = (bf16[128,1024]{1,0:T(8,128)(2,1)}, bf16[128,1024]{1,0:T(8,128)(2,1)S(1)}, u32[]{:S(2)}, u32[]{:S(2)}) collective-permute-start(bf16[128,1024]{1,0:T(8,128)(2,1)} %get-tuple-element.60), channel_id=1, source_target_pairs={{0,2},{1,3},{2,4},{3,5},{4,6},{5,7},{6,0},{7,1},{8,10},{9,11},{10,... | collective-permute-start | bytes 786440 | tf_op jit(solution)/shard_map/ppermute | solution.py:619
  59.9 54.2 %collective-permute-start.3 = (bf16[128,1024]{1,0:T(8,128)(2,1)}, bf16[128,1024]{1,0:T(8,128)(2,1)S(1)}, u32[]{:S(2)}, u32[]{:S(2)}) collective-permute-start(bf16[128,1024]{1,0:T(8,128)(2,1)} %get-tuple-element.61), channel_id=1, source_target_pairs={{0,3},{1,4},{2,5},{3,6},{4,7},{5,0},{6,1},{7,2},{8,11},{9,12},{10,... | collective-permute-start | bytes 786440 | tf_op jit(solution)/shard_map/ppermute | solution.py:619
  64.6 49.5 %collective-permute-start.4 = (bf16[128,1024]{1,0:T(8,128)(2,1)}, bf16[128,1024]{1,0:T(8,128)(2,1)S(1)}, u32[]{:S(2)}, u32[]{:S(2)}) collective-permute-start(bf16[128,1024]{1,0:T(8,128)(2,1)} %get-tuple-element.62), channel_id=1, source_target_pairs={{0,4},{1,5},{2,6},{3,7},{4,0},{5,1},{6,2},{7,3},{8,12},{9,13},{10,... | collective-permute-start | bytes 786440 | tf_op jit(solution)/shard_map/ppermute | solution.py:619
  65.5 48.5 %collective-permute-start.5 = (bf16[128,1024]{1,0:T(8,128)(2,1)}, bf16[128,1024]{1,0:T(8,128)(2,1)}, u32[]{:S(2)}, u32[]{:S(2)}) collective-permute-start(bf16[128,1024]{1,0:T(8,128)(2,1)} %get-tuple-element.63), channel_id=1, source_target_pairs={{0,5},{1,6},{2,7},{3,0},{4,1},{5,2},{6,3},{7,4},{8,13},{9,14},{10,... | collective-permute-start | bytes 786440 | tf_op jit(solution)/shard_map/ppermute | solution.py:619
  69.5 44.6 %collective-permute-start.6 = (bf16[128,1024]{1,0:T(8,128)(2,1)}, bf16[128,1024]{1,0:T(8,128)(2,1)}, u32[]{:S(2)}, u32[]{:S(2)}) collective-permute-start(bf16[128,1024]{1,0:T(8,128)(2,1)} %get-tuple-element.64), channel_id=1, source_target_pairs={{0,6},{1,7},{2,0},{3,1},{4,2},{5,3},{6,4},{7,5},{8,14},{9,15},{10,... | collective-permute-start | bytes 786440 | tf_op jit(solution)/shard_map/ppermute | solution.py:619
  71.9 1.7 copy-start.2
  76.3 19.9 %all-to-all-start.1 = ((f32[32,40,128]{2,1,0:T(8,128)}), f32[32,40,128]{2,1,0:T(8,128)S(1)}, u32[]{:S(2)}, u32[]{:S(2)}) async-start(f32[32,40,128]{2,1,0:T(8,128)} %shard_map.94), calls=%async_computation.1 | async-start | bytes 1310720 | tf_op jit(solution)/shard_map/all_to_all | solution.py:612
  96.2 0.8 copy-start.5
  97.0 24.6 %copy-start.8 = (bf16[128,1024]{1,0:T(8,128)(2,1)S(1)}, bf16[128,1024]{1,0:T(8,128)(2,1)}, u32[]{:S(2)}) copy-start(bf16[128,1024]{1,0:T(8,128)(2,1)} %get-tuple-element.68) | copy-start | bytes 786436
  97.0 24.7 %copy-start.7 = (bf16[128,1024]{1,0:T(8,128)(2,1)S(1)}, bf16[128,1024]{1,0:T(8,128)(2,1)}, u32[]{:S(2)}) copy-start(bf16[128,1024]{1,0:T(8,128)(2,1)} %get-tuple-element.69) | copy-start | bytes 786436
  97.0 56.9 %copy-start.3 = (bf16[128,1024]{1,0:T(8,128)(2,1)S(1)}, bf16[128,1024]{1,0:T(8,128)(2,1)}, u32[]{:S(2)}) copy-start(bf16[128,1024]{1,0:T(8,128)(2,1)} %get-tuple-element.71.refs_8_) | copy-start | bytes 786436
  114.1 20.5 %all-to-all-start.2 = ((f32[32,40,128]{2,1,0:T(8,128)}), f32[32,40,128]{2,1,0:T(8,128)S(1)}, u32[]{:S(2)}, u32[]{:S(2)}) async-start(f32[32,40,128]{2,1,0:T(8,128)} %shard_map.95), calls=%async_computation.2 | async-start | bytes 1310720 | tf_op jit(solution)/shard_map/all_to_all | solution.py:612
  121.6 13.0 %collective-permute-start.7 = (bf16[128,1024]{1,0:T(8,128)(2,1)S(1)}, bf16[128,1024]{1,0:T(8,128)(2,1)S(1)}, u32[]{:S(2)}, u32[]{:S(2)}) collective-permute-start(bf16[128,1024]{1,0:T(8,128)(2,1)S(1)} %copy-done.8), channel_id=1, source_target_pairs={{0,1},{1,2},{2,3},{3,4},{4,5},{5,6},{6,7},{7,0},{8,9},{9,10},{10,1... | collective-permute-start | bytes 786440 | tf_op jit(solution)/shard_map/ppermute | solution.py:619
  121.7 12.9 %collective-permute-start.8 = (bf16[128,1024]{1,0:T(8,128)(2,1)S(1)}, bf16[128,1024]{1,0:T(8,128)(2,1)S(1)}, u32[]{:S(2)}, u32[]{:S(2)}) collective-permute-start(bf16[128,1024]{1,0:T(8,128)(2,1)S(1)} %copy-done.7), channel_id=1, source_target_pairs={{0,7},{1,0},{2,1},{3,2},{4,3},{5,4},{6,5},{7,6},{8,15},{9,8},{10,9... | collective-permute-start | bytes 786440 | tf_op jit(solution)/shard_map/ppermute | solution.py:619
  134.6 10.4 %collective-permute-start.10 = (bf16[288,128]{1,0:T(8,128)(2,1)S(1)}, bf16[288,128]{1,0:T(8,128)(2,1)S(1)}, u32[]{:S(2)}, u32[]{:S(2)}) collective-permute-start(bf16[288,128]{1,0:T(8,128)(2,1)S(1)} %shard_map.96.refs_0_), channel_id=1, source_target_pairs={{0,2},{1,3},{2,4},{3,5},{4,6},{5,7},{6,0},{7,1},{8,10},{9,11},{10,... | collective-permute-start | bytes 221192 | tf_op jit(solution)/shard_map/ppermute | solution.py:619
  134.9 10.0 %collective-permute-start.11 = (bf16[288,128]{1,0:T(8,128)(2,1)S(1)}, bf16[288,128]{1,0:T(8,128)(2,1)S(1)}, u32[]{:S(2)}, u32[]{:S(2)}) collective-permute-start(bf16[288,128]{1,0:T(8,128)(2,1)S(1)} %shard_map.96.refs_0_), channel_id=1, source_target_pairs={{0,3},{1,4},{2,5},{3,6},{4,7},{5,0},{6,1},{7,2},{8,11},{9,12},{10,... | collective-permute-start | bytes 221192 | tf_op jit(solution)/shard_map/ppermute | solution.py:619
  138.1 11.3 %collective-permute-start.12 = (bf16[288,128]{1,0:T(8,128)(2,1)S(1)}, bf16[288,128]{1,0:T(8,128)(2,1)S(1)}, u32[]{:S(2)}, u32[]{:S(2)}) collective-permute-start(bf16[288,128]{1,0:T(8,128)(2,1)S(1)} %shard_map.96.refs_0_), channel_id=1, source_target_pairs={{0,4},{1,5},{2,6},{3,7},{4,0},{5,1},{6,2},{7,3},{8,12},{9,13},{10,... | collective-permute-start | bytes 221192 | tf_op jit(solution)/shard_map/ppermute | solution.py:619
  139.1 10.3 %collective-permute-start.13 = (bf16[288,128]{1,0:T(8,128)(2,1)S(1)}, bf16[288,128]{1,0:T(8,128)(2,1)S(1)}, u32[]{:S(2)}, u32[]{:S(2)}) collective-permute-start(bf16[288,128]{1,0:T(8,128)(2,1)S(1)} %shard_map.96.refs_0_), channel_id=1, source_target_pairs={{0,5},{1,6},{2,7},{3,0},{4,1},{5,2},{6,3},{7,4},{8,13},{9,14},{10,... | collective-permute-start | bytes 221192 | tf_op jit(solution)/shard_map/ppermute | solution.py:619
  143.5 9.4 %collective-permute-start.14 = (bf16[288,128]{1,0:T(8,128)(2,1)S(1)}, bf16[288,128]{1,0:T(8,128)(2,1)S(1)}, u32[]{:S(2)}, u32[]{:S(2)}) collective-permute-start(bf16[288,128]{1,0:T(8,128)(2,1)S(1)} %shard_map.96.refs_0_), channel_id=1, source_target_pairs={{0,6},{1,7},{2,0},{3,1},{4,2},{5,3},{6,4},{7,5},{8,14},{9,15},{10,... | collective-permute-start | bytes 221192 | tf_op jit(solution)/shard_map/ppermute | solution.py:619
  145.0 9.0 %collective-permute-start.15 = (bf16[288,128]{1,0:T(8,128)(2,1)S(1)}, bf16[288,128]{1,0:T(8,128)(2,1)S(1)}, u32[]{:S(2)}, u32[]{:S(2)}) collective-permute-start(bf16[288,128]{1,0:T(8,128)(2,1)S(1)} %shard_map.96.refs_0_), channel_id=1, source_target_pairs={{0,7},{1,0},{2,1},{3,2},{4,3},{5,4},{6,5},{7,6},{8,15},{9,8},{10,9... | collective-permute-start | bytes 221192 | tf_op jit(solution)/shard_map/ppermute | solution.py:619
  145.0 9.0 %collective-permute-start.9 = (bf16[288,128]{1,0:T(8,128)(2,1)S(1)}, bf16[288,128]{1,0:T(8,128)(2,1)S(1)}, u32[]{:S(2)}, u32[]{:S(2)}) collective-permute-start(bf16[288,128]{1,0:T(8,128)(2,1)S(1)} %shard_map.96.refs_0_), channel_id=1, source_target_pairs={{0,1},{1,2},{2,3},{3,4},{4,5},{5,6},{6,7},{7,0},{8,9},{9,10},{10,1... | collective-permute-start | bytes 221192 | tf_op jit(solution)/shard_map/ppermute | solution.py:619
  155.8 2.7 %collective-permute-start.16 = (f32[16,72,128]{2,1,0:T(8,128)S(1)}, f32[16,72,128]{2,1,0:T(8,128)S(1)}, u32[]{:S(2)}, u32[]{:S(2)}) collective-permute-start(f32[16,72,128]{2,1,0:T(8,128)S(1)} %get-tuple-element.80), channel_id=1, source_target_pairs={{0,8},{8,0},{16,24},{24,16},{32,40},{40,32},{48,56},{56,48},{64,72... | collective-permute-start | bytes 1769480 | tf_op jit(solution)/shard_map/ppermute | solution.py:663
  187.2 4.6 %collective-permute-start.17 = (f32[16,72,128]{2,1,0:T(8,128)S(1)}, f32[16,72,128]{2,1,0:T(8,128)S(1)}, u32[]{:S(2)}, u32[]{:S(2)}) collective-permute-start(f32[16,72,128]{2,1,0:T(8,128)S(1)} %all_to_all.27.own_ref), channel_id=1, source_target_pairs={{0,8},{8,0},{16,24},{24,16},{32,40},{40,32},{48,56},{56,48},{64,72... | collective-permute-start | bytes 1769480 | tf_op jit(solution)/shard_map/ppermute | solution.py:667
Sparse Core Ops, SparseCore 0:
  9.1 42.4 all-gather.2

commit v5 on v4

--- a/solution.py
+++ b/solution.py
@@ -97,23 +97,32 @@
     )(q, k, v, docs)
 
 
-def pack_hidden_kernel(part_ref, hid_ref, *out_refs):
-    width = out_refs[0].shape[1]
-    for k, ref in enumerate(out_refs):
-        block = lax.rem(part_ref[0] + k, PARTS)
-        ref[...] = hid_ref[0, :, pl.ds(pl.multiple_of(block * width, width), width)]
-
-
-def pack_hidden(part, hidden):
-    block = jax.ShapeDtypeStruct((ROWS, D // PARTS), BF16)
+def pack_hidden_kernel(core_ref, part_ref, hid_ref, stay_ref, across_ref, mine_ref, give_ref):
+    width = stay_ref.shape[1]
+    sign = 1 - 2 * core_ref[0]
+
+    def block(distance):
+        at = lax.rem(part_ref[0] + distance + PARTS, PARTS)
+        return hid_ref[0, :, pl.ds(pl.multiple_of(at * width, width), width)]
+
+    stay_ref[...] = block(0)
+    across_ref[...] = block(PARTS // 2)
+    for k in range(1, PARTS // 2):
+        mine_ref[k - 1] = block(sign * k)
+        give_ref[k - 1] = block(-sign * k)
+
+
+def pack_hidden(core, part, hidden):
+    one = jax.ShapeDtypeStruct((ROWS, D // PARTS), BF16)
+    three = jax.ShapeDtypeStruct((PARTS // 2 - 1, ROWS, D // PARTS), BF16)
     return pl.pallas_call(
         pack_hidden_kernel,
-        out_shape=(block,) * PARTS,
-        in_specs=[SMEM, VMEM],
-        out_specs=(VMEM,) * PARTS,
+        out_shape=(one, one, three, three),
+        in_specs=[SMEM, SMEM, VMEM],
+        out_specs=(VMEM,) * 4,
         compiler_params=params(60),
         cost_estimate=pl.CostEstimate(flops=0, bytes_accessed=4 << 20, transcendentals=0),
-    )(part, hidden)
+    )(core, part, hidden)
 
 
 def project_kernel(core_ref, hid_ref, own_ref, other_ref, out_ref, acc_ref):
@@ -564,12 +573,22 @@
 
 
 def product_kernel(core_ref, *refs):
-    grads, blocks, (keep_ref, send_ref) = refs[:PARTS], refs[PARTS : 2 * PARTS], refs[2 * PARTS :]
-    left = jnp.concatenate([grad[...] for grad in grads], 1)
-    half = blocks[0].shape[1] // 2
+    count = PARTS // 2 + 1
+    grads, blocks, (keep_ref, send_ref) = refs[:count], refs[count : 2 * count], refs[2 * count :]
+    left = []
+    for grad in grads:
+        left += [grad[...]] if len(grad.shape) == 2 else [grad[0], grad[1]]
+    left = jnp.concatenate(left, 1)
+    half = blocks[0].shape[-1] // 2
     for ref, core in ((send_ref, 1 - core_ref[0]), (keep_ref, core_ref[0])):
         lanes = pl.ds(pl.multiple_of(core * half, half), half)
-        part = mm(left, jnp.concatenate([block[:, lanes] for block in blocks], 0))
+        right = []
+        for block in blocks:
+            if len(block.shape) == 2:
+                right.append(block[:, lanes])
+            else:
+                right += [block[0, :, lanes], block[1, :, lanes]]
+        part = mm(left, jnp.concatenate(right, 0))
         for r in range(4):
             for q in range(4):
                 ref[4 * r + q] = part[r * 72 : (r + 1) * 72, q * 128 : (q + 1) * 128]
@@ -580,7 +599,7 @@
     return pl.pallas_call(
         product_kernel,
         out_shape=(shape, shape),
-        in_specs=[SMEM] + [VMEM] * (2 * PARTS),
+        in_specs=[SMEM] + [VMEM] * (PARTS + 2),
         out_specs=(VMEM, VMEM),
         compiler_params=params(24),
         cost_estimate=pl.CostEstimate(
@@ -612,12 +631,13 @@
     return lax.all_to_all(x, axis, 0, 0, tiled=True, axis_index_groups=groups)
 
 
-def spread_hidden(blocks, distances):
-    moved = []
-    for k in distances:
-        route = [(i, (i + k) % PARTS) for i in range(PARTS)]
-        moved.append(lax.ppermute(blocks[k], "dp", route))
-    return moved
+def both_ways(block, distance):
+    route = []
+    for s in range(lax.axis_size("seq")):
+        sign = 1 - 2 * (s % 2)
+        for z in range(PARTS):
+            route.append((s * PARTS + z, s * PARTS + (z + sign * distance) % PARTS))
+    return lax.ppermute(block, ("seq", "dp"), route)
 
 
 def local(hidden, queries, keys, values, docs, w_proj, conv_weight, dt_bias, decay_rate):
@@ -636,29 +656,36 @@
     own_w = lax.dynamic_slice_in_dim(turned_w, core[0] * half, half, 1)
     own_w = lax.all_gather(own_w, "dp", axis=0)
     own = swap_all(pack_teacher(queries, keys, values, docs), "seq")
+    stay, across, mine, give = pack_hidden(core, part, hidden)
+    taken = lax.ppermute(give, "seq", partner)
+    outgoing = [across] + [jnp.stack([mine[k], taken[k]]) for k in range(PARTS // 2 - 1)]
+    own, outgoing, taps = lax.optimization_barrier((own, outgoing, conv_weight.T))
     other = lax.ppermute(own[:, ROWS : 2 * ROWS, :], "seq", partner)
-    own, other, own_w, taps, blocks = lax.optimization_barrier(
-        (own, other, own_w, conv_weight.T, pack_hidden(part, hidden))
-    )
-    order, last = (4, 5, 3, 6, 2), (1, 7)
-    moved = {0: blocks[0]} | dict(zip(order, spread_hidden(blocks, order)))
-    waiting = {k: blocks[k] for k in last}
+    own, other, own_w, outgoing = lax.optimization_barrier((own, other, own_w, outgoing))
     other_w = lax.ppermute(own_w, "seq", partner)
+    far = PARTS // 2
+    arrived = {far: both_ways(outgoing[0], far)}
+    for k in (3, 2):
+        arrived[k] = both_ways(outgoing[k], k)
+    late = {k: outgoing[k] for k in (1,)}
     proj = swap_all(project(core, hidden, own_w, other_w), "seq")
     teach, v, vt, counts = attend(core, own, other)
     grads = student(
         head[None], counts, dt_bias, decay_rate, taps, proj, teach, v, vt, weight
     )
-    grads, moved, waiting = lax.optimization_barrier((grads, moved, waiting))
-    rounded, nearby = lax.optimization_barrier(
-        (combine(swap_all(grads, "seq")), spread_hidden(waiting, last))
-    )
-    moved.update(zip(last, nearby))
-    far_first = (4, 5, 3, 6, 2, 7, 1)
-    copies = {k: rounded for k in far_first}
-    spread_grads = {0: rounded} | dict(zip(far_first, spread_hidden(copies, far_first)))
+    grads, arrived, late = lax.optimization_barrier((grads, arrived, late))
+    late = {k: both_ways(late[k], k) for k in late}
+    rounded, late = lax.optimization_barrier((combine(swap_all(grads, "seq")), late))
+    arrived.update(late)
+    spread_grads = {far: both_ways(rounded, far)}
+    pair = jnp.stack([rounded, lax.ppermute(rounded, "seq", partner)])
+    order = (far, 3, 2, 1)
+    for k in order[1:]:
+        spread_grads[k] = both_ways(pair, k)
     keep, send = product(
-        core, [spread_grads[k] for k in range(PARTS)], [moved[k] for k in range(PARTS)]
+        core,
+        [rounded] + [spread_grads[k] for k in order],
+        [stay] + [arrived[k] for k in order],
     )
     partial = keep + lax.ppermute(send, "seq", partner)
     total = jnp.sum(swap_all(partial, "seq", same_core), axis=0)

time: 200 us -> 192 us (0.960)
  blocking collectives: 67.4 us -> 27.7 us
  waiting for transfers between devices: 21 us -> 45.7 us
  Pallas kernels: 43 us -> 45.2 us
  other arithmetic: 0.1 us -> 2.11 us
  starting transfers between devices: 47 us -> 49 us
    all_to_all x3 -> x2, blocking collectives: 67.4 us -> 27.7 us  [swap_all(): return lax.all_to_all(x, axis, 0, 0, tiled=True, axis_index_groups=groups)]
    all_to_all x2 -> x3, waiting for transfers between devices: 10.2 us -> 35 us  [swap_all(): return lax.all_to_all(x, axis, 0, 0, tiled=True, axis_index_groups=groups)]
    ppermute x14 -> x10, starting transfers between devices: 29.5 us -> 18.9 us  [the longest x8 18.5 us: both_ways(): return lax.ppermute(block, ('seq', 'dp'), route)]
    all_to_all x2 -> x3, starting transfers between devices: 12.9 us -> 20.2 us  [swap_all(): return lax.all_to_all(x, axis, 0, 0, tiled=True, axis_index_groups=groups)]
    ppermute x1, starting transfers between devices: 1.11 us -> 5.26 us  [local(): partial = keep + lax.ppermute(send, 'seq', partner)]
    ppermute x14 -> x10, waiting for transfers between devices: 7.54 us -> 4.97 us  [the longest x8 3.48 us: both_ways(): return lax.ppermute(block, ('seq', 'dp'), route)]
    ppermute x1, waiting for transfers between devices: 0.01 us -> 2.42 us  [local(): other = lax.ppermute(own[:, ROWS:2 * ROWS, :], 'seq', partner)]
    pallas_call x1, Pallas kernels: 14.6 us -> 16.8 us  [attend(): pl.pallas_call(attend_kernel, out_shape=(jax.ShapeDtypeStruct((DIM, SEQ),...]
  transfers between devices with their start and end apart: 21 -> 18, of which waited for: 7 -> 8; matrix products, arithmetic and copies ran while one was open for 1% -> 3% of each run, Pallas kernels for 20% -> 22%
where the time goes in v5:
time: 192 us; the launch traced here: 191 us
  starting transfers between devices  49 us (26%)
  waiting for transfers between devices  45.7 us (24%)
  Pallas kernels  45.2 us (24%)
  blocking collectives  27.7 us (14%)
  between operations  13.6 us (7%)
  local copies, waits for them, and re-layouts  7.67 us (4%)
  other arithmetic  2.11 us (1%)
    all_to_all x3, waiting for transfers between devices, swap_all(): return lax.all_to_all(x, axis, 0, 0, tiled=True, axis_index_groups=groups)  35 us
    all_to_all x2, blocking collectives, swap_all(): return lax.all_to_all(x, axis, 0, 0, tiled=True, axis_index_groups=groups)  27.7 us
    all_to_all x3, starting transfers between devices, swap_all(): return lax.all_to_all(x, axis, 0, 0, tiled=True, axis_index_groups=groups)  20.2 us
    ppermute x8, starting transfers between devices, both_ways(): return lax.ppermute(block, ('seq', 'dp'), route)  18.5 us
    pallas_call x1, Pallas kernels, student(): pl.pallas_call(lambda *refs: student_kernel(*refs, weight=weight), out_sh...  17 us
    pallas_call x1, Pallas kernels, attend(): pl.pallas_call(attend_kernel, out_shape=(jax.ShapeDtypeStruct((DIM, SEQ),...  16.8 us
    ppermute x1, starting transfers between devices, local(): partial = keep + lax.ppermute(send, 'seq', partner)  5.26 us
    unnamed x15, local copies, waits for them, and re-layouts  4.35 us
  transfers between devices with their start and end apart: 18, of which 8 were waited for; matrix products, arithmetic and copies ran while one was open for 3% of the time, Pallas kernels for 22%

profile of v5, /device:TPU:1, one launch (start us, length us, event | category | flops | bytes accessed | tf_op | source)
XLA Modules:
  0.0 190.9 jit_solution(867663153629581925)
XLA Ops:
  6.5 0.0 copy-start
  6.5 0.0 all-gather.3.cloned.1.call-start
  6.5 1.1 copy-done
  7.6 0.8 dynamic-slice_bitcast_fusion
  8.4 0.0 all-gather.3.cloned.1.call-update
  8.4 2.7 %shard_map.91 = bf16[32,272,128]{2,1,0:T(8,128)(2,1)} custom-call(bf16[1,128,4096]{2,1,0:T(8,128)(2,1)} %q_ref.1, bf16[1,128,1024]{2,1,0:T(8,128)(2,1)} %k_ref.1, bf16[1,128,1024]{2,1,0:T(8,128)(2,1)} %v_ref.1, s32[1,128]{1,0:T(1,128)} %doc_ref.1), custom_call_target="tpu_custom_call" | custom-call | bytes 4194304 | tf_op jit(solution)/shard_map/pallas_call | solution.py:84
  11.1 0.0 copy-start.6
  11.1 8.8 %all-to-all-start = ((bf16[32,272,128]{2,1,0:T(8,128)(2,1)}), bf16[32,272,128]{2,1,0:T(8,128)(2,1)}, u32[]{:S(2)}, u32[]{:S(2)}) async-start(bf16[32,272,128]{2,1,0:T(8,128)(2,1)} %shard_map.91), calls=%async_computation | async-start | bytes 4456448 | tf_op jit(solution)/shard_map/all_to_all | solution.py:631
  19.9 3.0 %shard_map.92 = (bf16[128,1024]{1,0:T(8,128)(2,1)}, bf16[128,1024]{1,0:T(8,128)(2,1)}, bf16[3,128,1024]{2,1,0:T(8,128)(2,1)}, bf16[3,128,1024]{2,1,0:T(8,128)(2,1)}) custom-call(s32[1]{0:T(128)} %bitcast.core_ref, s32[1]{0:T(128)} %bitcast.2.part_ref, bf16[1,128,8192]{2,1,0:T(8,128)(2,1)} %hid_ref.3), custom_call_target="tpu_custom_call" | custom-call | bytes 4194304 | tf_op jit(solution)/shard_map/pallas_call | solution.py:118
  22.9 0.3 collective-permute-start
  23.2 0.0 copy-done.6
  23.2 0.8 copy.10
  24.0 1.2 fusion
  25.2 0.2 collective-permute-done
  25.4 0.1 fusion.1
  25.5 0.8 pad_maximum_fusion.2
  26.3 0.0 copy-start.1
  26.3 1.2 pad_maximum_fusion
  27.5 22.2 %all-to-all-done.own_ref = bf16[32,272,128]{2,1,0:T(8,128)(2,1)} async-done(((bf16[32,272,128]{2,1,0:T(8,128)(2,1)}), bf16[32,272,128]{2,1,0:T(8,128)(2,1)}, u32[]{:S(2)}, u32[]{:S(2)}) %all-to-all-start) | async-done | bytes 2228256 | tf_op jit(solution)/shard_map/all_to_all | solution.py:631
  49.6 1.3 slice.27
  50.9 1.0 collective-permute-start.1
  52.0 2.4 %collective-permute-done.1.other_ref = bf16[32,128,128]{2,1,0:T(8,128)(2,1)} collective-permute-done((bf16[32,128,128]{2,1,0:T(8,128)(2,1)S(1)}, bf16[32,128,128]{2,1,0:T(8,128)(2,1)}, u32[]{:S(2)}, u32[]{:S(2)}) %collective-permute-start.1) | collective-permute-done | bytes 1048608 | tf_op jit(solution)/shard_map/ppermute | solution.py:663
  54.4 0.7 collective-permute-start.2
  55.1 5.6 %collective-permute-start.3 = (bf16[2,128,1024]{2,1,0:T(8,128)(2,1)}, bf16[2,128,1024]{2,1,0:T(8,128)(2,1)S(1)}, u32[]{:S(2)}, u32[]{:S(2)}) collective-permute-start(bf16[2,128,1024]{2,1,0:T(8,128)(2,1)} %get-tuple-element.51), channel_id=1, source_target_pairs={{0,2},{1,3},{2,4},{3,5},{4,6},{5,7},{6,0},{7,1},{8,14},{9,15},{10,... | collective-permute-start | bytes 1572872 | tf_op jit(solution)/shard_map/ppermute | solution.py:640
  60.8 0.7 collective-permute-start.4
  61.5 4.2 %collective-permute-start.5 = (bf16[128,1024]{1,0:T(8,128)(2,1)}, bf16[128,1024]{1,0:T(8,128)(2,1)S(1)}, u32[]{:S(2)}, u32[]{:S(2)}) collective-permute-start(bf16[128,1024]{1,0:T(8,128)(2,1)} %get-tuple-element.53), channel_id=1, source_target_pairs={{0,4},{1,5},{2,6},{3,7},{4,0},{5,1},{6,2},{7,3},{8,12},{9,13},{10,... | collective-permute-start | bytes 786440 | tf_op jit(solution)/shard_map/ppermute | solution.py:640
  65.7 0.0 collective-permute-done.2.other_ref
  65.7 0.0 copy-done.1
  65.7 1.7 copy-done.2
  67.4 2.6 %shard_map.94 = f32[32,40,128]{2,1,0:T(8,128)} custom-call(s32[1]{0:T(128)} %bitcast.core_ref, bf16[1,128,8192]{2,1,0:T(8,128)(2,1)S(1)} %copy-done.1, bf16[8,288,512]{2,1,0:T(8,128)(2,1)S(1)} %bitcast.11, bf16[8,288,512]{2,1,0:T(8,128)(2,1)S(1)} %collective-permute-done.2.other_ref), custom_call_target="tpu_custom_call" | custom-call | flops 603979776 | bytes 8388608 | tf_op jit(solution)/shard_map/pallas_call | solution.py:160
  70.0 3.9 %all-to-all-start.1 = ((f32[32,40,128]{2,1,0:T(8,128)}), f32[32,40,128]{2,1,0:T(8,128)S(1)}, u32[]{:S(2)}, u32[]{:S(2)}) async-start(f32[32,40,128]{2,1,0:T(8,128)} %shard_map.94), calls=%async_computation.1 | async-start | bytes 1310720 | tf_op jit(solution)/shard_map/all_to_all | solution.py:631
  73.9 16.8 %shard_map.93 = (bf16[128,4096]{1,0:T(8,128)(2,1)}, bf16[32,128,128]{2,1,0:T(8,128)(2,1)}, bf16[128,4096]{1,0:T(8,128)(2,1)}, s32[4]{0:T(128)}) custom-call(s32[1]{0:T(128)} %bitcast.core_ref, bf16[32,272,128]{2,1,0:T(8,128)(2,1)} %all-to-all-done.own_ref, bf16[32,128,128]{2,1,0:T(8,128)(2,1)} %collective-permute-done.1.other_ref), custom_call_target="tpu_custom_call" | custom-call | flops 8589934592 | bytes 8388608 | tf_op jit(solution)/shard_map/pallas_call | solution.py:312
  90.8 0.0 all-to-all-done.1.refs_5_
  90.8 0.0 copy-start.4
  90.8 0.8 copy-done.4
  91.6 17.0 %shard_map.95 = f32[32,40,128]{2,1,0:T(8,128)} custom-call(s32[1]{0:T(128)} %bitcast.1.refs_0_, s32[4]{0:T(128)} %get-tuple-element.45.refs_1_, f32[32]{0:T(128)} %refs_2_.1, f32[32]{0:T(128)} %refs_3_.1, f32[256,4]{1,0:T(8,128)} %bitcast.13, f32[32,40,128]{2,1,0:T(8,128)} %copy-done.4, bf16[128,4096]{1,0:T(8,128)(2,1)} %get-tuple-element.48.refs_6_, ...), custom_call_target="tpu_custom_call" | custom-call | flops 8589934592 | bytes 8388608 | tf_op jit(solution)/shard_map/pallas_call | solution.py:525
  108.6 0.0 collective-permute-done.5.refs_6_
  108.6 0.0 collective-permute-done.3.refs_8_
  108.7 0.0 collective-permute-done.4.refs_7_
  108.7 7.5 %all-to-all-start.2 = ((f32[32,40,128]{2,1,0:T(8,128)}), f32[32,40,128]{2,1,0:T(8,128)S(1)}, u32[]{:S(2)}, u32[]{:S(2)}) async-start(f32[32,40,128]{2,1,0:T(8,128)} %shard_map.95), calls=%async_computation.2 | async-start | bytes 1310720 | tf_op jit(solution)/shard_map/all_to_all | solution.py:631
  116.2 0.0 copy-done.5
  116.2 0.1 collective-permute-start.6
  116.3 12.8 %all-to-all-done.2.in_ref = f32[32,40,128]{2,1,0:T(8,128)S(1)} async-done(((f32[32,40,128]{2,1,0:T(8,128)}), f32[32,40,128]{2,1,0:T(8,128)S(1)}, u32[]{:S(2)}, u32[]{:S(2)}) %all-to-all-start.2) | async-done | bytes 655392 | tf_op jit(solution)/shard_map/all_to_all | solution.py:631
  129.2 0.0 collective-permute-done.6.refs_9_
  129.2 0.1 collective-permute-start.8
  129.3 1.3 collective-permute-done.8
  130.6 2.2 %collective-permute-start.10 = (bf16[2,288,128]{2,1,0:T(8,128)(2,1)S(1)}, bf16[2,288,128]{2,1,0:T(8,128)(2,1)S(1)}, u32[]{:S(2)}, u32[]{:S(2)}) collective-permute-start(bf16[2,288,128]{2,1,0:T(8,128)(2,1)S(1)} %pad_maximum_fusion.3), channel_id=1, source_target_pairs={{0,2},{1,3},{2,4},{3,5},{4,6},{5,7},{6,0},{7,1},{8,14},{9,15},{10,... | collective-permute-start | bytes 442376 | tf_op jit(solution)/shard_map/ppermute | solution.py:640
  132.8 0.7 collective-permute-start.11
  133.5 0.0 collective-permute-start.9
  133.5 4.9 %collective-permute-start.7 = (bf16[288,128]{1,0:T(8,128)(2,1)S(1)}, bf16[288,128]{1,0:T(8,128)(2,1)S(1)}, u32[]{:S(2)}, u32[]{:S(2)}) collective-permute-start(bf16[288,128]{1,0:T(8,128)(2,1)S(1)} %shard_map.96.refs_0_), channel_id=1, source_target_pairs={{0,4},{1,5},{2,6},{3,7},{4,0},{5,1},{6,2},{7,3},{8,12},{9,13},{10,... | collective-permute-start | bytes 221192 | tf_op jit(solution)/shard_map/ppermute | solution.py:640
  138.4 3.5 %collective-permute-done.7.refs_1_ = bf16[288,128]{1,0:T(8,128)(2,1)S(1)} collective-permute-done((bf16[288,128]{1,0:T(8,128)(2,1)S(1)}, bf16[288,128]{1,0:T(8,128)(2,1)S(1)}, u32[]{:S(2)}, u32[]{:S(2)}) %collective-permute-start.7) | collective-permute-done | bytes 73760 | tf_op jit(solution)/shard_map/ppermute | solution.py:640
  141.9 0.0 collective-permute-done.10.refs_3_
  141.9 0.0 collective-permute-done.11.refs_4_
  141.9 0.0 collective-permute-done.9.refs_2_
  141.9 0.0 copy-done.3
  141.9 1.8 shard_map.97
  143.8 5.3 %collective-permute-start.12 = (f32[16,72,128]{2,1,0:T(8,128)S(1)}, f32[16,72,128]{2,1,0:T(8,128)S(1)}, u32[]{:S(2)}, u32[]{:S(2)}) collective-permute-start(f32[16,72,128]{2,1,0:T(8,128)S(1)} %get-tuple-element.64), channel_id=1, source_target_pairs={{0,8},{8,0},{16,24},{24,16},{32,40},{40,32},{48,56},{56,48},{64,72... | collective-permute-start | bytes 1769480 | tf_op jit(solution)/shard_map/ppermute | solution.py:690
  149.0 1.6 collective-permute-done.12
  150.6 0.1 add.7
  150.7 14.2 %all_to_all.25 = f32[16,72,128]{2,1,0:T(8,128)S(1)} all-to-all(f32[16,72,128]{2,1,0:T(8,128)S(1)} %add.7), channel_id=1, replica_groups={{0,16,32,48,64,80,96,112,128,144,160,176,192,208,224,240},{8,24,40,56,7..., dimensions={0} | all-to-all | bytes 1179648 | tf_op jit(solution)/shard_map/all_to_all | solution.py:631
  164.9 13.6 %all_to_all.26.own_ref = f32[16,72,128]{2,1,0:T(8,128)S(1)} all-to-all(f32[16,72,128]{2,1,0:T(8,128)S(1)} %broadcast_in_dim.18), channel_id=1, replica_groups={{0,16,32,48,64,80,96,112,128,144,160,176,192,208,224,240},{8,24,40,56,7..., dimensions={0} | all-to-all | bytes 1179648 | tf_op jit(solution)/shard_map/all_to_all | solution.py:631
  178.5 2.8 %collective-permute-start.13 = (f32[16,72,128]{2,1,0:T(8,128)S(1)}, f32[16,72,128]{2,1,0:T(8,128)S(1)}, u32[]{:S(2)}, u32[]{:S(2)}) collective-permute-start(f32[16,72,128]{2,1,0:T(8,128)S(1)} %all_to_all.26.own_ref), channel_id=1, source_target_pairs={{0,8},{8,0},{16,24},{24,16},{32,40},{40,32},{48,56},{56,48},{64,72... | collective-permute-start | bytes 1769480 | tf_op jit(solution)/shard_map/ppermute | solution.py:694
  181.3 1.6 collective-permute-done.13.other_ref
  183.0 1.1 shard_map.98
  (8 shorter events, 0.1 us)
Async XLA Ops:
  6.5 1.1 copy-start
  6.5 47.8 %all-gather.3.cloned.1.call-start = ((), (), s32[]{:S(2)}) async-start(), calls=%async_computation.5 | async-start | bytes 2654208 | tf_op jit(solution)/shard_map/all_gather | solution.py:657
  11.1 12.1 %copy-start.6 = (f32[4,256]{1,0:T(4,128)S(1)}, f32[4,256]{1,0:T(4,128)}, u32[]{:S(2)}) copy-start(f32[4,256]{1,0:T(4,128)} %param.15) | copy-start | bytes 12292
  11.1 38.5 %all-to-all-start = ((bf16[32,272,128]{2,1,0:T(8,128)(2,1)}), bf16[32,272,128]{2,1,0:T(8,128)(2,1)}, u32[]{:S(2)}, u32[]{:S(2)}) async-start(bf16[32,272,128]{2,1,0:T(8,128)(2,1)} %shard_map.91), calls=%async_computation | async-start | bytes 4456448 | tf_op jit(solution)/shard_map/all_to_all | solution.py:631
  22.9 2.5 %collective-permute-start = (bf16[3,128,1024]{2,1,0:T(8,128)(2,1)}, bf16[3,128,1024]{2,1,0:T(8,128)(2,1)S(1)}, u32[]{:S(2)}, u32[]{:S(2)}) collective-permute-start(bf16[3,128,1024]{2,1,0:T(8,128)(2,1)} %get-tuple-element.37), channel_id=1, source_target_pairs={{0,8},{8,0},{16,24},{24,16},{32,40},{40,32},{48,56},{56,48},{64,72... | collective-permute-start | bytes 2359304 | tf_op jit(solution)/shard_map/ppermute | solution.py:660
  26.3 39.4 %copy-start.1 = (bf16[1,128,8192]{2,1,0:T(8,128)(2,1)S(1)}, bf16[1,128,8192]{2,1,0:T(8,128)(2,1)}, u32[]{:S(2)}) copy-start(bf16[1,128,8192]{2,1,0:T(8,128)(2,1)} %hid_ref.3) | copy-start | bytes 6291460
  50.9 3.4 %collective-permute-start.1 = (bf16[32,128,128]{2,1,0:T(8,128)(2,1)S(1)}, bf16[32,128,128]{2,1,0:T(8,128)(2,1)}, u32[]{:S(2)}, u32[]{:S(2)}) collective-permute-start(bf16[32,128,128]{2,1,0:T(8,128)(2,1)S(1)} %slice.27), channel_id=1, source_target_pairs={{0,8},{8,0},{16,24},{24,16},{32,40},{40,32},{48,56},{56,48},{64,72... | collective-permute-start | bytes 3145736 | tf_op jit(solution)/shard_map/ppermute | solution.py:663
  54.4 11.3 %collective-permute-start.2 = (bf16[8,288,512]{2,1,0:T(8,128)(2,1)}, bf16[8,288,512]{2,1,0:T(8,128)(2,1)S(1)}, u32[]{:S(2)}, u32[]{:S(2)}) collective-permute-start(bf16[8,288,512]{2,1,0:T(8,128)(2,1)} %bitcast.10), channel_id=1, source_target_pairs={{0,8},{8,0},{16,24},{24,16},{32,40},{40,32},{48,56},{56,48},{64,72... | collective-permute-start | bytes 7077896 | tf_op jit(solution)/shard_map/ppermute | solution.py:665
  55.1 53.5 %collective-permute-start.3 = (bf16[2,128,1024]{2,1,0:T(8,128)(2,1)}, bf16[2,128,1024]{2,1,0:T(8,128)(2,1)S(1)}, u32[]{:S(2)}, u32[]{:S(2)}) collective-permute-start(bf16[2,128,1024]{2,1,0:T(8,128)(2,1)} %get-tuple-element.51), channel_id=1, source_target_pairs={{0,2},{1,3},{2,4},{3,5},{4,6},{5,7},{6,0},{7,1},{8,14},{9,15},{10,... | collective-permute-start | bytes 1572872 | tf_op jit(solution)/shard_map/ppermute | solution.py:640
  60.8 47.9 %collective-permute-start.4 = (bf16[2,128,1024]{2,1,0:T(8,128)(2,1)}, bf16[2,128,1024]{2,1,0:T(8,128)(2,1)}, u32[]{:S(2)}, u32[]{:S(2)}) collective-permute-start(bf16[2,128,1024]{2,1,0:T(8,128)(2,1)} %pad_maximum_fusion.2), channel_id=1, source_target_pairs={{0,3},{1,4},{2,5},{3,6},{4,7},{5,0},{6,1},{7,2},{8,13},{9,14},{10,... | collective-permute-start | bytes 1572872 | tf_op jit(solution)/shard_map/ppermute | solution.py:640
  61.5 47.2 %collective-permute-start.5 = (bf16[128,1024]{1,0:T(8,128)(2,1)}, bf16[128,1024]{1,0:T(8,128)(2,1)S(1)}, u32[]{:S(2)}, u32[]{:S(2)}) collective-permute-start(bf16[128,1024]{1,0:T(8,128)(2,1)} %get-tuple-element.53), channel_id=1, source_target_pairs={{0,4},{1,5},{2,6},{3,7},{4,0},{5,1},{6,2},{7,3},{8,12},{9,13},{10,... | collective-permute-start | bytes 786440 | tf_op jit(solution)/shard_map/ppermute | solution.py:640
  65.7 1.7 copy-start.2
  70.0 20.8 %all-to-all-start.1 = ((f32[32,40,128]{2,1,0:T(8,128)}), f32[32,40,128]{2,1,0:T(8,128)S(1)}, u32[]{:S(2)}, u32[]{:S(2)}) async-start(f32[32,40,128]{2,1,0:T(8,128)} %shard_map.94), calls=%async_computation.1 | async-start | bytes 1310720 | tf_op jit(solution)/shard_map/all_to_all | solution.py:631
  90.8 0.8 copy-start.4
  91.6 24.6 %copy-start.5 = (bf16[2,128,1024]{2,1,0:T(8,128)(2,1)S(1)}, bf16[2,128,1024]{2,1,0:T(8,128)(2,1)}, u32[]{:S(2)}) copy-start(bf16[2,128,1024]{2,1,0:T(8,128)(2,1)} %get-tuple-element.56) | copy-start | bytes 1572868
  108.6 33.3 %copy-start.3 = (bf16[128,1024]{1,0:T(8,128)(2,1)S(1)}, bf16[128,1024]{1,0:T(8,128)(2,1)}, u32[]{:S(2)}) copy-start(bf16[128,1024]{1,0:T(8,128)(2,1)} %get-tuple-element.58.refs_5_) | copy-start | bytes 786436
  108.7 20.5 %all-to-all-start.2 = ((f32[32,40,128]{2,1,0:T(8,128)}), f32[32,40,128]{2,1,0:T(8,128)S(1)}, u32[]{:S(2)}, u32[]{:S(2)}) async-start(f32[32,40,128]{2,1,0:T(8,128)} %shard_map.95), calls=%async_computation.2 | async-start | bytes 1310720 | tf_op jit(solution)/shard_map/all_to_all | solution.py:631
  116.2 13.0 %collective-permute-start.6 = (bf16[2,128,1024]{2,1,0:T(8,128)(2,1)S(1)}, bf16[2,128,1024]{2,1,0:T(8,128)(2,1)S(1)}, u32[]{:S(2)}, u32[]{:S(2)}) collective-permute-start(bf16[2,128,1024]{2,1,0:T(8,128)(2,1)S(1)} %copy-done.5), channel_id=1, source_target_pairs={{0,1},{1,2},{2,3},{3,4},{4,5},{5,6},{6,7},{7,0},{8,15},{9,8},{10,9... | collective-permute-start | bytes 1572872 | tf_op jit(solution)/shard_map/ppermute | solution.py:640
  129.2 1.4 collective-permute-start.8
  130.6 11.3 %collective-permute-start.10 = (bf16[2,288,128]{2,1,0:T(8,128)(2,1)S(1)}, bf16[2,288,128]{2,1,0:T(8,128)(2,1)S(1)}, u32[]{:S(2)}, u32[]{:S(2)}) collective-permute-start(bf16[2,288,128]{2,1,0:T(8,128)(2,1)S(1)} %pad_maximum_fusion.3), channel_id=1, source_target_pairs={{0,2},{1,3},{2,4},{3,5},{4,6},{5,7},{6,0},{7,1},{8,14},{9,15},{10,... | collective-permute-start | bytes 442376 | tf_op jit(solution)/shard_map/ppermute | solution.py:640
  132.8 9.1 %collective-permute-start.11 = (bf16[2,288,128]{2,1,0:T(8,128)(2,1)S(1)}, bf16[2,288,128]{2,1,0:T(8,128)(2,1)S(1)}, u32[]{:S(2)}, u32[]{:S(2)}) collective-permute-start(bf16[2,288,128]{2,1,0:T(8,128)(2,1)S(1)} %pad_maximum_fusion.3), channel_id=1, source_target_pairs={{0,1},{1,2},{2,3},{3,4},{4,5},{5,6},{6,7},{7,0},{8,15},{9,8},{10,9... | collective-permute-start | bytes 442376 | tf_op jit(solution)/shard_map/ppermute | solution.py:640
  133.5 8.5 %collective-permute-start.9 = (bf16[2,288,128]{2,1,0:T(8,128)(2,1)S(1)}, bf16[2,288,128]{2,1,0:T(8,128)(2,1)S(1)}, u32[]{:S(2)}, u32[]{:S(2)}) collective-permute-start(bf16[2,288,128]{2,1,0:T(8,128)(2,1)S(1)} %pad_maximum_fusion.3), channel_id=1, source_target_pairs={{0,3},{1,4},{2,5},{3,6},{4,7},{5,0},{6,1},{7,2},{8,13},{9,14},{10,... | collective-permute-start | bytes 442376 | tf_op jit(solution)/shard_map/ppermute | solution.py:640
  133.5 8.4 %collective-permute-start.7 = (bf16[288,128]{1,0:T(8,128)(2,1)S(1)}, bf16[288,128]{1,0:T(8,128)(2,1)S(1)}, u32[]{:S(2)}, u32[]{:S(2)}) collective-permute-start(bf16[288,128]{1,0:T(8,128)(2,1)S(1)} %shard_map.96.refs_0_), channel_id=1, source_target_pairs={{0,4},{1,5},{2,6},{3,7},{4,0},{5,1},{6,2},{7,3},{8,12},{9,13},{10,... | collective-permute-start | bytes 221192 | tf_op jit(solution)/shard_map/ppermute | solution.py:640
  143.8 6.9 %collective-permute-start.12 = (f32[16,72,128]{2,1,0:T(8,128)S(1)}, f32[16,72,128]{2,1,0:T(8,128)S(1)}, u32[]{:S(2)}, u32[]{:S(2)}) collective-permute-start(f32[16,72,128]{2,1,0:T(8,128)S(1)} %get-tuple-element.64), channel_id=1, source_target_pairs={{0,8},{8,0},{16,24},{24,16},{32,40},{40,32},{48,56},{56,48},{64,72... | collective-permute-start | bytes 1769480 | tf_op jit(solution)/shard_map/ppermute | solution.py:690
  178.5 4.4 %collective-permute-start.13 = (f32[16,72,128]{2,1,0:T(8,128)S(1)}, f32[16,72,128]{2,1,0:T(8,128)S(1)}, u32[]{:S(2)}, u32[]{:S(2)}) collective-permute-start(f32[16,72,128]{2,1,0:T(8,128)S(1)} %all_to_all.26.own_ref), channel_id=1, source_target_pairs={{0,8},{8,0},{16,24},{24,16},{32,40},{40,32},{48,56},{56,48},{64,72... | collective-permute-start | bytes 1769480 | tf_op jit(solution)/shard_map/ppermute | solution.py:694
Sparse Core Ops, SparseCore 0:
  9.1 42.4 all-gather.2

commit v6 on v5

--- a/solution.py
+++ b/solution.py
@@ -239,7 +239,6 @@
         many = QUERIES // ROWS
         query = queries[pl.ds(many * i, many)].reshape(QUERIES, DIM)
         first = scalar_start(q0, n_ref)
-        last = scalar_start(q0 + QUERIES - 1, n_ref)
         need = q0 + QUERIES - first
         rest = lax.rem(need, KEYS)
         count = need // KEYS + (rest > HALF).astype(jnp.int32)
@@ -251,31 +250,23 @@
             low = q0 + QUERIES - at - size
             return low, low + PAD, pl.ds(pl.multiple_of(at, HALF), size)
 
-        def score(at, size, masked, top):
+        def score(at, size, top):
             low, key_at, rows_at = tile(at, size)
             block = keys[pl.ds(key_at // ROWS, size // ROWS)].reshape(size, DIM)
             s = mm_nt(block, query)
-            if masked:
-                k_at = low + lax.broadcasted_iota(jnp.int32, (size, QUERIES), 0)
-                s = jnp.where((k_at <= q_at) & (k_at >= start), s, NEG)
+            k_at = low + lax.broadcasted_iota(jnp.int32, (size, QUERIES), 0)
+            s = jnp.where((k_at <= q_at) & (k_at >= start), s, NEG)
             scores[rows_at, :] = s
             return jnp.maximum(top, jnp.max(s.reshape(size // 8, 8, QUERIES), axis=0))
 
         def masked(j, top):
-            return score(j * KEYS, KEYS, True, top)
-
-        def plain(j, top):
-            return score(j * KEYS, KEYS, False, top)
+            return score(j * KEYS, KEYS, top)
 
         def masked_half(j, top):
-            return score(count * KEYS, HALF, True, top)
-
-        one = jnp.minimum(count, 1)
-        inner = jnp.clip((q0 + QUERIES - last) // KEYS, one, count)
+            return score(count * KEYS, HALF, top)
+
         top = jnp.full((8, QUERIES), NEG, F32)
-        top = lax.fori_loop(0, one, masked, top)
-        top = lax.fori_loop(one, inner, plain, top)
-        top = lax.fori_loop(inner, count, masked, top)
+        top = lax.fori_loop(0, count, masked, top)
         top = lax.fori_loop(0, ends, masked_half, top)
         top = jnp.max(top, axis=0, keepdims=True)
 
@@ -660,9 +651,10 @@
     taken = lax.ppermute(give, "seq", partner)
     outgoing = [across] + [jnp.stack([mine[k], taken[k]]) for k in range(PARTS // 2 - 1)]
     own, outgoing, taps = lax.optimization_barrier((own, outgoing, conv_weight.T))
-    other = lax.ppermute(own[:, ROWS : 2 * ROWS, :], "seq", partner)
-    own, other, own_w, outgoing = lax.optimization_barrier((own, other, own_w, outgoing))
+    shared = own[:, ROWS : 2 * ROWS, :]
+    own, shared, own_w, outgoing = lax.optimization_barrier((own, shared, own_w, outgoing))
     other_w = lax.ppermute(own_w, "seq", partner)
+    other = lax.ppermute(shared, "seq", partner)
     far = PARTS // 2
     arrived = {far: both_ways(outgoing[0], far)}
     for k in (3, 2):

time: 192 us -> 193 us (level)
    ppermute x8, waiting for transfers between devices: 3.48 us -> 6.69 us  [both_ways(): return lax.ppermute(block, ('seq', 'dp'), route)]
    ppermute x1, starting transfers between devices: 0.74 us -> 3.16 us  [local(): other_w = lax.ppermute(own_w, 'seq', partner)]
    ppermute x1, waiting for transfers between devices: 2.42 us -> 0.01 us  [local(): other = lax.ppermute(shared, 'seq', partner)]
    ppermute x8, starting transfers between devices: 18.5 us -> 16.4 us  [both_ways(): return lax.ppermute(block, ('seq', 'dp'), route)]
    ppermute x1, starting transfers between devices: 5.26 us -> 3.3 us  [local(): partial = keep + lax.ppermute(send, 'seq', partner)]
where the time goes in v6:
time: 193 us; the launch traced here: 192 us
  starting transfers between devices  48.3 us (25%)
  waiting for transfers between devices  45.4 us (24%)
  Pallas kernels  45 us (23%)
  blocking collectives  28.6 us (15%)
  between operations  13.5 us (7%)
  local copies, waits for them, and re-layouts  8.68 us (4%)
  other arithmetic  2.11 us (1%)
    all_to_all x3, waiting for transfers between devices, swap_all(): return lax.all_to_all(x, axis, 0, 0, tiled=True, axis_index_groups=groups)  33.9 us
    all_to_all x2, blocking collectives, swap_all(): return lax.all_to_all(x, axis, 0, 0, tiled=True, axis_index_groups=groups)  28.6 us
    all_to_all x3, starting transfers between devices, swap_all(): return lax.all_to_all(x, axis, 0, 0, tiled=True, axis_index_groups=groups)  22.2 us
    pallas_call x1, Pallas kernels, student(): pl.pallas_call(lambda *refs: student_kernel(*refs, weight=weight), out_sh...  17 us
    pallas_call x1, Pallas kernels, attend(): pl.pallas_call(attend_kernel, out_shape=(jax.ShapeDtypeStruct((DIM, SEQ),...  16.6 us
    ppermute x8, starting transfers between devices, both_ways(): return lax.ppermute(block, ('seq', 'dp'), route)  16.4 us
    ppermute x8, waiting for transfers between devices, both_ways(): return lax.ppermute(block, ('seq', 'dp'), route)  6.69 us
    unnamed x15, local copies, waits for them, and re-layouts  4.35 us
  transfers between devices with their start and end apart: 18, of which 8 were waited for; matrix products, arithmetic and copies ran while one was open for 3% of the time, Pallas kernels for 22%

profile of v6, /device:TPU:1, one launch (start us, length us, event | category | flops | bytes accessed | tf_op | source)
XLA Modules:
  0.0 191.6 jit_solution(8710700508787761372)
XLA Ops:
  6.5 0.0 copy-start
  6.5 0.0 all-gather.3.cloned.1.call-start
  6.5 1.1 copy-done
  7.6 0.8 dynamic-slice_bitcast_fusion
  8.4 0.0 all-gather.3.cloned.1.call-update
  8.4 2.7 %shard_map.91 = bf16[32,272,128]{2,1,0:T(8,128)(2,1)} custom-call(bf16[1,128,4096]{2,1,0:T(8,128)(2,1)} %q_ref.1, bf16[1,128,1024]{2,1,0:T(8,128)(2,1)} %k_ref.1, bf16[1,128,1024]{2,1,0:T(8,128)(2,1)} %v_ref.1, s32[1,128]{1,0:T(1,128)} %doc_ref.1), custom_call_target="tpu_custom_call" | custom-call | bytes 4194304 | tf_op jit(solution)/shard_map/pallas_call | solution.py:84
  11.1 0.0 copy-start.6
  11.1 8.8 %all-to-all-start = ((bf16[32,272,128]{2,1,0:T(8,128)(2,1)}), bf16[32,272,128]{2,1,0:T(8,128)(2,1)}, u32[]{:S(2)}, u32[]{:S(2)}) async-start(bf16[32,272,128]{2,1,0:T(8,128)(2,1)} %shard_map.91), calls=%async_computation | async-start | bytes 4456448 | tf_op jit(solution)/shard_map/all_to_all | solution.py:622
  19.9 3.0 %shard_map.92 = (bf16[128,1024]{1,0:T(8,128)(2,1)}, bf16[128,1024]{1,0:T(8,128)(2,1)}, bf16[3,128,1024]{2,1,0:T(8,128)(2,1)}, bf16[3,128,1024]{2,1,0:T(8,128)(2,1)}) custom-call(s32[1]{0:T(128)} %bitcast.core_ref, s32[1]{0:T(128)} %bitcast.2.part_ref, bf16[1,128,8192]{2,1,0:T(8,128)(2,1)} %hid_ref.3), custom_call_target="tpu_custom_call" | custom-call | bytes 4194304 | tf_op jit(solution)/shard_map/pallas_call | solution.py:118
  22.9 0.3 collective-permute-start
  23.2 0.0 copy-done.6
  23.2 0.8 copy.10
  24.0 1.2 fusion
  25.2 0.2 collective-permute-done
  25.4 0.1 fusion.1
  25.5 0.8 pad_maximum_fusion.2
  26.3 0.0 copy-start.1
  26.3 1.2 pad_maximum_fusion
  27.5 22.2 %all-to-all-done.own_ref = bf16[32,272,128]{2,1,0:T(8,128)(2,1)} async-done(((bf16[32,272,128]{2,1,0:T(8,128)(2,1)}), bf16[32,272,128]{2,1,0:T(8,128)(2,1)}, u32[]{:S(2)}, u32[]{:S(2)}) %all-to-all-start) | async-done | bytes 2228256 | tf_op jit(solution)/shard_map/all_to_all | solution.py:622
  49.6 2.3 %slice.27 = bf16[32,128,128]{2,1,0:T(8,128)(2,1)} slice(bf16[32,272,128]{2,1,0:T(8,128)(2,1)} %all-to-all-done.own_ref), slice={[0:32], [128:256], [0:128]} | slice | bytes 2097152 | tf_op jit(solution)/shard_map/slice | solution.py:654
  52.0 3.2 %collective-permute-start.2 = (bf16[8,288,512]{2,1,0:T(8,128)(2,1)}, bf16[8,288,512]{2,1,0:T(8,128)(2,1)S(1)}, u32[]{:S(2)}, u32[]{:S(2)}) collective-permute-start(bf16[8,288,512]{2,1,0:T(8,128)(2,1)} %bitcast.10), channel_id=1, source_target_pairs={{0,8},{8,0},{16,24},{24,16},{32,40},{40,32},{48,56},{56,48},{64,72... | collective-permute-start | bytes 7077896 | tf_op jit(solution)/shard_map/ppermute | solution.py:656
  55.1 0.0 collective-permute-start.1
  55.1 3.8 %collective-permute-start.3 = (bf16[2,128,1024]{2,1,0:T(8,128)(2,1)}, bf16[2,128,1024]{2,1,0:T(8,128)(2,1)S(1)}, u32[]{:S(2)}, u32[]{:S(2)}) collective-permute-start(bf16[2,128,1024]{2,1,0:T(8,128)(2,1)} %get-tuple-element.51), channel_id=1, source_target_pairs={{0,2},{1,3},{2,4},{3,5},{4,6},{5,7},{6,0},{7,1},{8,14},{9,15},{10,... | collective-permute-start | bytes 1572872 | tf_op jit(solution)/shard_map/ppermute | solution.py:631
  58.9 1.1 collective-permute-start.4
  60.0 3.8 %collective-permute-start.5 = (bf16[128,1024]{1,0:T(8,128)(2,1)}, bf16[128,1024]{1,0:T(8,128)(2,1)S(1)}, u32[]{:S(2)}, u32[]{:S(2)}) collective-permute-start(bf16[128,1024]{1,0:T(8,128)(2,1)} %get-tuple-element.53), channel_id=1, source_target_pairs={{0,4},{1,5},{2,6},{3,7},{4,0},{5,1},{6,2},{7,3},{8,12},{9,13},{10,... | collective-permute-start | bytes 786440 | tf_op jit(solution)/shard_map/ppermute | solution.py:631
  63.8 0.0 collective-permute-done.2.other_ref
  63.8 0.0 copy-done.1
  63.8 1.7 copy-done.2
  65.5 2.6 %shard_map.94 = f32[32,40,128]{2,1,0:T(8,128)} custom-call(s32[1]{0:T(128)} %bitcast.core_ref, bf16[1,128,8192]{2,1,0:T(8,128)(2,1)S(1)} %copy-done.1, bf16[8,288,512]{2,1,0:T(8,128)(2,1)S(1)} %bitcast.11, bf16[8,288,512]{2,1,0:T(8,128)(2,1)S(1)} %collective-permute-done.2.other_ref), custom_call_target="tpu_custom_call" | custom-call | flops 603979776 | bytes 8388608 | tf_op jit(solution)/shard_map/pallas_call | solution.py:160
  68.1 5.9 %all-to-all-start.1 = ((f32[32,40,128]{2,1,0:T(8,128)}), f32[32,40,128]{2,1,0:T(8,128)S(1)}, u32[]{:S(2)}, u32[]{:S(2)}) async-start(f32[32,40,128]{2,1,0:T(8,128)} %shard_map.94), calls=%async_computation.1 | async-start | bytes 1310720 | tf_op jit(solution)/shard_map/all_to_all | solution.py:622
  74.0 0.0 collective-permute-done.1.other_ref
  74.0 16.6 %shard_map.93 = (bf16[128,4096]{1,0:T(8,128)(2,1)}, bf16[32,128,128]{2,1,0:T(8,128)(2,1)}, bf16[128,4096]{1,0:T(8,128)(2,1)}, s32[4]{0:T(128)}) custom-call(s32[1]{0:T(128)} %bitcast.core_ref, bf16[32,272,128]{2,1,0:T(8,128)(2,1)} %all-to-all-done.own_ref, bf16[32,128,128]{2,1,0:T(8,128)(2,1)} %collective-permute-done.1.other_ref), custom_call_target="tpu_custom_call" | custom-call | flops 8589934592 | bytes 8388608 | tf_op jit(solution)/shard_map/pallas_call | solution.py:303
  90.6 0.0 all-to-all-done.1.refs_5_
  90.6 0.0 copy-start.4
  90.6 0.8 copy-done.4
  91.5 17.0 %shard_map.95 = f32[32,40,128]{2,1,0:T(8,128)} custom-call(s32[1]{0:T(128)} %bitcast.1.refs_0_, s32[4]{0:T(128)} %get-tuple-element.45.refs_1_, f32[32]{0:T(128)} %refs_2_.1, f32[32]{0:T(128)} %refs_3_.1, f32[256,4]{1,0:T(8,128)} %bitcast.13, f32[32,40,128]{2,1,0:T(8,128)} %copy-done.4, bf16[128,4096]{1,0:T(8,128)(2,1)} %get-tuple-element.48.refs_6_, ...), custom_call_target="tpu_custom_call" | custom-call | flops 8589934592 | bytes 8388608 | tf_op jit(solution)/shard_map/pallas_call | solution.py:516
  108.5 0.0 collective-permute-done.5.refs_6_
  108.5 0.0 collective-permute-done.3.refs_8_
  108.5 0.0 collective-permute-done.4.refs_7_
  108.5 7.5 %all-to-all-start.2 = ((f32[32,40,128]{2,1,0:T(8,128)}), f32[32,40,128]{2,1,0:T(8,128)S(1)}, u32[]{:S(2)}, u32[]{:S(2)}) async-start(f32[32,40,128]{2,1,0:T(8,128)} %shard_map.95), calls=%async_computation.2 | async-start | bytes 1310720 | tf_op jit(solution)/shard_map/all_to_all | solution.py:622
  116.0 0.0 copy-done.5
  116.0 1.2 collective-permute-start.6
  117.2 11.8 %all-to-all-done.2.in_ref = f32[32,40,128]{2,1,0:T(8,128)S(1)} async-done(((f32[32,40,128]{2,1,0:T(8,128)}), f32[32,40,128]{2,1,0:T(8,128)S(1)}, u32[]{:S(2)}, u32[]{:S(2)}) %all-to-all-start.2) | async-done | bytes 655392 | tf_op jit(solution)/shard_map/all_to_all | solution.py:622
  129.0 0.0 collective-permute-done.6.refs_9_
  129.0 0.1 collective-permute-start.8
  129.1 1.3 collective-permute-done.8
  130.4 0.3 collective-permute-start.10
  130.7 1.0 collective-permute-start.11
  131.6 1.4 collective-permute-start.9
  133.0 3.9 %collective-permute-start.7 = (bf16[288,128]{1,0:T(8,128)(2,1)S(1)}, bf16[288,128]{1,0:T(8,128)(2,1)S(1)}, u32[]{:S(2)}, u32[]{:S(2)}) collective-permute-start(bf16[288,128]{1,0:T(8,128)(2,1)S(1)} %shard_map.96.refs_0_), channel_id=1, source_target_pairs={{0,4},{1,5},{2,6},{3,7},{4,0},{5,1},{6,2},{7,3},{8,12},{9,13},{10,... | collective-permute-start | bytes 221192 | tf_op jit(solution)/shard_map/ppermute | solution.py:631
  136.9 5.8 %collective-permute-done.7.refs_1_ = bf16[288,128]{1,0:T(8,128)(2,1)S(1)} collective-permute-done((bf16[288,128]{1,0:T(8,128)(2,1)S(1)}, bf16[288,128]{1,0:T(8,128)(2,1)S(1)}, u32[]{:S(2)}, u32[]{:S(2)}) %collective-permute-start.7) | collective-permute-done | bytes 73760 | tf_op jit(solution)/shard_map/ppermute | solution.py:631
  142.7 0.0 collective-permute-done.10.refs_3_
  142.7 0.9 collective-permute-done.11.refs_4_
  143.6 0.0 collective-permute-done.9.refs_2_
  143.6 0.0 copy-done.3
  143.6 1.8 shard_map.97
  145.4 3.3 %collective-permute-start.12 = (f32[16,72,128]{2,1,0:T(8,128)S(1)}, f32[16,72,128]{2,1,0:T(8,128)S(1)}, u32[]{:S(2)}, u32[]{:S(2)}) collective-permute-start(f32[16,72,128]{2,1,0:T(8,128)S(1)} %get-tuple-element.64), channel_id=1, source_target_pairs={{0,8},{8,0},{16,24},{24,16},{32,40},{40,32},{48,56},{56,48},{64,72... | collective-permute-start | bytes 1769480 | tf_op jit(solution)/shard_map/ppermute | solution.py:682
  148.7 1.6 collective-permute-done.12
  150.4 0.1 add.7
  150.4 15.2 %all_to_all.25 = f32[16,72,128]{2,1,0:T(8,128)S(1)} all-to-all(f32[16,72,128]{2,1,0:T(8,128)S(1)} %add.7), channel_id=1, replica_groups={{0,16,32,48,64,80,96,112,128,144,160,176,192,208,224,240},{8,24,40,56,7..., dimensions={0} | all-to-all | bytes 1179648 | tf_op jit(solution)/shard_map/all_to_all | solution.py:622
  165.8 13.3 %all_to_all.26.own_ref = f32[16,72,128]{2,1,0:T(8,128)S(1)} all-to-all(f32[16,72,128]{2,1,0:T(8,128)S(1)} %broadcast_in_dim.18), channel_id=1, replica_groups={{0,16,32,48,64,80,96,112,128,144,160,176,192,208,224,240},{8,24,40,56,7..., dimensions={0} | all-to-all | bytes 1179648 | tf_op jit(solution)/shard_map/all_to_all | solution.py:622
  179.1 2.9 %collective-permute-start.13 = (f32[16,72,128]{2,1,0:T(8,128)S(1)}, f32[16,72,128]{2,1,0:T(8,128)S(1)}, u32[]{:S(2)}, u32[]{:S(2)}) collective-permute-start(f32[16,72,128]{2,1,0:T(8,128)S(1)} %all_to_all.26.own_ref), channel_id=1, source_target_pairs={{0,8},{8,0},{16,24},{24,16},{32,40},{40,32},{48,56},{56,48},{64,72... | collective-permute-start | bytes 1769480 | tf_op jit(solution)/shard_map/ppermute | solution.py:686
  182.0 1.6 collective-permute-done.13.other_ref
  183.7 1.1 shard_map.98
  (8 shorter events, 0.1 us)
Async XLA Ops:
  6.5 1.1 copy-start
  6.5 45.4 %all-gather.3.cloned.1.call-start = ((), (), s32[]{:S(2)}) async-start(), calls=%async_computation.5 | async-start | bytes 2654208 | tf_op jit(solution)/shard_map/all_gather | solution.py:648
  11.1 12.1 %copy-start.6 = (f32[4,256]{1,0:T(4,128)S(1)}, f32[4,256]{1,0:T(4,128)}, u32[]{:S(2)}) copy-start(f32[4,256]{1,0:T(4,128)} %param.15) | copy-start | bytes 12292
  11.1 38.5 %all-to-all-start = ((bf16[32,272,128]{2,1,0:T(8,128)(2,1)}), bf16[32,272,128]{2,1,0:T(8,128)(2,1)}, u32[]{:S(2)}, u32[]{:S(2)}) async-start(bf16[32,272,128]{2,1,0:T(8,128)(2,1)} %shard_map.91), calls=%async_computation | async-start | bytes 4456448 | tf_op jit(solution)/shard_map/all_to_all | solution.py:622
  22.9 2.5 %collective-permute-start = (bf16[3,128,1024]{2,1,0:T(8,128)(2,1)}, bf16[3,128,1024]{2,1,0:T(8,128)(2,1)S(1)}, u32[]{:S(2)}, u32[]{:S(2)}) collective-permute-start(bf16[3,128,1024]{2,1,0:T(8,128)(2,1)} %get-tuple-element.37), channel_id=1, source_target_pairs={{0,8},{8,0},{16,24},{24,16},{32,40},{40,32},{48,56},{56,48},{64,72... | collective-permute-start | bytes 2359304 | tf_op jit(solution)/shard_map/ppermute | solution.py:651
  26.3 37.5 %copy-start.1 = (bf16[1,128,8192]{2,1,0:T(8,128)(2,1)S(1)}, bf16[1,128,8192]{2,1,0:T(8,128)(2,1)}, u32[]{:S(2)}) copy-start(bf16[1,128,8192]{2,1,0:T(8,128)(2,1)} %hid_ref.3) | copy-start | bytes 6291460
  52.0 11.9 %collective-permute-start.2 = (bf16[8,288,512]{2,1,0:T(8,128)(2,1)}, bf16[8,288,512]{2,1,0:T(8,128)(2,1)S(1)}, u32[]{:S(2)}, u32[]{:S(2)}) collective-permute-start(bf16[8,288,512]{2,1,0:T(8,128)(2,1)} %bitcast.10), channel_id=1, source_target_pairs={{0,8},{8,0},{16,24},{24,16},{32,40},{40,32},{48,56},{56,48},{64,72... | collective-permute-start | bytes 7077896 | tf_op jit(solution)/shard_map/ppermute | solution.py:656
  55.1 18.9 %collective-permute-start.1 = (bf16[32,128,128]{2,1,0:T(8,128)(2,1)}, bf16[32,128,128]{2,1,0:T(8,128)(2,1)}, u32[]{:S(2)}, u32[]{:S(2)}) collective-permute-start(bf16[32,128,128]{2,1,0:T(8,128)(2,1)} %slice.27), channel_id=1, source_target_pairs={{0,8},{8,0},{16,24},{24,16},{32,40},{40,32},{48,56},{56,48},{64,72... | collective-permute-start | bytes 3145736 | tf_op jit(solution)/shard_map/ppermute | solution.py:657
  55.1 53.4 %collective-permute-start.3 = (bf16[2,128,1024]{2,1,0:T(8,128)(2,1)}, bf16[2,128,1024]{2,1,0:T(8,128)(2,1)S(1)}, u32[]{:S(2)}, u32[]{:S(2)}) collective-permute-start(bf16[2,128,1024]{2,1,0:T(8,128)(2,1)} %get-tuple-element.51), channel_id=1, source_target_pairs={{0,2},{1,3},{2,4},{3,5},{4,6},{5,7},{6,0},{7,1},{8,14},{9,15},{10,... | collective-permute-start | bytes 1572872 | tf_op jit(solution)/shard_map/ppermute | solution.py:631
  58.9 49.6 %collective-permute-start.4 = (bf16[2,128,1024]{2,1,0:T(8,128)(2,1)}, bf16[2,128,1024]{2,1,0:T(8,128)(2,1)}, u32[]{:S(2)}, u32[]{:S(2)}) collective-permute-start(bf16[2,128,1024]{2,1,0:T(8,128)(2,1)} %pad_maximum_fusion.2), channel_id=1, source_target_pairs={{0,3},{1,4},{2,5},{3,6},{4,7},{5,0},{6,1},{7,2},{8,13},{9,14},{10,... | collective-permute-start | bytes 1572872 | tf_op jit(solution)/shard_map/ppermute | solution.py:631
  60.0 48.5 %collective-permute-start.5 = (bf16[128,1024]{1,0:T(8,128)(2,1)}, bf16[128,1024]{1,0:T(8,128)(2,1)S(1)}, u32[]{:S(2)}, u32[]{:S(2)}) collective-permute-start(bf16[128,1024]{1,0:T(8,128)(2,1)} %get-tuple-element.53), channel_id=1, source_target_pairs={{0,4},{1,5},{2,6},{3,7},{4,0},{5,1},{6,2},{7,3},{8,12},{9,13},{10,... | collective-permute-start | bytes 786440 | tf_op jit(solution)/shard_map/ppermute | solution.py:631
  63.8 1.7 copy-start.2
  68.1 22.5 %all-to-all-start.1 = ((f32[32,40,128]{2,1,0:T(8,128)}), f32[32,40,128]{2,1,0:T(8,128)S(1)}, u32[]{:S(2)}, u32[]{:S(2)}) async-start(f32[32,40,128]{2,1,0:T(8,128)} %shard_map.94), calls=%async_computation.1 | async-start | bytes 1310720 | tf_op jit(solution)/shard_map/all_to_all | solution.py:622
  90.6 0.8 copy-start.4
  91.5 24.6 %copy-start.5 = (bf16[2,128,1024]{2,1,0:T(8,128)(2,1)S(1)}, bf16[2,128,1024]{2,1,0:T(8,128)(2,1)}, u32[]{:S(2)}) copy-start(bf16[2,128,1024]{2,1,0:T(8,128)(2,1)} %get-tuple-element.56) | copy-start | bytes 1572868
  108.5 35.1 %copy-start.3 = (bf16[128,1024]{1,0:T(8,128)(2,1)S(1)}, bf16[128,1024]{1,0:T(8,128)(2,1)}, u32[]{:S(2)}) copy-start(bf16[128,1024]{1,0:T(8,128)(2,1)} %get-tuple-element.58.refs_5_) | copy-start | bytes 786436
  108.5 20.5 %all-to-all-start.2 = ((f32[32,40,128]{2,1,0:T(8,128)}), f32[32,40,128]{2,1,0:T(8,128)S(1)}, u32[]{:S(2)}, u32[]{:S(2)}) async-start(f32[32,40,128]{2,1,0:T(8,128)} %shard_map.95), calls=%async_computation.2 | async-start | bytes 1310720 | tf_op jit(solution)/shard_map/all_to_all | solution.py:622
  116.0 13.0 %collective-permute-start.6 = (bf16[2,128,1024]{2,1,0:T(8,128)(2,1)S(1)}, bf16[2,128,1024]{2,1,0:T(8,128)(2,1)S(1)}, u32[]{:S(2)}, u32[]{:S(2)}) collective-permute-start(bf16[2,128,1024]{2,1,0:T(8,128)(2,1)S(1)} %copy-done.5), channel_id=1, source_target_pairs={{0,1},{1,2},{2,3},{3,4},{4,5},{5,6},{6,7},{7,0},{8,15},{9,8},{10,9... | collective-permute-start | bytes 1572872 | tf_op jit(solution)/shard_map/ppermute | solution.py:631
  129.0 1.4 collective-permute-start.8
  130.4 12.3 %collective-permute-start.10 = (bf16[2,288,128]{2,1,0:T(8,128)(2,1)S(1)}, bf16[2,288,128]{2,1,0:T(8,128)(2,1)S(1)}, u32[]{:S(2)}, u32[]{:S(2)}) collective-permute-start(bf16[2,288,128]{2,1,0:T(8,128)(2,1)S(1)} %pad_maximum_fusion.3), channel_id=1, source_target_pairs={{0,2},{1,3},{2,4},{3,5},{4,6},{5,7},{6,0},{7,1},{8,14},{9,15},{10,... | collective-permute-start | bytes 442376 | tf_op jit(solution)/shard_map/ppermute | solution.py:631
  130.7 12.9 %collective-permute-start.11 = (bf16[2,288,128]{2,1,0:T(8,128)(2,1)S(1)}, bf16[2,288,128]{2,1,0:T(8,128)(2,1)S(1)}, u32[]{:S(2)}, u32[]{:S(2)}) collective-permute-start(bf16[2,288,128]{2,1,0:T(8,128)(2,1)S(1)} %pad_maximum_fusion.3), channel_id=1, source_target_pairs={{0,1},{1,2},{2,3},{3,4},{4,5},{5,6},{6,7},{7,0},{8,15},{9,8},{10,9... | collective-permute-start | bytes 442376 | tf_op jit(solution)/shard_map/ppermute | solution.py:631
  131.6 12.0 %collective-permute-start.9 = (bf16[2,288,128]{2,1,0:T(8,128)(2,1)S(1)}, bf16[2,288,128]{2,1,0:T(8,128)(2,1)S(1)}, u32[]{:S(2)}, u32[]{:S(2)}) collective-permute-start(bf16[2,288,128]{2,1,0:T(8,128)(2,1)S(1)} %pad_maximum_fusion.3), channel_id=1, source_target_pairs={{0,3},{1,4},{2,5},{3,6},{4,7},{5,0},{6,1},{7,2},{8,13},{9,14},{10,... | collective-permute-start | bytes 442376 | tf_op jit(solution)/shard_map/ppermute | solution.py:631
  133.0 9.7 %collective-permute-start.7 = (bf16[288,128]{1,0:T(8,128)(2,1)S(1)}, bf16[288,128]{1,0:T(8,128)(2,1)S(1)}, u32[]{:S(2)}, u32[]{:S(2)}) collective-permute-start(bf16[288,128]{1,0:T(8,128)(2,1)S(1)} %shard_map.96.refs_0_), channel_id=1, source_target_pairs={{0,4},{1,5},{2,6},{3,7},{4,0},{5,1},{6,2},{7,3},{8,12},{9,13},{10,... | collective-permute-start | bytes 221192 | tf_op jit(solution)/shard_map/ppermute | solution.py:631
  145.4 4.9 %collective-permute-start.12 = (f32[16,72,128]{2,1,0:T(8,128)S(1)}, f32[16,72,128]{2,1,0:T(8,128)S(1)}, u32[]{:S(2)}, u32[]{:S(2)}) collective-permute-start(f32[16,72,128]{2,1,0:T(8,128)S(1)} %get-tuple-element.64), channel_id=1, source_target_pairs={{0,8},{8,0},{16,24},{24,16},{32,40},{40,32},{48,56},{56,48},{64,72... | collective-permute-start | bytes 1769480 | tf_op jit(solution)/shard_map/ppermute | solution.py:682
  179.1 4.6 %collective-permute-start.13 = (f32[16,72,128]{2,1,0:T(8,128)S(1)}, f32[16,72,128]{2,1,0:T(8,128)S(1)}, u32[]{:S(2)}, u32[]{:S(2)}) collective-permute-start(f32[16,72,128]{2,1,0:T(8,128)S(1)} %all_to_all.26.own_ref), channel_id=1, source_target_pairs={{0,8},{8,0},{16,24},{24,16},{32,40},{40,32},{48,56},{56,48},{64,72... | collective-permute-start | bytes 1769480 | tf_op jit(solution)/shard_map/ppermute | solution.py:686
Sparse Core Ops, SparseCore 0:
  9.1 42.4 all-gather.2
